TPU v7x, 512 devices: a whole 4x8x8 slice. The times are simulated.
512 devices in a mesh: group: 2 (over z_lo), dp: 32 (over z_hi, y), tensor: 8 (over x, core).
Axes of the slice: x: 4, y: 8, z: 8 (z_hi: 4, z_lo: 2; z = z_hi * 2 + z_lo), core: 2. Of those that a mesh axis runs over, the one named last changes fastest.
Arguments:
- teacher_stream: float32 [8192, 6144], P('dp', ('group', 'tensor')), may hold values from -1100 to 1100
- teacher_gain: float32 [6144], P(('group', 'tensor')), may hold values from 0.25 to 1.75
- projection: bfloat16 [6144, 4096], P('dp', ('group', 'tensor')), may hold values from -0.078125 to 0.078125
- student_stream: float32 [8192, 4096], P('dp', ('group', 'tensor')), may hold values from -1100 to 1100
- student_context: bfloat16 [8192, 4096], P('dp', ('group', 'tensor')), may hold values from -12 to 12
- out_weight: bfloat16 [4096, 4096], P('dp', ('group', 'tensor')), may hold values from -0.09375 to 0.09375
- student_gain: float32 [4096], P(('group', 'tensor')), may hold values from 0.25 to 1.75
Outputs:
- student_out: float32 [8192, 4096], P('dp', ('group', 'tensor'))
- weight_grad: float32 [4096, 4096], P('dp', ('group', 'tensor'))
All inputs are finite; a program needn't handle non-finite values.
Results may differ from a plain program's by a relative error of at most 0.004.
Values may be sent and summed in bfloat16 or wider, within the bound.
No kernel may reach another device: no remote copies, remote signals or barrier semaphores. Data moves between devices by JAX's collectives and lax.ppermute only.
A program may use at most 64 MiB of HBM per device.

v0:
```python
import math

import jax
import jax.numpy as jnp
from jax import lax
from jax.sharding import PartitionSpec as P

EPSILON = 1e-05


def split_norm(values, feature_count):
    row_mean = lax.psum(jnp.sum(values, axis=1, keepdims=True), ("group", "tensor")) / feature_count
    centered = values - row_mean
    row_var = (
        lax.psum(jnp.sum(centered * centered, axis=1, keepdims=True), ("group", "tensor"))
        / feature_count
    )
    inv_std = lax.rsqrt(row_var + EPSILON)
    return (centered * inv_std, inv_std)


def teacher_part(teacher_stream, teacher_gain, projection, model_split):
    teacher_norm, _ = split_norm(teacher_stream, teacher_stream.shape[1] * model_split)
    teacher_hidden = (teacher_norm * teacher_gain).astype(jnp.bfloat16)
    hidden_full = lax.all_gather(teacher_hidden, ("group", "tensor"), axis=1, tiled=True)
    return jnp.dot(
        hidden_full,
        lax.all_gather(projection, "dp", axis=0, tiled=True),
        preferred_element_type=jnp.float32,
    )


def student_part(student_stream, student_context, out_weight):
    context_full = lax.all_gather(student_context, ("group", "tensor"), axis=1, tiled=True)
    branch = jnp.dot(
        context_full,
        lax.all_gather(out_weight, "dp", axis=0, tiled=True),
        preferred_element_type=jnp.float32,
    )
    return (student_stream + branch, context_full)


def shards(
    teacher_stream,
    teacher_gain,
    projection,
    student_stream,
    student_context,
    out_weight,
    student_gain,
):
    model_split = lax.axis_size(("group", "tensor"))
    row_count = teacher_stream.shape[0]
    token_count = row_count * lax.axis_size("dp")
    target = teacher_part(teacher_stream, teacher_gain, projection, model_split)
    pre_norm, context_full = student_part(student_stream, student_context, out_weight)
    feature_count = student_stream.shape[1] * model_split
    normalized, inv_std = split_norm(pre_norm, feature_count)
    student_out = normalized * student_gain
    scaled = (student_out - target) * (1.0 / math.sqrt(token_count))
    grad_norm = scaled * student_gain
    first_sum, second_sum = lax.psum(
        (
            jnp.sum(grad_norm, axis=1, keepdims=True),
            jnp.sum(grad_norm * normalized, axis=1, keepdims=True),
        ),
        ("group", "tensor"),
    )
    grad_pre = (
        inv_std
        * (grad_norm - first_sum / feature_count - normalized * (second_sum / feature_count))
    ).astype(jnp.bfloat16)
    weight_grad = lax.psum_scatter(
        lax.dot_general(
            context_full, grad_pre, (((0,), (0,)), ((), ())), preferred_element_type=jnp.float32
        ),
        "dp",
        scatter_dimension=0,
        tiled=True,
    )
    return (student_out, weight_grad)


def solution(mesh):
    return jax.shard_map(
        shards,
        mesh=mesh,
        in_specs=(
            P("dp", ("group", "tensor")),
            P(("group", "tensor")),
            P("dp", ("group", "tensor")),
            P("dp", ("group", "tensor")),
            P("dp", ("group", "tensor")),
            P("dp", ("group", "tensor")),
            P(("group", "tensor")),
        ),
        out_specs=(P("dp", ("group", "tensor")), P("dp", ("group", "tensor"))),
        check_vma=False,
    )
```

profile of v0, /device:TPU:2, one launch (start us, length us, event | category | flops | bytes accessed | tf_op | source)
XLA Modules:
  0.0 556.2 jit_solution(2453334690486029299)
XLA Ops:
  7.2 0.0 all-gather.5.cloned.1.call-start
  7.2 0.7 all-gather.5.cloned.1.call-update
  7.9 0.0 all-gather.7.cloned.1.call-start
  7.9 0.7 all-gather.7.cloned.1.call-update
  8.6 0.0 all-gather.11.cloned.1.call-start
  8.7 0.7 all-gather.11.cloned.1.call-update
  9.4 0.0 all-gather.9.cloned.1.call-start
  9.4 1.1 copy.12
  10.5 1.1 reduce_sum.56
  11.6 0.0 copy-start.1
  11.6 0.0 copy-start.3
  11.7 0.0 copy-start.2
  11.7 45.5 %all-gather.5.cloned.1.call-done = bf16[256,4096]{1,0:T(8,128)(2,1)} async-done(((bf16[256,256]{1,0:T(8,128)(2,1)}), bf16[256,4096]{1,0:T(8,128)(2,1)}) %all-gather.5.cloned.1.call-update) | async-done | bytes 2097168 | tf_op jit(solution)/shard_map/all_gather | solution.py:34
  57.1 91.1 %all-gather.7.cloned.1.call-done = bf16[4096,256]{1,0:T(8,128)(2,1)} async-done(((bf16[128,256]{1,0:T(8,128)(2,1)}), bf16[4096,256]{1,0:T(8,128)(2,1)}) %all-gather.7.cloned.1.call-update) | async-done | bytes 2097168 | tf_op jit(solution)/shard_map/all_gather | solution.py:37
  148.2 3.2 fusion.7
  151.3 23.4 %all-reduce.2 = (f32[256,1]{0,1:T(1,128)S(1)}, f32[256,1]{0,1:T(1,128)S(1)}) all-reduce(f32[256,1]{0,1:T(1,128)S(1)} %bitcast.33, f32[256,1]{0,1:T(1,128)S(1)} %bitcast.30), channel_id=1, replica_groups=mesh['group'=2,'dp'=32,'tensor'=8] {'group','tensor'}, use_global_device_ids=true, to_apply=%region_1.0 | all-reduce | flops 512 | bytes 4096 | tf_op jit(solution)/shard_map/psum | solution.py:12
  174.7 0.1 multiply_reduce_fusion.2
  174.8 0.0 copy-done.1
  174.8 0.2 multiply_reduce_fusion
  175.0 27.5 %all-reduce.1 = (f32[256,1]{0,1:T(1,128)S(1)}, f32[256,1]{0,1:T(1,128)S(1)}) all-reduce(f32[256,1]{0,1:T(1,128)S(1)} %bitcast.34, f32[256,1]{0,1:T(1,128)S(1)} %bitcast.35), channel_id=1, replica_groups=mesh['group'=2,'dp'=32,'tensor'=8] {'group','tensor'}, use_global_device_ids=true, to_apply=%region_3.0 | all-reduce | flops 512 | bytes 4096 | tf_op jit(solution)/shard_map/psum | solution.py:15
  202.5 0.0 copy-done.3
  202.5 0.8 multiply_convert_fusion
  203.3 0.0 all-gather.9.cloned.1.call-update
  203.3 0.0 reduce-scatter.2.cloned.1.call-start
  203.4 0.0 copy-done.2
  203.4 38.1 %all-gather.11.cloned.1.call-done = bf16[6144,256]{1,0:T(8,128)(2,1)} async-done(((bf16[192,256]{1,0:T(8,128)(2,1)}), bf16[6144,256]{1,0:T(8,128)(2,1)}) %all-gather.11.cloned.1.call-update) | async-done | bytes 3145744 | tf_op jit(solution)/shard_map/all_gather | solution.py:28
  241.6 39.0 %all-gather.9.cloned.1.call-done = bf16[256,6144]{1,0:T(8,128)(2,1)} async-done(((bf16[256,384]{1,0:T(8,128)(2,1)}), bf16[256,6144]{1,0:T(8,128)(2,1)}) %all-gather.9.cloned.1.call-update) | async-done | bytes 3145744 | tf_op jit(solution)/shard_map/all_gather | solution.py:25
  280.5 0.0 copy-start
  280.5 4.4 fusion.6
  284.9 25.4 %all-reduce = (f32[256,1]{0,1:T(1,128)S(1)}, f32[256,1]{0,1:T(1,128)S(1)}) all-reduce(f32[256,1]{0,1:T(1,128)S(1)} %bitcast.32, f32[256,1]{0,1:T(1,128)S(1)} %bitcast.31), channel_id=1, replica_groups=mesh['group'=2,'dp'=32,'tensor'=8] {'group','tensor'}, use_global_device_ids=true, to_apply=%region_11.0 | all-reduce | flops 512 | bytes 4096 | tf_op jit(solution)/shard_map/psum | solution.py:62
  310.2 0.0 copy-done
  310.2 2.7 convolution_bitcast_fusion
  312.9 0.0 reduce-scatter.2.cloned.1.call-update
  312.9 0.1 fusion.1
  313.0 0.8 copy.13
  313.9 234.1 %reduce-scatter.2.cloned.1.call-done = f32[128,256]{0,1:T(8,128)} async-done(((f32[4096,256]{0,1:T(8,128)}), f32[128,256]{0,1:T(8,128)}) %reduce-scatter.2.cloned.1.call-update) | async-done | bytes 131088 | tf_op jit(solution)/shard_map/reduce_scatter | solution.py:73
  548.0 1.7 copy.14
  (6 shorter events, 0.0 us)
Async XLA Ops:
  7.2 50.0 %all-gather.5.cloned.1.call-start = ((), (), s32[]{:S(2)}) async-start(), calls=%async_computation.1 | async-start | bytes 2228224 | tf_op jit(solution)/shard_map/all_gather | solution.py:34
  7.9 140.3 %all-gather.7.cloned.1.call-start = ((), (), s32[]{:S(2)}) async-start(), calls=%async_computation.2 | async-start | bytes 2162688 | tf_op jit(solution)/shard_map/all_gather | solution.py:37
  8.6 232.9 %all-gather.11.cloned.1.call-start = ((), (), s32[]{:S(2)}) async-start(), calls=%async_computation.4 | async-start | bytes 3244032 | tf_op jit(solution)/shard_map/all_gather | solution.py:28
  9.4 271.1 %all-gather.9.cloned.1.call-start = ((), (), s32[]{:S(2)}) async-start(), calls=%async_computation.3 | async-start | bytes 3342336 | tf_op jit(solution)/shard_map/all_gather | solution.py:25
  11.6 163.2 %copy-start.1 = (f32[256,384]{1,0:T(8,128)S(1)}, f32[256,384]{1,0:T(8,128)}, u32[]{:S(2)}) copy-start(f32[256,384]{1,0:T(8,128)} %param.7) | copy-start | bytes 1179652
  11.6 190.8 %copy-start.3 = (f32[384]{0:T(512)S(1)}, f32[384]{0:T(512)}, u32[]{:S(2)}) copy-start(f32[384]{0:T(512)} %param.8) | copy-start | bytes 4612
  11.7 191.7 %copy-start.2 = (f32[256]{0:T(256)S(1)}, f32[256]{0:T(256)}, u32[]{:S(2)}) copy-start(f32[256]{0:T(256)} %param.13) | copy-start | bytes 3076
  203.3 344.7 %reduce-scatter.2.cloned.1.call-start = ((), (), s32[]{:S(2)}) async-start(), calls=%async_computation.5 | async-start | bytes 4325376 | tf_op jit(solution)/shard_map/reduce_scatter | solution.py:73
  280.5 29.7 %copy-start = (bf16[256,4096]{1,0:T(8,128)(2,1)S(1)}, bf16[256,4096]{1,0:T(8,128)(2,1)}, u32[]{:S(2)}) copy-start(bf16[256,4096]{1,0:T(8,128)(2,1)} %all-gather.5.cloned.1.call-done) | copy-start | bytes 6291460
Sparse Core Ops, SparseCore 0:
  10.1 47.0 all-gather.4
  60.3 87.8 all-gather.6
  151.4 90.1 all-gather.10
  244.1 36.3 all-gather.8
  313.0 234.9 reduce-scatter.1
where the time goes:
time: 556 us
  waiting for transfers between devices  450 us (81%)
  blocking collectives  76.2 us (14%)
  between operations  13.9 us (2%)
  matrix products  10.2 us (2%)
    reduce_scatter x1, waiting for transfers between devices, shards(): lax.psum_scatter(lax.dot_general(context_full, grad_pre, (((0,), (0,)), (...  234 us
    all_gather x1, waiting for transfers between devices, student_part(): lax.all_gather(out_weight, 'dp', axis=0, tiled=True)  91.1 us
    all_gather x1, waiting for transfers between devices, student_part(): lax.all_gather(student_context, ('group', 'tensor'), axis=1, tiled=True)  45.5 us
    all_gather x1, waiting for transfers between devices, teacher_part(): lax.all_gather(teacher_hidden, ('group', 'tensor'), axis=1, tiled=True)  39 us
    all_gather x1, waiting for transfers between devices, teacher_part(): lax.all_gather(projection, 'dp', axis=0, tiled=True)  38.1 us
    psum x1, blocking collectives, split_norm(): lax.psum(jnp.sum(centered * centered, axis=1, keepdims=True), ('group', '...  27.5 us
    psum x1, blocking collectives, shards(): lax.psum((jnp.sum(grad_norm, axis=1, keepdims=True), jnp.sum(grad_norm *...  25.4 us
    psum x1, blocking collectives, split_norm(): lax.psum(jnp.sum(values, axis=1, keepdims=True), ('group', 'tensor'))  23.4 us
  transfers between devices with their start and end apart: 5, of which 5 were waited for; matrix products, arithmetic and copies ran while one was open for 1% of the time, Pallas kernels for 0%

commit v1 on v0

v1 whole, which is shorter than its diff:
```python
import math

import jax
import jax.numpy as jnp
from jax import lax
from jax.sharding import Mesh, PartitionSpec as P

EPSILON = 1e-05
BF16 = jnp.bfloat16
F32 = jnp.float32

TOKEN_AXES = ("zhigh", "yhigh", "row")
GATHER_AXES = ("zhigh", "yhigh")
FEATURE_AXES = ("group", "x", "core")


def swap(values, axis):
    return lax.ppermute(values, axis, [(0, 1), (1, 0)])


def ordered(mine, other, place, axis):
    first = place == 0
    return jnp.concatenate(
        [jnp.where(first, mine, other), jnp.where(first, other, mine)], axis=axis
    )


def my_half(values, place):
    half = values.shape[1] // 2
    return (
        jnp.where(place == 0, values[:, :half], values[:, half:]),
        jnp.where(place == 0, values[:, half:], values[:, :half]),
    )


def split_tokens(values, row):
    keep, give = my_half(values, row)
    return jnp.concatenate([keep, swap(give, "row")], axis=0)


def gather_line(values):
    count = lax.axis_size("x")
    place = lax.axis_index("x")
    ahead = [(i, (i + 1) % count) for i in range(count)]
    back = [(i, (i - 1) % count) for i in range(count)]
    rows = values.shape[0] // 2
    previous = lax.ppermute(values, "x", ahead)
    following = lax.ppermute(values, "x", back)
    opposite = jnp.concatenate(
        [
            lax.ppermute(previous[:rows], "x", ahead),
            lax.ppermute(following[rows:], "x", back),
        ],
        axis=0,
    )
    pieces = [values, previous, opposite, following]
    return jnp.concatenate(
        [lax.select_n((place - j) & (count - 1), *pieces) for j in range(count)], axis=1
    )


def gather_features(values):
    pair = ordered(values, swap(values, "group"), lax.axis_index("group"), 1)
    line = gather_line(pair)
    return line, swap(line, "core")


def both(first, place):
    return (
        jnp.where(place == 0, first[0], first[1]),
        jnp.where(place == 0, first[1], first[0]),
    )


def product(pair, weight_pair):
    return jnp.dot(pair[0], weight_pair[0], preferred_element_type=F32) + jnp.dot(
        pair[1], weight_pair[1], preferred_element_type=F32
    )


def moments(values):
    mean = jnp.mean(values, axis=1)
    centered = values - mean[:, None]
    return mean, centered, jnp.sum(centered * centered, axis=1)


def combine(means, squares, width):
    mean = jnp.mean(means, axis=0)
    shift = means - mean
    variance = jnp.mean(squares / width + shift * shift, axis=0)
    return mean, shift, lax.rsqrt(variance + EPSILON)


def gather_rows(rows):
    return lax.all_gather(jnp.stack(rows, axis=0), FEATURE_AXES, axis=0)


def shards(
    teacher_stream,
    teacher_gain,
    projection,
    student_stream,
    student_context,
    out_weight,
    student_gain,
):
    row = lax.axis_index("row")
    groups, lanes, cores = (lax.axis_size(name) for name in FEATURE_AXES)
    blocks = groups * lanes * cores
    tokens = teacher_stream.shape[0]
    token_count = tokens * lax.axis_size(TOKEN_AXES)
    width = student_stream.shape[1]
    depth = out_weight.shape[0]

    weights = lax.all_gather(
        jnp.concatenate([out_weight, projection], axis=0), GATHER_AXES, axis=0
    )
    weights = weights.reshape(groups, lanes, cores, *weights.shape[1:])
    weights = weights.transpose(2, 1, 0, 3, 4)
    core = lax.axis_index("core")
    out_full = both(weights[:, :, :, :depth].reshape(cores, -1, width), core)
    projection_full = both(weights[:, :, :, depth:].reshape(cores, -1, width), core)

    context = gather_features(split_tokens(student_context, row))

    teacher_mean, _, teacher_square = moments(teacher_stream)
    table = gather_rows([teacher_mean, teacher_square])
    mean, _, inv_std = combine(table[:, 0], table[:, 1], teacher_stream.shape[1])
    hidden = ((teacher_stream - mean[:, None]) * inv_std[:, None] * teacher_gain).astype(BF16)
    hidden = gather_features(split_tokens(hidden, row))

    branch = product(context, out_full)
    pre_norm = student_stream + (branch[:tokens] + swap(branch[tokens:].astype(BF16), "row").astype(F32))
    target = product(hidden, projection_full)
    target = target[:tokens] + swap(target[tokens:].astype(BF16), "row").astype(F32)

    block_mean, centered, square = moments(pre_norm)
    gain_square = student_gain * student_gain
    weighted = centered * gain_square
    scaled_target = target * student_gain
    table = gather_rows(
        [
            block_mean,
            square,
            jnp.sum(weighted, axis=1),
            jnp.sum(weighted * centered, axis=1),
            jnp.sum(scaled_target, axis=1),
            jnp.sum(scaled_target * centered, axis=1),
            jnp.full((tokens,), jnp.sum(gain_square), F32),
        ]
    )
    mean, shift, inv_std = combine(table[:, 0], table[:, 1], width)
    gains = table[:, 6]
    linear = jnp.sum(table[:, 2] + shift * gains, axis=0)
    quadratic = jnp.sum(table[:, 3] + shift * (2.0 * table[:, 2] + shift * gains), axis=0)
    target_sum = jnp.sum(table[:, 4], axis=0)
    target_cross = jnp.sum(table[:, 5] + shift * table[:, 4], axis=0)
    count = width * blocks
    scale = 1.0 / math.sqrt(token_count)
    first_mean = (inv_std * linear - target_sum) * (scale / count)
    second_mean = (inv_std * inv_std * quadratic - inv_std * target_cross) * (scale / count)

    normalized = (pre_norm - mean[:, None]) * inv_std[:, None]
    student_out = normalized * student_gain
    grad_norm = (student_out - target) * scale * student_gain
    grad_pre = (
        inv_std[:, None] * (grad_norm - first_mean[:, None] - normalized * second_mean[:, None])
    ).astype(BF16)
    grad_pre = jnp.concatenate([grad_pre, swap(grad_pre, "row")], axis=0)

    partial = [
        lax.dot_general(
            half, grad_pre, (((0,), (0,)), ((), ())), preferred_element_type=F32
        ).astype(BF16)
        for half in context
    ]
    partial = jnp.stack(both(partial, core), axis=0)
    partial = partial.reshape(cores, lanes, groups, depth, width).transpose(2, 1, 0, 3, 4)
    parts = lax.all_to_all(partial.reshape(blocks, depth, width), GATHER_AXES, 0, 0, tiled=True)
    weight_grad = jnp.sum(parts.astype(F32), axis=0)
    return (student_out, weight_grad)


def solution(mesh):
    groups, token_blocks, columns = (mesh.shape[name] for name in ("group", "dp", "tensor"))
    cores = 2
    zhigh = min(4, token_blocks // 4)
    fine = Mesh(
        mesh.devices.reshape(
            groups, zhigh, token_blocks // (2 * zhigh), 2, columns // cores, cores
        ),
        ("group", "zhigh", "yhigh", "row", "x", "core"),
    )
    split = P(TOKEN_AXES, FEATURE_AXES)
    return jax.shard_map(
        shards,
        mesh=fine,
        in_specs=(
            split,
            P(FEATURE_AXES),
            split,
            split,
            split,
            split,
            P(FEATURE_AXES),
        ),
        out_specs=(split, split),
        check_vma=False,
    )
```

time: 556 us -> 209 us (0.38)
  the two profiles are of different devices: /device:TPU:2 before, /device:TPU:64 now
where the time goes in v1:
time: 209 us; the launch traced here: 208 us
  starting transfers between devices  75.6 us (36%)
  waiting for transfers between devices  54.2 us (26%)
  blocking collectives  37.8 us (18%)
  between operations  14.8 us (7%)
  other arithmetic  13.5 us (6%)
  matrix products  6.04 us (3%)
  local copies, waits for them, and re-layouts  5.89 us (3%)
    all_gather x2, blocking collectives, gather_rows(): return lax.all_gather(jnp.stack(rows, axis=0), FEATURE_AXES, axis=0)  37.8 us
    all_to_all x1, waiting for transfers between devices, shards(): lax.all_to_all(partial.reshape(blocks, depth, width), GATHER_AXES, 0, 0,...  34.1 us
    ppermute x9, starting transfers between devices, swap(): return lax.ppermute(values, axis, [(0, 1), (1, 0)])  27.7 us
    all_to_all x1, starting transfers between devices, shards(): lax.all_to_all(partial.reshape(blocks, depth, width), GATHER_AXES, 0, 0,...  19.6 us
    ppermute x9, waiting for transfers between devices, swap(): return lax.ppermute(values, axis, [(0, 1), (1, 0)])  12.7 us
    ppermute x2, starting transfers between devices, gather_line(): lax.ppermute(following[rows:], 'x', back)  10.3 us
    ppermute x2, starting transfers between devices, gather_line(): following = lax.ppermute(values, 'x', back)  9.01 us
    ppermute x2, waiting for transfers between devices, gather_line(): previous = lax.ppermute(values, 'x', ahead)  5.21 us
  transfers between devices with their start and end apart: 19, of which 9 were waited for; matrix products, arithmetic and copies ran while one was open for 8% of the time, Pallas kernels for 0%

profile of v1, /device:TPU:64, one launch (start us, length us, event | category | flops | bytes accessed | tf_op | source)
XLA Modules:
  0.0 207.9 jit_solution(7004966053579512741)
XLA Ops:
  7.2 1.6 pad_maximum_fusion.9
  8.8 0.9 broadcast_select_fusion.13
  9.7 3.5 %collective-permute-start = (bf16[256,128]{1,0:T(8,128)(2,1)S(1)}, bf16[256,128]{1,0:T(8,128)(2,1)S(1)}, u32[]{:S(2)}, u32[]{:S(2)}) collective-permute-start(bf16[256,128]{1,0:T(8,128)(2,1)S(1)} %get-tuple-element.54), channel_id=1, source_target_pairs={{0,8},{8,0},{1,9},{9,1},{2,10},{10,2},{3,11},{11,3},{4,12},{12,4},... | collective-permute-start | bytes 196616 | tf_op jit(solution)/shard_map/ppermute | solution.py:18
  13.2 1.1 reduce_sum.166
  14.3 1.2 multiply_reduce_fusion
  15.5 17.8 %all-gather.3 = f32[16,2,256]{2,1,0:T(2,128)S(1)} all-gather(f32[1,2,256]{2,1,0:T(2,128)S(1)} %maximum_bitcast_fusion), channel_id=3, replica_groups=mesh['group'=2,'zhigh'=4,'yhigh'=4,'row'=2,'x'=4,'core'=2] {'group','x',..., dimensions={0}, use_global_device_ids=true | all-gather | bytes 34816 | tf_op jit(solution)/shard_map/all_gather | solution.py:95
  33.4 1.1 multiply_convert_fusion
  34.6 4.3 %collective-permute-start.1 = (bf16[512,128]{1,0:T(8,128)(2,1)S(1)}, bf16[512,128]{1,0:T(8,128)(2,1)S(1)}, u32[]{:S(2)}, u32[]{:S(2)}) collective-permute-start(bf16[512,128]{1,0:T(8,128)(2,1)S(1)} %pad_maximum_fusion.10), channel_id=1, source_target_pairs={{0,256},{256,0},{1,257},{257,1},{2,258},{258,2},{3,259},{259,3},{4... | collective-permute-start | bytes 393224 | tf_op jit(solution)/shard_map/ppermute | solution.py:18
  39.0 3.2 %collective-permute-start.8 = (bf16[256,192]{1,0:T(8,128)(2,1)S(1)}, bf16[256,192]{1,0:T(8,128)(2,1)S(1)}, u32[]{:S(2)}, u32[]{:S(2)}) collective-permute-start(bf16[256,192]{1,0:T(8,128)(2,1)S(1)} %get-tuple-element.45), channel_id=1, source_target_pairs={{0,8},{8,0},{1,9},{9,1},{2,10},{10,2},{3,11},{11,3},{4,12},{12,4},... | collective-permute-start | bytes 294920 | tf_op jit(solution)/shard_map/ppermute | solution.py:18
  42.2 2.3 %collective-permute-done.1 = bf16[512,128]{1,0:T(8,128)(2,1)S(1)} collective-permute-done((bf16[512,128]{1,0:T(8,128)(2,1)S(1)}, bf16[512,128]{1,0:T(8,128)(2,1)S(1)}, u32[]{:S(2)}, u32[]{:S(2)}) %collective-permute-start.1) | collective-permute-done | bytes 131104 | tf_op jit(solution)/shard_map/ppermute | solution.py:18
  44.6 3.2 %collective-permute-start.2 = (bf16[512,256]{1,0:T(8,128)(2,1)S(1)}, bf16[512,256]{1,0:T(8,128)(2,1)S(1)}, u32[]{:S(2)}, u32[]{:S(2)}) collective-permute-start(bf16[512,256]{1,0:T(8,128)(2,1)S(1)} %pad_maximum_fusion.4), channel_id=1, source_target_pairs={{0,2},{2,4},{4,6},{6,0},{1,3},{3,5},{5,7},{7,1},{8,10},{10,12},{12... | collective-permute-start | bytes 786440 | tf_op jit(solution)/shard_map/ppermute | solution.py:47
  47.9 3.4 %collective-permute-start.9 = (bf16[512,192]{1,0:T(8,128)(2,1)S(1)}, bf16[512,192]{1,0:T(8,128)(2,1)S(1)}, u32[]{:S(2)}, u32[]{:S(2)}) collective-permute-start(bf16[512,192]{1,0:T(8,128)(2,1)S(1)} %pad_maximum_fusion.5), channel_id=1, source_target_pairs={{0,256},{256,0},{1,257},{257,1},{2,258},{258,2},{3,259},{259,3},{4... | collective-permute-start | bytes 589832 | tf_op jit(solution)/shard_map/ppermute | solution.py:18
  51.3 3.9 %collective-permute-start.4 = (bf16[512,256]{1,0:T(8,128)(2,1)S(1)}, bf16[512,256]{1,0:T(8,128)(2,1)S(1)}, u32[]{:S(2)}, u32[]{:S(2)}) collective-permute-start(bf16[512,256]{1,0:T(8,128)(2,1)S(1)} %pad_maximum_fusion.4), channel_id=1, source_target_pairs={{0,6},{2,0},{4,2},{6,4},{1,7},{3,1},{5,3},{7,5},{8,14},{10,8},{12,... | collective-permute-start | bytes 786440 | tf_op jit(solution)/shard_map/ppermute | solution.py:48
  55.2 0.8 collective-permute-done.2
  56.0 1.9 collective-permute-start.3
  58.1 2.2 %collective-permute-done.4 = bf16[512,256]{1,0:T(8,128)(2,1)S(1)} collective-permute-done((bf16[512,256]{1,0:T(8,128)(2,1)S(1)}, bf16[512,256]{1,0:T(8,128)(2,1)S(1)}, u32[]{:S(2)}, u32[]{:S(2)}) %collective-permute-start.4) | collective-permute-done | bytes 262176 | tf_op jit(solution)/shard_map/ppermute | solution.py:48
  60.3 5.1 %collective-permute-start.5 = (bf16[256,256]{1,0:T(8,128)(2,1)S(1)}, bf16[256,256]{1,0:T(8,128)(2,1)S(1)}, u32[]{:S(2)}, u32[]{:S(2)}) collective-permute-start(bf16[256,256]{1,0:T(8,128)(2,1)S(1)} %slice.123), channel_id=1, source_target_pairs={{0,6},{2,0},{4,2},{6,4},{1,7},{3,1},{5,3},{7,5},{8,14},{10,8},{12,... | collective-permute-start | bytes 393224 | tf_op jit(solution)/shard_map/ppermute | solution.py:52
  65.6 1.9 collective-permute-start.10
  67.5 5.1 %collective-permute-start.12 = (bf16[512,384]{1,0:T(8,128)(2,1)S(1)}, bf16[512,384]{1,0:T(8,128)(2,1)S(1)}, u32[]{:S(2)}, u32[]{:S(2)}) collective-permute-start(bf16[512,384]{1,0:T(8,128)(2,1)S(1)} %pad_maximum_fusion.3), channel_id=1, source_target_pairs={{0,6},{2,0},{4,2},{6,4},{1,7},{3,1},{5,3},{7,5},{8,14},{10,8},{12,... | collective-permute-start | bytes 1179656 | tf_op jit(solution)/shard_map/ppermute | solution.py:48
  73.0 4.4 %collective-permute-done.10 = bf16[512,384]{1,0:T(8,128)(2,1)S(1)} collective-permute-done((bf16[512,384]{1,0:T(8,128)(2,1)S(1)}, bf16[512,384]{1,0:T(8,128)(2,1)S(1)}, u32[]{:S(2)}, u32[]{:S(2)}) %collective-permute-start.10) | collective-permute-done | bytes 393248 | tf_op jit(solution)/shard_map/ppermute | solution.py:47
  77.4 1.9 collective-permute-start.11
  79.6 5.1 %collective-permute-start.13 = (bf16[256,384]{1,0:T(8,128)(2,1)S(1)}, bf16[256,384]{1,0:T(8,128)(2,1)S(1)}, u32[]{:S(2)}, u32[]{:S(2)}) collective-permute-start(bf16[256,384]{1,0:T(8,128)(2,1)S(1)} %slice.133), channel_id=1, source_target_pairs={{0,6},{2,0},{4,2},{6,4},{1,7},{3,1},{5,3},{7,5},{8,14},{10,8},{12,... | collective-permute-start | bytes 589832 | tf_op jit(solution)/shard_map/ppermute | solution.py:52
  84.7 1.1 pad_maximum_fusion.1
  85.8 1.9 collective-permute-start.6
  87.9 0.6 select_select_fusion.3
  88.5 0.7 copy-done
  89.7 2.4 %collective-permute-start.14 = (bf16[512,1536]{1,0:T(8,128)(2,1)S(1)}, bf16[512,1536]{1,0:T(8,128)(2,1)S(1)}, u32[]{:S(2)}, u32[]{:S(2)}) collective-permute-start(bf16[512,1536]{1,0:T(8,128)(2,1)S(1)} %pad_maximum_fusion), channel_id=1, source_target_pairs={{0,1},{1,0},{2,3},{3,2},{4,5},{5,4},{6,7},{7,6},{8,9},{9,8},{10,11... | collective-permute-start | bytes 4718600 | tf_op jit(solution)/shard_map/ppermute | solution.py:18
  92.1 1.8 copy.46
  93.9 0.6 broadcast_multiply_fusion
  94.5 1.5 broadcast_select_fusion.1
  96.1 1.3 broadcast_select_fusion.5
  97.5 1.8 fusion.20
  99.9 4.8 %collective-permute-start.7 = (bf16[256,256]{0,1:T(8,128)(2,1)S(1)}, bf16[256,256]{0,1:T(8,128)(2,1)S(1)}, u32[]{:S(2)}, u32[]{:S(2)}) collective-permute-start(bf16[256,256]{0,1:T(8,128)(2,1)S(1)} %slice.177), channel_id=1, source_target_pairs={{0,8},{8,0},{1,9},{9,1},{2,10},{10,2},{3,11},{11,3},{4,12},{12,4},... | collective-permute-start | bytes 393224 | tf_op jit(solution)/shard_map/ppermute | solution.py:18
  104.7 0.6 fusion.21
  105.4 1.0 convolution_add_fusion.1
  106.4 1.9 collective-permute-start.15
  108.5 5.0 %collective-permute-done.15 = bf16[256,256]{0,1:T(8,128)(2,1)S(1)} collective-permute-done((bf16[256,256]{0,1:T(8,128)(2,1)S(1)}, bf16[256,256]{0,1:T(8,128)(2,1)S(1)}, u32[]{:S(2)}, u32[]{:S(2)}) %collective-permute-start.15) | collective-permute-done | bytes 131104 | tf_op jit(solution)/shard_map/ppermute | solution.py:18
  113.6 0.7 stack_broadcast_in_dim.3
  114.4 20.0 %all-gather.4 = f32[16,7,256]{2,1,0:T(8,128)S(1)} all-gather(f32[1,7,256]{2,1,0:T(8,128)S(1)} %bitcast.102), channel_id=4, replica_groups=mesh['group'=2,'zhigh'=4,'yhigh'=4,'row'=2,'x'=4,'core'=2] {'group','x',..., dimensions={0}, use_global_device_ids=true | all-gather | bytes 121856 | tf_op jit(solution)/shard_map/all_gather | solution.py:95
  134.7 2.3 %collective-permute-start.16 = (bf16[256,256]{0,1:T(8,128)(2,1)S(1)}, bf16[256,256]{0,1:T(8,128)(2,1)S(1)}, u32[]{:S(2)}, u32[]{:S(2)}) collective-permute-start(bf16[256,256]{0,1:T(8,128)(2,1)S(1)} %get-tuple-element.40), channel_id=1, source_target_pairs={{0,8},{8,0},{1,9},{9,1},{2,10},{10,2},{3,11},{11,3},{4,12},{12,4},... | collective-permute-start | bytes 393224 | tf_op jit(solution)/shard_map/ppermute | solution.py:18
  137.0 5.4 %collective-permute-done.16 = bf16[256,256]{0,1:T(8,128)(2,1)S(1)} collective-permute-done((bf16[256,256]{0,1:T(8,128)(2,1)S(1)}, bf16[256,256]{0,1:T(8,128)(2,1)S(1)}, u32[]{:S(2)}, u32[]{:S(2)}) %collective-permute-start.16) | collective-permute-done | bytes 131104 | tf_op jit(solution)/shard_map/ppermute | solution.py:18
  142.3 1.7 convolution_convert_fusion
  144.1 0.5 broadcast_select_fusion.3
  144.7 1.0 copy.59
  145.7 19.6 %all-to-all-start = ((bf16[16,128,256]{2,1,0:T(8,128)(2,1)}), bf16[16,128,256]{2,1,0:T(8,128)(2,1)S(1)}, u32[]{:S(2)}, u32[]{:S(2)}) async-start(bf16[16,128,256]{2,1,0:T(8,128)(2,1)} %bitcast.27), calls=%async_computation | async-start | bytes 2097152 | tf_op jit(solution)/shard_map/all_to_all | solution.py:179
  165.4 0.8 copy.58
  166.2 34.1 %all-to-all-done = bf16[16,128,256]{2,1,0:T(8,128)(2,1)S(1)} async-done(((bf16[16,128,256]{2,1,0:T(8,128)(2,1)}), bf16[16,128,256]{2,1,0:T(8,128)(2,1)S(1)}, u32[]{:S(2)}, u32[]{:S(2)}) %all-to-all-start) | async-done | bytes 1048608 | tf_op jit(solution)/shard_map/all_to_all | solution.py:179
  200.3 0.8 convert_reduce_fusion
  (94 shorter events, 3.3 us)
Async XLA Ops:
  7.2 87.3 %all-gather.7.cloned.1.call-start = ((), (), s32[]{:S(2)}) async-start(), calls=%async_computation.1 | async-start | bytes 2785280 | tf_op jit(solution)/shard_map/all_gather | solution.py:115
  9.7 24.9 %collective-permute-start = (bf16[256,128]{1,0:T(8,128)(2,1)S(1)}, bf16[256,128]{1,0:T(8,128)(2,1)S(1)}, u32[]{:S(2)}, u32[]{:S(2)}) collective-permute-start(bf16[256,128]{1,0:T(8,128)(2,1)S(1)} %get-tuple-element.54), channel_id=1, source_target_pairs={{0,8},{8,0},{1,9},{9,1},{2,10},{10,2},{3,11},{11,3},{4,12},{12,4},... | collective-permute-start | bytes 196616 | tf_op jit(solution)/shard_map/ppermute | solution.py:18
  34.6 9.9 %collective-permute-start.1 = (bf16[512,128]{1,0:T(8,128)(2,1)S(1)}, bf16[512,128]{1,0:T(8,128)(2,1)S(1)}, u32[]{:S(2)}, u32[]{:S(2)}) collective-permute-start(bf16[512,128]{1,0:T(8,128)(2,1)S(1)} %pad_maximum_fusion.10), channel_id=1, source_target_pairs={{0,256},{256,0},{1,257},{257,1},{2,258},{258,2},{3,259},{259,3},{4... | collective-permute-start | bytes 393224 | tf_op jit(solution)/shard_map/ppermute | solution.py:18
  39.0 8.8 %collective-permute-start.8 = (bf16[256,192]{1,0:T(8,128)(2,1)S(1)}, bf16[256,192]{1,0:T(8,128)(2,1)S(1)}, u32[]{:S(2)}, u32[]{:S(2)}) collective-permute-start(bf16[256,192]{1,0:T(8,128)(2,1)S(1)} %get-tuple-element.45), channel_id=1, source_target_pairs={{0,8},{8,0},{1,9},{9,1},{2,10},{10,2},{3,11},{11,3},{4,12},{12,4},... | collective-permute-start | bytes 294920 | tf_op jit(solution)/shard_map/ppermute | solution.py:18
  44.6 11.4 %collective-permute-start.2 = (bf16[512,256]{1,0:T(8,128)(2,1)S(1)}, bf16[512,256]{1,0:T(8,128)(2,1)S(1)}, u32[]{:S(2)}, u32[]{:S(2)}) collective-permute-start(bf16[512,256]{1,0:T(8,128)(2,1)S(1)} %pad_maximum_fusion.4), channel_id=1, source_target_pairs={{0,2},{2,4},{4,6},{6,0},{1,3},{3,5},{5,7},{7,1},{8,10},{10,12},{12... | collective-permute-start | bytes 786440 | tf_op jit(solution)/shard_map/ppermute | solution.py:47
  47.9 10.1 %collective-permute-start.9 = (bf16[512,192]{1,0:T(8,128)(2,1)S(1)}, bf16[512,192]{1,0:T(8,128)(2,1)S(1)}, u32[]{:S(2)}, u32[]{:S(2)}) collective-permute-start(bf16[512,192]{1,0:T(8,128)(2,1)S(1)} %pad_maximum_fusion.5), channel_id=1, source_target_pairs={{0,256},{256,0},{1,257},{257,1},{2,258},{258,2},{3,259},{259,3},{4... | collective-permute-start | bytes 589832 | tf_op jit(solution)/shard_map/ppermute | solution.py:18
  51.3 9.0 %collective-permute-start.4 = (bf16[512,256]{1,0:T(8,128)(2,1)S(1)}, bf16[512,256]{1,0:T(8,128)(2,1)S(1)}, u32[]{:S(2)}, u32[]{:S(2)}) collective-permute-start(bf16[512,256]{1,0:T(8,128)(2,1)S(1)} %pad_maximum_fusion.4), channel_id=1, source_target_pairs={{0,6},{2,0},{4,2},{6,4},{1,7},{3,1},{5,3},{7,5},{8,14},{10,8},{12,... | collective-permute-start | bytes 786440 | tf_op jit(solution)/shard_map/ppermute | solution.py:48
  56.0 16.6 %collective-permute-start.3 = (bf16[256,256]{1,0:T(8,128)(2,1)S(1)}, bf16[256,256]{1,0:T(8,128)(2,1)S(1)}, u32[]{:S(2)}, u32[]{:S(2)}) collective-permute-start(bf16[256,256]{1,0:T(8,128)(2,1)S(1)} %slice.122), channel_id=1, source_target_pairs={{0,2},{2,4},{4,6},{6,0},{1,3},{3,5},{5,7},{7,1},{8,10},{10,12},{12... | collective-permute-start | bytes 393224 | tf_op jit(solution)/shard_map/ppermute | solution.py:51
  60.3 12.4 %collective-permute-start.5 = (bf16[256,256]{1,0:T(8,128)(2,1)S(1)}, bf16[256,256]{1,0:T(8,128)(2,1)S(1)}, u32[]{:S(2)}, u32[]{:S(2)}) collective-permute-start(bf16[256,256]{1,0:T(8,128)(2,1)S(1)} %slice.123), channel_id=1, source_target_pairs={{0,6},{2,0},{4,2},{6,4},{1,7},{3,1},{5,3},{7,5},{8,14},{10,8},{12,... | collective-permute-start | bytes 393224 | tf_op jit(solution)/shard_map/ppermute | solution.py:52
  65.6 11.8 %collective-permute-start.10 = (bf16[512,384]{1,0:T(8,128)(2,1)S(1)}, bf16[512,384]{1,0:T(8,128)(2,1)S(1)}, u32[]{:S(2)}, u32[]{:S(2)}) collective-permute-start(bf16[512,384]{1,0:T(8,128)(2,1)S(1)} %pad_maximum_fusion.3), channel_id=1, source_target_pairs={{0,2},{2,4},{4,6},{6,0},{1,3},{3,5},{5,7},{7,1},{8,10},{10,12},{12... | collective-permute-start | bytes 1179656 | tf_op jit(solution)/shard_map/ppermute | solution.py:47
  67.5 12.0 %collective-permute-start.12 = (bf16[512,384]{1,0:T(8,128)(2,1)S(1)}, bf16[512,384]{1,0:T(8,128)(2,1)S(1)}, u32[]{:S(2)}, u32[]{:S(2)}) collective-permute-start(bf16[512,384]{1,0:T(8,128)(2,1)S(1)} %pad_maximum_fusion.3), channel_id=1, source_target_pairs={{0,6},{2,0},{4,2},{6,4},{1,7},{3,1},{5,3},{7,5},{8,14},{10,8},{12,... | collective-permute-start | bytes 1179656 | tf_op jit(solution)/shard_map/ppermute | solution.py:48
  73.0 12.9 %copy-start.7 = (bf16[512,256]{1,0:T(8,128)(2,1)}, bf16[512,256]{1,0:T(8,128)(2,1)S(1)}, u32[]{:S(2)}) copy-start(bf16[512,256]{1,0:T(8,128)(2,1)S(1)} %get-tuple-element.35) | copy-start | bytes 786436
  73.0 12.9 %copy-start.10 = (bf16[512,256]{1,0:T(8,128)(2,1)}, bf16[512,256]{1,0:T(8,128)(2,1)S(1)}, u32[]{:S(2)}) copy-start(bf16[512,256]{1,0:T(8,128)(2,1)S(1)} %get-tuple-element.36) | copy-start | bytes 786436
  73.0 12.9 %copy-start.13 = (bf16[512,256]{1,0:T(8,128)(2,1)}, bf16[512,256]{1,0:T(8,128)(2,1)S(1)}, u32[]{:S(2)}) copy-start(bf16[512,256]{1,0:T(8,128)(2,1)S(1)} %get-tuple-element.37) | copy-start | bytes 786436
  77.4 10.3 %collective-permute-start.11 = (bf16[256,384]{1,0:T(8,128)(2,1)S(1)}, bf16[256,384]{1,0:T(8,128)(2,1)S(1)}, u32[]{:S(2)}, u32[]{:S(2)}) collective-permute-start(bf16[256,384]{1,0:T(8,128)(2,1)S(1)} %slice.132), channel_id=1, source_target_pairs={{0,2},{2,4},{4,6},{6,0},{1,3},{3,5},{5,7},{7,1},{8,10},{10,12},{12... | collective-permute-start | bytes 589832 | tf_op jit(solution)/shard_map/ppermute | solution.py:51
  79.5 9.0 %copy-start.16 = (bf16[512,256]{1,0:T(8,128)(2,1)}, bf16[512,256]{1,0:T(8,128)(2,1)S(1)}, u32[]{:S(2)}) copy-start(bf16[512,256]{1,0:T(8,128)(2,1)S(1)} %select_select_fusion.6) | copy-start | bytes 786436
  79.6 8.3 %collective-permute-start.13 = (bf16[256,384]{1,0:T(8,128)(2,1)S(1)}, bf16[256,384]{1,0:T(8,128)(2,1)S(1)}, u32[]{:S(2)}, u32[]{:S(2)}) collective-permute-start(bf16[256,384]{1,0:T(8,128)(2,1)S(1)} %slice.133), channel_id=1, source_target_pairs={{0,6},{2,0},{4,2},{6,4},{1,7},{3,1},{5,3},{7,5},{8,14},{10,8},{12,... | collective-permute-start | bytes 589832 | tf_op jit(solution)/shard_map/ppermute | solution.py:52
  85.8 11.6 %collective-permute-start.6 = (bf16[512,1024]{1,0:T(8,128)(2,1)}, bf16[512,1024]{1,0:T(8,128)(2,1)}, u32[]{:S(2)}, u32[]{:S(2)}) collective-permute-start(bf16[512,1024]{1,0:T(8,128)(2,1)} %pad_maximum_fusion.1), channel_id=1, source_target_pairs={{0,1},{1,0},{2,3},{3,2},{4,5},{5,4},{6,7},{7,6},{8,9},{9,8},{10,11... | collective-permute-start | bytes 3145736 | tf_op jit(solution)/shard_map/ppermute | solution.py:18
  88.5 0.8 copy-start
  88.5 0.9 copy-start.2
  88.5 1.0 copy-start.4
  88.5 5.3 %copy-start.19 = (f32[256]{0:T(256)S(1)}, f32[256]{0:T(256)}, u32[]{:S(2)}) copy-start(f32[256]{0:T(256)} %param.13) | copy-start | bytes 3076
  89.7 15.0 %collective-permute-start.14 = (bf16[512,1536]{1,0:T(8,128)(2,1)S(1)}, bf16[512,1536]{1,0:T(8,128)(2,1)S(1)}, u32[]{:S(2)}, u32[]{:S(2)}) collective-permute-start(bf16[512,1536]{1,0:T(8,128)(2,1)S(1)} %pad_maximum_fusion), channel_id=1, source_target_pairs={{0,1},{1,0},{2,3},{3,2},{4,5},{5,4},{6,7},{7,6},{8,9},{9,8},{10,11... | collective-permute-start | bytes 4718600 | tf_op jit(solution)/shard_map/ppermute | solution.py:18
  97.3 1.9 copy-start.8
  97.4 1.9 copy-start.11
  97.4 1.9 copy-start.14
  97.4 1.9 copy-start.17
  99.8 5.5 %copy-start.1 = (bf16[512,384]{1,0:T(8,128)(2,1)S(1)}, bf16[512,384]{1,0:T(8,128)(2,1)}, u32[]{:S(2)}) copy-start(bf16[512,384]{1,0:T(8,128)(2,1)} %copy-done) | copy-start | bytes 1179652
  99.8 5.5 %copy-start.3 = (bf16[512,384]{1,0:T(8,128)(2,1)S(1)}, bf16[512,384]{1,0:T(8,128)(2,1)}, u32[]{:S(2)}) copy-start(bf16[512,384]{1,0:T(8,128)(2,1)} %copy-done.2) | copy-start | bytes 1179652
  99.8 5.5 %copy-start.5 = (bf16[512,384]{1,0:T(8,128)(2,1)S(1)}, bf16[512,384]{1,0:T(8,128)(2,1)}, u32[]{:S(2)}) copy-start(bf16[512,384]{1,0:T(8,128)(2,1)} %copy-done.4) | copy-start | bytes 1179652
  99.9 8.5 %collective-permute-start.7 = (bf16[256,256]{0,1:T(8,128)(2,1)S(1)}, bf16[256,256]{0,1:T(8,128)(2,1)S(1)}, u32[]{:S(2)}, u32[]{:S(2)}) collective-permute-start(bf16[256,256]{0,1:T(8,128)(2,1)S(1)} %slice.177), channel_id=1, source_target_pairs={{0,8},{8,0},{1,9},{9,1},{2,10},{10,2},{3,11},{11,3},{4,12},{12,4},... | collective-permute-start | bytes 393224 | tf_op jit(solution)/shard_map/ppermute | solution.py:18
  105.4 3.0 %copy-start.6 = (f32[256,256]{0,1:T(8,128)S(1)}, f32[256,256]{0,1:T(8,128)}, u32[]{:S(2)}) copy-start(f32[256,256]{0,1:T(8,128)} %copy.46) | copy-start | bytes 786436
  106.4 7.1 %collective-permute-start.15 = (bf16[256,256]{0,1:T(8,128)(2,1)S(1)}, bf16[256,256]{0,1:T(8,128)(2,1)S(1)}, u32[]{:S(2)}, u32[]{:S(2)}) collective-permute-start(bf16[256,256]{0,1:T(8,128)(2,1)S(1)} %slice.176), channel_id=1, source_target_pairs={{0,8},{8,0},{1,9},{9,1},{2,10},{10,2},{3,11},{11,3},{4,12},{12,4},... | collective-permute-start | bytes 393224 | tf_op jit(solution)/shard_map/ppermute | solution.py:18
  113.4 30.6 %copy-start.9 = (bf16[512,256]{1,0:T(8,128)(2,1)S(1)}, bf16[512,256]{1,0:T(8,128)(2,1)}, u32[]{:S(2)}) copy-start(bf16[512,256]{1,0:T(8,128)(2,1)} %copy-done.7) | copy-start | bytes 786436
  113.4 30.6 %copy-start.12 = (bf16[512,256]{1,0:T(8,128)(2,1)S(1)}, bf16[512,256]{1,0:T(8,128)(2,1)}, u32[]{:S(2)}) copy-start(bf16[512,256]{1,0:T(8,128)(2,1)} %copy-done.10) | copy-start | bytes 786436
  113.4 30.6 %copy-start.15 = (bf16[512,256]{1,0:T(8,128)(2,1)S(1)}, bf16[512,256]{1,0:T(8,128)(2,1)}, u32[]{:S(2)}) copy-start(bf16[512,256]{1,0:T(8,128)(2,1)} %copy-done.13) | copy-start | bytes 786436
  113.4 30.6 %copy-start.18 = (bf16[512,256]{1,0:T(8,128)(2,1)S(1)}, bf16[512,256]{1,0:T(8,128)(2,1)}, u32[]{:S(2)}) copy-start(bf16[512,256]{1,0:T(8,128)(2,1)} %copy-done.16) | copy-start | bytes 786436
  134.7 7.6 %collective-permute-start.16 = (bf16[256,256]{0,1:T(8,128)(2,1)S(1)}, bf16[256,256]{0,1:T(8,128)(2,1)S(1)}, u32[]{:S(2)}, u32[]{:S(2)}) collective-permute-start(bf16[256,256]{0,1:T(8,128)(2,1)S(1)} %get-tuple-element.40), channel_id=1, source_target_pairs={{0,8},{8,0},{1,9},{9,1},{2,10},{10,2},{3,11},{11,3},{4,12},{12,4},... | collective-permute-start | bytes 393224 | tf_op jit(solution)/shard_map/ppermute | solution.py:18
  145.7 54.5 %all-to-all-start = ((bf16[16,128,256]{2,1,0:T(8,128)(2,1)}), bf16[16,128,256]{2,1,0:T(8,128)(2,1)S(1)}, u32[]{:S(2)}, u32[]{:S(2)}) async-start(bf16[16,128,256]{2,1,0:T(8,128)(2,1)} %bitcast.27), calls=%async_computation | async-start | bytes 2097152 | tf_op jit(solution)/shard_map/all_to_all | solution.py:179
Sparse Core Ops, SparseCore 0:
  11.0 73.7 all-gather.6

commit v2 on v1

--- a/solution.py
+++ b/solution.py
@@ -18,13 +18,6 @@
     return lax.ppermute(values, axis, [(0, 1), (1, 0)])
 
 
-def ordered(mine, other, place, axis):
-    first = place == 0
-    return jnp.concatenate(
-        [jnp.where(first, mine, other), jnp.where(first, other, mine)], axis=axis
-    )
-
-
 def my_half(values, place):
     half = values.shape[1] // 2
     return (
@@ -38,31 +31,15 @@
     return jnp.concatenate([keep, swap(give, "row")], axis=0)
 
 
-def gather_line(values):
-    count = lax.axis_size("x")
-    place = lax.axis_index("x")
-    ahead = [(i, (i + 1) % count) for i in range(count)]
-    back = [(i, (i - 1) % count) for i in range(count)]
-    rows = values.shape[0] // 2
-    previous = lax.ppermute(values, "x", ahead)
-    following = lax.ppermute(values, "x", back)
-    opposite = jnp.concatenate(
-        [
-            lax.ppermute(previous[:rows], "x", ahead),
-            lax.ppermute(following[rows:], "x", back),
-        ],
-        axis=0,
+def gather_features(values):
+    axes = ("group", "x")
+    count = lax.axis_size(axes)
+    copies = jnp.broadcast_to(values[None], (count, *values.shape))
+    line = lax.all_to_all(copies, axes, 0, 0, tiled=True)
+    other = swap(line, "core")
+    return tuple(
+        part.transpose(1, 0, 2).reshape(values.shape[0], -1) for part in (line, other)
     )
-    pieces = [values, previous, opposite, following]
-    return jnp.concatenate(
-        [lax.select_n((place - j) & (count - 1), *pieces) for j in range(count)], axis=1
-    )
-
-
-def gather_features(values):
-    pair = ordered(values, swap(values, "group"), lax.axis_index("group"), 1)
-    line = gather_line(pair)
-    return line, swap(line, "core")
 
 
 def both(first, place):
@@ -116,7 +93,7 @@
         jnp.concatenate([out_weight, projection], axis=0), GATHER_AXES, axis=0
     )
     weights = weights.reshape(groups, lanes, cores, *weights.shape[1:])
-    weights = weights.transpose(2, 1, 0, 3, 4)
+    weights = weights.transpose(2, 0, 1, 3, 4)
     core = lax.axis_index("core")
     out_full = both(weights[:, :, :, :depth].reshape(cores, -1, width), core)
     projection_full = both(weights[:, :, :, depth:].reshape(cores, -1, width), core)
@@ -175,7 +152,7 @@
         for half in context
     ]
     partial = jnp.stack(both(partial, core), axis=0)
-    partial = partial.reshape(cores, lanes, groups, depth, width).transpose(2, 1, 0, 3, 4)
+    partial = partial.reshape(cores, groups, lanes, depth, width).transpose(1, 2, 0, 3, 4)
     parts = lax.all_to_all(partial.reshape(blocks, depth, width), GATHER_AXES, 0, 0, tiled=True)
     weight_grad = jnp.sum(parts.astype(F32), axis=0)
     return (student_out, weight_grad)

time: 209 us -> 205 us (0.981)
  the two profiles are of different devices: /device:TPU:64 before, /device:TPU:24 now
where the time goes in v2:
time: 205 us
  waiting for transfers between devices  84.3 us (41%)
  blocking collectives  43.9 us (21%)
  starting transfers between devices  42.1 us (21%)
  between operations  14.3 us (7%)
  other arithmetic  8.57 us (4%)
  matrix products  7.15 us (3%)
  local copies, waits for them, and re-layouts  4.33 us (2%)
    all_gather x2, blocking collectives, gather_rows(): return lax.all_gather(jnp.stack(rows, axis=0), FEATURE_AXES, axis=0)  43.9 us
    all_to_all x2, waiting for transfers between devices, gather_features(): line = lax.all_to_all(copies, axes, 0, 0, tiled=True)  37.1 us
    all_to_all x1, waiting for transfers between devices, shards(): lax.all_to_all(partial.reshape(blocks, depth, width), GATHER_AXES, 0, 0,...  33.3 us
    ppermute x7, starting transfers between devices, swap(): return lax.ppermute(values, axis, [(0, 1), (1, 0)])  18.5 us
    ppermute x7, waiting for transfers between devices, swap(): return lax.ppermute(values, axis, [(0, 1), (1, 0)])  13.9 us
    all_to_all x1, starting transfers between devices, shards(): lax.all_to_all(partial.reshape(blocks, depth, width), GATHER_AXES, 0, 0,...  12.9 us
    all_to_all x2, starting transfers between devices, gather_features(): line = lax.all_to_all(copies, axes, 0, 0, tiled=True)  10.7 us
  transfers between devices with their start and end apart: 11, of which 6 were waited for; matrix products, arithmetic and copies ran while one was open for 7% of the time, Pallas kernels for 0%

profile of v2, /device:TPU:24, one launch (start us, length us, event | category | flops | bytes accessed | tf_op | source)
XLA Modules:
  0.0 204.6 jit_solution(7453701146270776462)
XLA Ops:
  7.2 0.0 all-gather.7.cloned.1.call-start
  7.2 0.9 broadcast_select_fusion.9
  8.1 2.4 %collective-permute-start = (bf16[256,128]{1,0:T(8,128)(2,1)S(1)}, bf16[256,128]{1,0:T(8,128)(2,1)S(1)}, u32[]{:S(2)}, u32[]{:S(2)}) collective-permute-start(bf16[256,128]{1,0:T(8,128)(2,1)S(1)} %get-tuple-element.41), channel_id=1, source_target_pairs={{0,8},{8,0},{1,9},{9,1},{2,10},{10,2},{3,11},{11,3},{4,12},{12,4},... | collective-permute-start | bytes 196616 | tf_op jit(solution)/shard_map/ppermute | solution.py:18
  10.5 1.6 pad_maximum_fusion.5
  12.0 0.0 all-gather.7.cloned.1.call-update
  12.1 1.1 reduce_sum.166
  13.2 1.1 collective-permute-done
  14.3 0.1 copy.31
  14.4 1.1 broadcast_in_dim.4
  15.5 6.2 %all-to-all-start = ((bf16[8,512,128]{1,2,0:T(8,128)(2,1)}), bf16[8,512,128]{1,2,0:T(8,128)(2,1)S(1)}, u32[]{:S(2)}, u32[]{:S(2)}) async-start(bf16[8,512,128]{1,2,0:T(8,128)(2,1)} %broadcast_in_dim.4), calls=%async_computation | async-start | bytes 2097152 | tf_op jit(solution)/shard_map/all_to_all | solution.py:38
  21.8 0.2 multiply_reduce_fusion
  22.0 25.1 %all-gather.3 = f32[16,2,256]{2,1,0:T(2,128)S(1)} all-gather(f32[1,2,256]{2,1,0:T(2,128)S(1)} %maximum_bitcast_fusion), channel_id=3, replica_groups=mesh['group'=2,'zhigh'=4,'yhigh'=4,'row'=2,'x'=4,'core'=2] {'group','x',..., dimensions={0}, use_global_device_ids=true | all-gather | bytes 34816 | tf_op jit(solution)/shard_map/all_gather | solution.py:72
  47.2 0.1 multiply_convert_fusion
  47.3 0.1 broadcast_select_fusion.7
  47.4 3.1 %collective-permute-start.3 = (bf16[256,192]{1,0:T(8,128)(2,1)S(1)}, bf16[256,192]{1,0:T(8,128)(2,1)S(1)}, u32[]{:S(2)}, u32[]{:S(2)}) collective-permute-start(bf16[256,192]{1,0:T(8,128)(2,1)S(1)} %get-tuple-element.32), channel_id=1, source_target_pairs={{0,8},{8,0},{1,9},{9,1},{2,10},{10,2},{3,11},{11,3},{4,12},{12,4},... | collective-permute-start | bytes 294920 | tf_op jit(solution)/shard_map/ppermute | solution.py:18
  50.5 4.5 %collective-permute-done.3 = bf16[256,192]{1,0:T(8,128)(2,1)S(1)} collective-permute-done((bf16[256,192]{1,0:T(8,128)(2,1)S(1)}, bf16[256,192]{1,0:T(8,128)(2,1)S(1)}, u32[]{:S(2)}, u32[]{:S(2)}) %collective-permute-start.3) | collective-permute-done | bytes 98336 | tf_op jit(solution)/shard_map/ppermute | solution.py:18
  55.1 0.1 copy.34
  55.3 1.3 broadcast_in_dim.5
  56.6 4.4 %all-to-all-start.1 = ((bf16[8,512,192]{1,2,0:T(8,128)(2,1)}), bf16[8,512,192]{1,2,0:T(8,128)(2,1)}, u32[]{:S(2)}, u32[]{:S(2)}) async-start(bf16[8,512,192]{1,2,0:T(8,128)(2,1)} %broadcast_in_dim.5), calls=%async_computation.1 | async-start | bytes 3145728 | tf_op jit(solution)/shard_map/all_to_all | solution.py:38
  61.0 1.9 collective-permute-start.1
  62.9 0.1 copy.32
  63.1 37.1 %all-to-all-done.1 = bf16[8,512,192]{1,2,0:T(8,128)(2,1)} async-done(((bf16[8,512,192]{1,2,0:T(8,128)(2,1)}), bf16[8,512,192]{1,2,0:T(8,128)(2,1)}, u32[]{:S(2)}, u32[]{:S(2)}) %all-to-all-start.1) | async-done | bytes 1572896 | tf_op jit(solution)/shard_map/all_to_all | solution.py:38
  100.1 1.9 collective-permute-start.4
  102.1 0.6 broadcast_multiply_fusion
  102.7 1.3 broadcast_select_fusion.4
  104.0 0.5 fusion.20
  104.5 1.9 convolution_add_fusion
  106.4 2.4 %collective-permute-start.2 = (bf16[256,256]{0,1:T(8,128)(2,1)S(1)}, bf16[256,256]{0,1:T(8,128)(2,1)S(1)}, u32[]{:S(2)}, u32[]{:S(2)}) collective-permute-start(bf16[256,256]{0,1:T(8,128)(2,1)S(1)} %slice.157), channel_id=1, source_target_pairs={{0,8},{8,0},{1,9},{9,1},{2,10},{10,2},{3,11},{11,3},{4,12},{12,4},... | collective-permute-start | bytes 393224 | tf_op jit(solution)/shard_map/ppermute | solution.py:18
  108.8 0.1 broadcast_select_fusion
  108.9 2.0 fusion.21
  111.0 0.6 convolution_add_fusion.1
  111.7 3.4 %collective-permute-start.5 = (bf16[256,256]{0,1:T(8,128)(2,1)S(1)}, bf16[256,256]{0,1:T(8,128)(2,1)S(1)}, u32[]{:S(2)}, u32[]{:S(2)}) collective-permute-start(bf16[256,256]{0,1:T(8,128)(2,1)S(1)} %slice.156), channel_id=1, source_target_pairs={{0,8},{8,0},{1,9},{9,1},{2,10},{10,2},{3,11},{11,3},{4,12},{12,4},... | collective-permute-start | bytes 393224 | tf_op jit(solution)/shard_map/ppermute | solution.py:18
  115.1 0.1 fusion.18
  115.2 4.0 %collective-permute-done.5 = bf16[256,256]{0,1:T(8,128)(2,1)S(1)} collective-permute-done((bf16[256,256]{0,1:T(8,128)(2,1)S(1)}, bf16[256,256]{0,1:T(8,128)(2,1)S(1)}, u32[]{:S(2)}, u32[]{:S(2)}) %collective-permute-start.5) | collective-permute-done | bytes 131104 | tf_op jit(solution)/shard_map/ppermute | solution.py:18
  119.2 0.2 multiply_reduce_fusion.2
  119.3 0.6 stack_broadcast_in_dim.3
  120.0 18.7 %all-gather.4 = f32[16,7,256]{2,1,0:T(8,128)S(1)} all-gather(f32[1,7,256]{2,1,0:T(8,128)S(1)} %bitcast.124), channel_id=4, replica_groups=mesh['group'=2,'zhigh'=4,'yhigh'=4,'row'=2,'x'=4,'core'=2] {'group','x',..., dimensions={0}, use_global_device_ids=true | all-gather | bytes 121856 | tf_op jit(solution)/shard_map/all_gather | solution.py:72
  138.8 0.1 slice_reduce_fusion
  138.9 0.2 multiply_convert_fusion.1
  139.1 3.4 %collective-permute-start.6 = (bf16[256,256]{0,1:T(8,128)(2,1)S(1)}, bf16[256,256]{0,1:T(8,128)(2,1)S(1)}, u32[]{:S(2)}, u32[]{:S(2)}) collective-permute-start(bf16[256,256]{0,1:T(8,128)(2,1)S(1)} %get-tuple-element.29), channel_id=1, source_target_pairs={{0,8},{8,0},{1,9},{9,1},{2,10},{10,2},{3,11},{11,3},{4,12},{12,4},... | collective-permute-start | bytes 393224 | tf_op jit(solution)/shard_map/ppermute | solution.py:18
  142.5 4.3 %collective-permute-done.6 = bf16[256,256]{0,1:T(8,128)(2,1)S(1)} collective-permute-done((bf16[256,256]{0,1:T(8,128)(2,1)S(1)}, bf16[256,256]{0,1:T(8,128)(2,1)S(1)}, u32[]{:S(2)}, u32[]{:S(2)}) %collective-permute-start.6) | collective-permute-done | bytes 131104 | tf_op jit(solution)/shard_map/ppermute | solution.py:18
  146.7 1.7 convolution_convert_fusion
  148.4 0.5 broadcast_select_fusion.3
  148.9 1.1 pad_maximum_fusion
  150.0 12.9 %all-to-all-start.2 = ((bf16[16,128,256]{2,1,0:T(8,128)(2,1)}), bf16[16,128,256]{2,1,0:T(8,128)(2,1)S(1)}, u32[]{:S(2)}, u32[]{:S(2)}) async-start(bf16[16,128,256]{2,1,0:T(8,128)(2,1)} %bitcast.39), calls=%async_computation.2 | async-start | bytes 2097152 | tf_op jit(solution)/shard_map/all_to_all | solution.py:156
  162.8 0.8 copy.43
  163.7 33.3 %all-to-all-done.2 = bf16[16,128,256]{2,1,0:T(8,128)(2,1)S(1)} async-done(((bf16[16,128,256]{2,1,0:T(8,128)(2,1)}), bf16[16,128,256]{2,1,0:T(8,128)(2,1)S(1)}, u32[]{:S(2)}, u32[]{:S(2)}) %all-to-all-start.2) | async-done | bytes 1048608 | tf_op jit(solution)/shard_map/all_to_all | solution.py:156
  197.0 0.8 convert_reduce_fusion
  (30 shorter events, 0.3 us)
Async XLA Ops:
  7.2 95.5 %all-gather.7.cloned.1.call-start = ((), (), s32[]{:S(2)}) async-start(), calls=%async_computation.3 | async-start | bytes 2785280 | tf_op jit(solution)/shard_map/all_gather | solution.py:92
  8.1 6.2 %collective-permute-start = (bf16[256,128]{1,0:T(8,128)(2,1)S(1)}, bf16[256,128]{1,0:T(8,128)(2,1)S(1)}, u32[]{:S(2)}, u32[]{:S(2)}) collective-permute-start(bf16[256,128]{1,0:T(8,128)(2,1)S(1)} %get-tuple-element.41), channel_id=1, source_target_pairs={{0,8},{8,0},{1,9},{9,1},{2,10},{10,2},{3,11},{11,3},{4,12},{12,4},... | collective-permute-start | bytes 196616 | tf_op jit(solution)/shard_map/ppermute | solution.py:18
  14.4 7.3 %copy-start = (f32[256,384]{1,0:T(8,128)S(1)}, f32[256,384]{1,0:T(8,128)}, u32[]{:S(2)}) copy-start(f32[256,384]{1,0:T(8,128)} %param.7) | copy-start | bytes 1179652
  15.5 31.7 %copy-start.4 = (f32[384]{0:T(512)S(1)}, f32[384]{0:T(512)}, u32[]{:S(2)}) copy-start(f32[384]{0:T(512)} %param.8) | copy-start | bytes 4612
  15.5 39.8 %all-to-all-start = ((bf16[8,512,128]{1,2,0:T(8,128)(2,1)}), bf16[8,512,128]{1,2,0:T(8,128)(2,1)S(1)}, u32[]{:S(2)}, u32[]{:S(2)}) async-start(bf16[8,512,128]{1,2,0:T(8,128)(2,1)} %broadcast_in_dim.4), calls=%async_computation | async-start | bytes 2097152 | tf_op jit(solution)/shard_map/all_to_all | solution.py:38
  47.4 7.6 %collective-permute-start.3 = (bf16[256,192]{1,0:T(8,128)(2,1)S(1)}, bf16[256,192]{1,0:T(8,128)(2,1)S(1)}, u32[]{:S(2)}, u32[]{:S(2)}) collective-permute-start(bf16[256,192]{1,0:T(8,128)(2,1)S(1)} %get-tuple-element.32), channel_id=1, source_target_pairs={{0,8},{8,0},{1,9},{9,1},{2,10},{10,2},{3,11},{11,3},{4,12},{12,4},... | collective-permute-start | bytes 294920 | tf_op jit(solution)/shard_map/ppermute | solution.py:18
  56.6 6.4 %copy-start.2 = (f32[256,256]{1,0:T(8,128)S(1)}, f32[256,256]{1,0:T(8,128)}, u32[]{:S(2)}) copy-start(f32[256,256]{1,0:T(8,128)} %param.10) | copy-start | bytes 786436
  56.6 45.5 %copy-start.3 = (f32[256]{0:T(256)S(1)}, f32[256]{0:T(256)}, u32[]{:S(2)}) copy-start(f32[256]{0:T(256)} %param.13) | copy-start | bytes 3076
  56.6 43.6 %all-to-all-start.1 = ((bf16[8,512,192]{1,2,0:T(8,128)(2,1)}), bf16[8,512,192]{1,2,0:T(8,128)(2,1)}, u32[]{:S(2)}, u32[]{:S(2)}) async-start(bf16[8,512,192]{1,2,0:T(8,128)(2,1)} %broadcast_in_dim.5), calls=%async_computation.1 | async-start | bytes 3145728 | tf_op jit(solution)/shard_map/all_to_all | solution.py:38
  61.0 43.5 %collective-permute-start.1 = (bf16[8,512,128]{1,2,0:T(8,128)(2,1)S(1)}, bf16[8,512,128]{1,2,0:T(8,128)(2,1)}, u32[]{:S(2)}, u32[]{:S(2)}) collective-permute-start(bf16[8,512,128]{1,2,0:T(8,128)(2,1)S(1)} %all-to-all-done), channel_id=1, source_target_pairs={{0,1},{1,0},{2,3},{3,2},{4,5},{5,4},{6,7},{7,6},{8,9},{9,8},{10,11... | collective-permute-start | bytes 3145736 | tf_op jit(solution)/shard_map/ppermute | solution.py:18
  100.1 10.8 %collective-permute-start.4 = (bf16[8,512,192]{1,2,0:T(8,128)(2,1)}, bf16[8,512,192]{1,2,0:T(8,128)(2,1)S(1)}, u32[]{:S(2)}, u32[]{:S(2)}) collective-permute-start(bf16[8,512,192]{1,2,0:T(8,128)(2,1)} %all-to-all-done.1), channel_id=1, source_target_pairs={{0,1},{1,0},{2,3},{3,2},{4,5},{5,4},{6,7},{7,6},{8,9},{9,8},{10,11... | collective-permute-start | bytes 4718600 | tf_op jit(solution)/shard_map/ppermute | solution.py:18
  104.4 4.4 %copy-start.1 = (bf16[5120,256]{1,0:T(8,128)(2,1)S(1)}, bf16[5120,256]{1,0:T(8,128)(2,1)}, u32[]{:S(2)}) copy-start(bf16[5120,256]{1,0:T(8,128)(2,1)} %all-gather.7.cloned.1.call-done) | copy-start | bytes 7864324
  106.4 8.7 %collective-permute-start.2 = (bf16[256,256]{0,1:T(8,128)(2,1)S(1)}, bf16[256,256]{0,1:T(8,128)(2,1)S(1)}, u32[]{:S(2)}, u32[]{:S(2)}) collective-permute-start(bf16[256,256]{0,1:T(8,128)(2,1)S(1)} %slice.157), channel_id=1, source_target_pairs={{0,8},{8,0},{1,9},{9,1},{2,10},{10,2},{3,11},{11,3},{4,12},{12,4},... | collective-permute-start | bytes 393224 | tf_op jit(solution)/shard_map/ppermute | solution.py:18
  111.7 7.5 %collective-permute-start.5 = (bf16[256,256]{0,1:T(8,128)(2,1)S(1)}, bf16[256,256]{0,1:T(8,128)(2,1)S(1)}, u32[]{:S(2)}, u32[]{:S(2)}) collective-permute-start(bf16[256,256]{0,1:T(8,128)(2,1)S(1)} %slice.156), channel_id=1, source_target_pairs={{0,8},{8,0},{1,9},{9,1},{2,10},{10,2},{3,11},{11,3},{4,12},{12,4},... | collective-permute-start | bytes 393224 | tf_op jit(solution)/shard_map/ppermute | solution.py:18
  139.1 7.6 %collective-permute-start.6 = (bf16[256,256]{0,1:T(8,128)(2,1)S(1)}, bf16[256,256]{0,1:T(8,128)(2,1)S(1)}, u32[]{:S(2)}, u32[]{:S(2)}) collective-permute-start(bf16[256,256]{0,1:T(8,128)(2,1)S(1)} %get-tuple-element.29), channel_id=1, source_target_pairs={{0,8},{8,0},{1,9},{9,1},{2,10},{10,2},{3,11},{11,3},{4,12},{12,4},... | collective-permute-start | bytes 393224 | tf_op jit(solution)/shard_map/ppermute | solution.py:18
  150.0 47.0 %all-to-all-start.2 = ((bf16[16,128,256]{2,1,0:T(8,128)(2,1)}), bf16[16,128,256]{2,1,0:T(8,128)(2,1)S(1)}, u32[]{:S(2)}, u32[]{:S(2)}) async-start(bf16[16,128,256]{2,1,0:T(8,128)(2,1)} %bitcast.39), calls=%async_computation.2 | async-start | bytes 2097152 | tf_op jit(solution)/shard_map/all_to_all | solution.py:156
Sparse Core Ops, SparseCore 0:
  12.2 82.3 all-gather.6

commit v3 on v2

--- a/solution.py
+++ b/solution.py
@@ -9,37 +9,34 @@
 BF16 = jnp.bfloat16
 F32 = jnp.float32
 
-TOKEN_AXES = ("zhigh", "yhigh", "row")
-GATHER_AXES = ("zhigh", "yhigh")
-FEATURE_AXES = ("group", "x", "core")
+TOKEN_AXES = ("zhigh", "pair", "y")
+GATHER_AXES = ("zhigh", "y")
+FEATURE_AXES = ("group", "xhigh", "xlow", "core")
+CHIP_AXES = ("group", "xhigh", "xlow")
 
 
 def swap(values, axis):
     return lax.ppermute(values, axis, [(0, 1), (1, 0)])
 
 
-def my_half(values, place):
-    half = values.shape[1] // 2
-    return (
-        jnp.where(place == 0, values[:, :half], values[:, half:]),
-        jnp.where(place == 0, values[:, half:], values[:, :half]),
-    )
+def turned(values):
+    return lax.ppermute(values, ("pair", "xhigh"), [(0, 0), (1, 2), (2, 1), (3, 3)])
 
 
-def split_tokens(values, row):
-    keep, give = my_half(values, row)
-    return jnp.concatenate([keep, swap(give, "row")], axis=0)
-
-
-def gather_features(values):
-    axes = ("group", "x")
-    count = lax.axis_size(axes)
-    copies = jnp.broadcast_to(values[None], (count, *values.shape))
-    line = lax.all_to_all(copies, axes, 0, 0, tiled=True)
+def gather_features(values, after=None):
+    tokens, width = values.shape
+    count = lax.axis_size(CHIP_AXES)
+    copies = jnp.broadcast_to(values[None], (count, tokens, width))
+    line = lax.all_to_all(copies, CHIP_AXES, 0, 0, tiled=True)
+    if after is not None:
+        line, after = lax.optimization_barrier((line, after))
     other = swap(line, "core")
-    return tuple(
-        part.transpose(1, 0, 2).reshape(values.shape[0], -1) for part in (line, other)
+    shape = (lax.axis_size("group"), 2, lax.axis_size("xlow"), tokens, width)
+    gathered = tuple(
+        part.reshape(shape).transpose(1, 3, 0, 2, 4).reshape(2 * tokens, -1)
+        for part in (line, other)
     )
+    return gathered, after
 
 
 def both(first, place):
@@ -81,9 +78,10 @@
     out_weight,
     student_gain,
 ):
-    row = lax.axis_index("row")
-    groups, lanes, cores = (lax.axis_size(name) for name in FEATURE_AXES)
-    blocks = groups * lanes * cores
+    pair = lax.axis_index("pair")
+    core = lax.axis_index("core")
+    groups, lanes, cores = (lax.axis_size(name) for name in ("group", "xlow", "core"))
+    blocks = lax.axis_size(FEATURE_AXES)
     tokens = teacher_stream.shape[0]
     token_count = tokens * lax.axis_size(TOKEN_AXES)
     width = student_stream.shape[1]
@@ -92,24 +90,26 @@
     weights = lax.all_gather(
         jnp.concatenate([out_weight, projection], axis=0), GATHER_AXES, axis=0
     )
-    weights = weights.reshape(groups, lanes, cores, *weights.shape[1:])
-    weights = weights.transpose(2, 0, 1, 3, 4)
-    core = lax.axis_index("core")
-    out_full = both(weights[:, :, :, :depth].reshape(cores, -1, width), core)
-    projection_full = both(weights[:, :, :, depth:].reshape(cores, -1, width), core)
-
-    context = gather_features(split_tokens(student_context, row))
-
+    context = turned(student_context)
     teacher_mean, _, teacher_square = moments(teacher_stream)
     table = gather_rows([teacher_mean, teacher_square])
+    context, table = lax.optimization_barrier((context, table))
     mean, _, inv_std = combine(table[:, 0], table[:, 1], teacher_stream.shape[1])
     hidden = ((teacher_stream - mean[:, None]) * inv_std[:, None] * teacher_gain).astype(BF16)
-    hidden = gather_features(split_tokens(hidden, row))
+    context, _ = gather_features(context)
+    hidden, weights = gather_features(turned(hidden), weights)
 
-    branch = product(context, out_full)
-    pre_norm = student_stream + (branch[:tokens] + swap(branch[tokens:].astype(BF16), "row").astype(F32))
-    target = product(hidden, projection_full)
-    target = target[:tokens] + swap(target[tokens:].astype(BF16), "row").astype(F32)
+    weights = weights.reshape(groups, lanes, cores, 2, *weights.shape[1:])
+    weights = weights.transpose(2, 0, 1, 3, 4, 5)
+    out_full = both(weights[..., :depth, :].reshape(cores, -1, width), core)
+    projection_full = both(weights[..., depth:, :].reshape(cores, -1, width), core)
+
+    def shared(partial):
+        mine, other = both(partial.reshape(2, tokens, width), pair)
+        return mine + swap(other.astype(BF16), "pair").astype(F32)
+
+    pre_norm = student_stream + shared(product(context, out_full))
+    target = shared(product(hidden, projection_full))
 
     block_mean, centered, square = moments(pre_norm)
     gain_square = student_gain * student_gain
@@ -143,7 +143,7 @@
     grad_pre = (
         inv_std[:, None] * (grad_norm - first_mean[:, None] - normalized * second_mean[:, None])
     ).astype(BF16)
-    grad_pre = jnp.concatenate([grad_pre, swap(grad_pre, "row")], axis=0)
+    grad_pre = jnp.concatenate(both((grad_pre, swap(grad_pre, "pair")), pair), axis=0)
 
     partial = [
         lax.dot_general(
@@ -152,21 +152,21 @@
         for half in context
     ]
     partial = jnp.stack(both(partial, core), axis=0)
-    partial = partial.reshape(cores, groups, lanes, depth, width).transpose(1, 2, 0, 3, 4)
-    parts = lax.all_to_all(partial.reshape(blocks, depth, width), GATHER_AXES, 0, 0, tiled=True)
+    partial = partial.reshape(cores, groups, lanes, 2 * depth, width).transpose(1, 2, 0, 3, 4)
+    parts = lax.all_to_all(partial.reshape(-1, depth, width), GATHER_AXES, 0, 0, tiled=True)
     weight_grad = jnp.sum(parts.astype(F32), axis=0)
     return (student_out, weight_grad)
 
 
 def solution(mesh):
     groups, token_blocks, columns = (mesh.shape[name] for name in ("group", "dp", "tensor"))
-    cores = 2
-    zhigh = min(4, token_blocks // 4)
+    cores, xhigh, pairs = 2, 2, 2
+    zhigh = groups
     fine = Mesh(
         mesh.devices.reshape(
-            groups, zhigh, token_blocks // (2 * zhigh), 2, columns // cores, cores
+            groups, zhigh, pairs, token_blocks // (zhigh * pairs), xhigh, columns // (xhigh * cores), cores
         ),
-        ("group", "zhigh", "yhigh", "row", "x", "core"),
+        ("group", "zhigh", "pair", "y", "xhigh", "xlow", "core"),
     )
     split = P(TOKEN_AXES, FEATURE_AXES)
     return jax.shard_map(

time: 205 us -> 256 us (1.25)
  the two profiles are of different devices: /device:TPU:24 before, /device:TPU:8 now
where the time goes in v3:
time: 256 us
  waiting for transfers between devices  131 us (51%)
  blocking collectives  43.6 us (17%)
  starting transfers between devices  30.6 us (12%)
  local copies, waits for them, and re-layouts  21.7 us (8%)
  between operations  14.4 us (6%)
  other arithmetic  9.65 us (4%)
  matrix products  5.25 us (2%)
    all_to_all x2, waiting for transfers between devices, gather_features(): line = lax.all_to_all(copies, CHIP_AXES, 0, 0, tiled=True)  49.9 us
    all_gather x2, blocking collectives, gather_rows(): return lax.all_gather(jnp.stack(rows, axis=0), FEATURE_AXES, axis=0)  43.6 us
    all_gather x1, waiting for transfers between devices, shards(): lax.all_gather(jnp.concatenate([out_weight, projection], axis=0), GATHER_...  30.4 us
    all_to_all x1, waiting for transfers between devices, shards(): lax.all_to_all(partial.reshape(-1, depth, width), GATHER_AXES, 0, 0, tile...  29.1 us
    ppermute x5, waiting for transfers between devices, swap(): return lax.ppermute(values, axis, [(0, 1), (1, 0)])  21.2 us
    ppermute x5, starting transfers between devices, swap(): return lax.ppermute(values, axis, [(0, 1), (1, 0)])  14.3 us
    transpose x4, local copies, waits for them, and re-layouts, gather_features(): part.reshape(shape).transpose(1, 3, 0, 2, 4).reshape(2 * tokens, -1)  8.99 us
    all_to_all x2, starting transfers between devices, gather_features(): line = lax.all_to_all(copies, CHIP_AXES, 0, 0, tiled=True)  8.42 us
  transfers between devices with their start and end apart: 11, of which 7 were waited for; matrix products, arithmetic and copies ran while one was open for 10% of the time, Pallas kernels for 0%

profile of v3, /device:TPU:8, one launch (start us, length us, event | category | flops | bytes accessed | tf_op | source)
XLA Modules:
  0.0 255.7 jit_solution(2803055041680264081)
XLA Ops:
  7.2 1.6 collective-permute-start
  8.8 1.6 pad_maximum_fusion.4
  10.4 1.1 reduce_sum.162
  11.5 1.2 multiply_reduce_fusion
  12.7 25.9 %all-gather.3 = f32[16,2,256]{2,1,0:T(2,128)S(1)} all-gather(f32[1,2,256]{2,1,0:T(2,128)S(1)} %maximum_bitcast_fusion), channel_id=2, replica_groups=mesh['group'=2,'zhigh'=2,'pair'=2,'y'=8,'xhigh'=2,'xlow'=2,'core'=2] {'g..., dimensions={0}, use_global_device_ids=true | all-gather | bytes 34816 | tf_op jit(solution)/shard_map/all_gather | solution.py:69
  38.6 1.1 broadcast_in_dim.4
  39.7 3.6 %all-to-all-start = ((bf16[8,256,256]{2,1,0:T(8,128)(2,1)}), bf16[8,256,256]{2,1,0:T(8,128)(2,1)S(1)}, u32[]{:S(2)}, u32[]{:S(2)}) async-start(bf16[8,256,256]{2,1,0:T(8,128)(2,1)} %broadcast_in_dim.4), calls=%async_computation | async-start | bytes 2097152 | tf_op jit(solution)/shard_map/all_to_all | solution.py:30
  43.5 0.7 collective-permute-start.1
  44.2 17.6 %all-to-all-done = bf16[8,256,256]{2,1,0:T(8,128)(2,1)S(1)} async-done(((bf16[8,256,256]{2,1,0:T(8,128)(2,1)}), bf16[8,256,256]{2,1,0:T(8,128)(2,1)S(1)}, u32[]{:S(2)}, u32[]{:S(2)}) %all-to-all-start) | async-done | bytes 1048608 | tf_op jit(solution)/shard_map/all_to_all | solution.py:30
  61.8 1.3 broadcast_in_dim.5
  63.1 4.9 %all-to-all-start.1 = ((bf16[8,256,384]{2,1,0:T(8,128)(2,1)}), bf16[8,256,384]{2,1,0:T(8,128)(2,1)S(1)}, u32[]{:S(2)}, u32[]{:S(2)}) async-start(bf16[8,256,384]{2,1,0:T(8,128)(2,1)} %broadcast_in_dim.5), calls=%async_computation.1 | async-start | bytes 3145728 | tf_op jit(solution)/shard_map/all_to_all | solution.py:30
  68.0 1.9 collective-permute-start.2
  69.9 0.8 copy.47
  70.8 0.6 broadcast_multiply_fusion
  71.4 2.0 copy.44
  73.4 2.7 %reshape.139 = bf16[512,1024]{1,0:T(8,128)(2,1)} reshape(bf16[2,256,2,2,256]{4,3,2,1,0:T(2,128)(2,1)} %copy.44) | data formatting | bytes 2097152 | tf_op jit(solution)/shard_map/reshape | solution.py:36
  76.1 2.3 copy.46
  78.4 1.5 reshape.142
  79.9 32.3 %all-to-all-done.1 = bf16[8,256,384]{2,1,0:T(8,128)(2,1)S(1)} async-done(((bf16[8,256,384]{2,1,0:T(8,128)(2,1)}), bf16[8,256,384]{2,1,0:T(8,128)(2,1)S(1)}, u32[]{:S(2)}, u32[]{:S(2)}) %all-to-all-start.1) | async-done | bytes 1572896 | tf_op jit(solution)/shard_map/all_to_all | solution.py:30
  112.2 30.4 %all-gather.7.cloned.1.call-done = bf16[5120,256]{1,0:T(8,128)(2,1)} async-done(((bf16[320,256]{1,0:T(8,128)(2,1)}), bf16[5120,256]{1,0:T(8,128)(2,1)}) %all-gather.7.cloned.1.call-update) | async-done | bytes 2621456 | tf_op jit(solution)/shard_map/all_gather | solution.py:90
  142.6 1.9 collective-permute-start.4
  144.5 1.6 copy.48
  146.1 1.9 reshape.144
  148.1 1.4 broadcast_select_fusion.4
  149.5 0.2 copy-done.1
  149.6 0.5 fusion.16
  150.1 0.6 copy-done.3
  150.7 0.5 convolution_add_fusion
  151.3 3.4 %collective-permute-start.3 = (bf16[256,256]{0,1:T(8,128)(2,1)S(1)}, bf16[256,256]{0,1:T(8,128)(2,1)S(1)}, u32[]{:S(2)}, u32[]{:S(2)}) collective-permute-start(bf16[256,256]{0,1:T(8,128)(2,1)S(1)} %select_convert_fusion.1), channel_id=1, source_target_pairs={{0,64},{64,0},{1,65},{65,1},{2,66},{66,2},{3,67},{67,3},{4,68},{68... | collective-permute-start | bytes 393224 | tf_op jit(solution)/shard_map/ppermute | solution.py:19
  154.7 1.0 broadcast_select_fusion
  155.7 1.4 fusion.17
  157.1 5.8 %collective-permute-done.3 = bf16[256,256]{0,1:T(8,128)(2,1)S(1)} collective-permute-done((bf16[256,256]{0,1:T(8,128)(2,1)S(1)}, bf16[256,256]{0,1:T(8,128)(2,1)S(1)}, u32[]{:S(2)}, u32[]{:S(2)}) %collective-permute-start.3) | collective-permute-done | bytes 131104 | tf_op jit(solution)/shard_map/ppermute | solution.py:19
  163.0 3.0 %copy.49 = bf16[2,256,2,2,384]{4,3,2,1,0:T(2,128)(2,1)S(1)} copy(bf16[2,256,2,2,384]{4,1,3,0,2:T(8,128)(2,1)} %bitcast.22) | data formatting | bytes 3145728 | tf_op jit(solution)/shard_map/transpose | solution.py:36
  166.0 1.0 reshape.146
  167.1 1.9 convolution_add_fusion.1
  169.0 2.1 collective-permute-start.5
  171.1 8.6 %collective-permute-done.5 = bf16[256,256]{0,1:T(8,128)(2,1)S(1)} collective-permute-done((bf16[256,256]{0,1:T(8,128)(2,1)S(1)}, bf16[256,256]{0,1:T(8,128)(2,1)S(1)}, u32[]{:S(2)}, u32[]{:S(2)}) %collective-permute-start.5) | collective-permute-done | bytes 131104 | tf_op jit(solution)/shard_map/ppermute | solution.py:19
  180.0 0.6 stack_broadcast_in_dim.3
  180.7 17.6 %all-gather.4 = f32[16,7,256]{2,1,0:T(8,128)S(1)} all-gather(f32[1,7,256]{2,1,0:T(8,128)S(1)} %bitcast.122), channel_id=4, replica_groups=mesh['group'=2,'zhigh'=2,'pair'=2,'y'=8,'xhigh'=2,'xlow'=2,'core'=2] {'g..., dimensions={0}, use_global_device_ids=true | all-gather | bytes 121856 | tf_op jit(solution)/shard_map/all_gather | solution.py:69
  198.7 5.0 %collective-permute-start.6 = (bf16[256,256]{0,1:T(8,128)(2,1)S(1)}, bf16[256,256]{0,1:T(8,128)(2,1)S(1)}, u32[]{:S(2)}, u32[]{:S(2)}) collective-permute-start(bf16[256,256]{0,1:T(8,128)(2,1)S(1)} %get-tuple-element.38), channel_id=1, source_target_pairs={{0,64},{64,0},{1,65},{65,1},{2,66},{66,2},{3,67},{67,3},{4,68},{68... | collective-permute-start | bytes 393224 | tf_op jit(solution)/shard_map/ppermute | solution.py:19
  203.7 6.8 %collective-permute-done.6 = bf16[256,256]{0,1:T(8,128)(2,1)S(1)} collective-permute-done((bf16[256,256]{0,1:T(8,128)(2,1)S(1)}, bf16[256,256]{0,1:T(8,128)(2,1)S(1)}, u32[]{:S(2)}, u32[]{:S(2)}) %collective-permute-start.6) | collective-permute-done | bytes 131104 | tf_op jit(solution)/shard_map/ppermute | solution.py:19
  210.5 0.5 convolution_convert_fusion
  211.0 0.5 broadcast_select_fusion.3
  211.5 1.1 pad_maximum_fusion
  212.6 5.5 %all-to-all-start.2 = ((bf16[16,128,256]{2,1,0:T(8,128)(2,1)}), bf16[16,128,256]{2,1,0:T(8,128)(2,1)S(1)}, u32[]{:S(2)}, u32[]{:S(2)}) async-start(bf16[16,128,256]{2,1,0:T(8,128)(2,1)} %bitcast.38), calls=%async_computation.2 | async-start | bytes 2097152 | tf_op jit(solution)/shard_map/all_to_all | solution.py:156
  218.1 0.8 copy.58
  219.0 29.1 %all-to-all-done.2 = bf16[16,128,256]{2,1,0:T(8,128)(2,1)S(1)} async-done(((bf16[16,128,256]{2,1,0:T(8,128)(2,1)}), bf16[16,128,256]{2,1,0:T(8,128)(2,1)S(1)}, u32[]{:S(2)}, u32[]{:S(2)}) %all-to-all-start.2) | async-done | bytes 1048608 | tf_op jit(solution)/shard_map/all_to_all | solution.py:156
  248.0 0.8 convert_reduce_fusion
  (48 shorter events, 1.1 us)
Async XLA Ops:
  7.2 135.4 %all-gather.7.cloned.1.call-start = ((), (), s32[]{:S(2)}) async-start(), calls=%async_computation.3 | async-start | bytes 2785280 | tf_op jit(solution)/shard_map/all_gather | solution.py:90
  7.2 31.4 %collective-permute-start = (bf16[256,256]{1,0:T(8,128)(2,1)}, bf16[256,256]{1,0:T(8,128)(2,1)S(1)}, u32[]{:S(2)}, u32[]{:S(2)}) collective-permute-start(bf16[256,256]{1,0:T(8,128)(2,1)} %param.11), channel_id=1, source_target_pairs={{0,0},{4,64},{64,4},{68,68},{1,1},{5,65},{65,5},{69,69},{2,2},{6,6... | collective-permute-start | bytes 393224 | tf_op jit(solution)/shard_map/ppermute | solution.py:23
  38.6 4.8 %copy-start.5 = (f32[256,384]{1,0:T(8,128)S(1)}, f32[256,384]{1,0:T(8,128)}, u32[]{:S(2)}) copy-start(f32[256,384]{1,0:T(8,128)} %param.7) | copy-start | bytes 1179652
  38.6 4.8 %copy-start.10 = (f32[384]{0:T(512)S(1)}, f32[384]{0:T(512)}, u32[]{:S(2)}) copy-start(f32[384]{0:T(512)} %param.8) | copy-start | bytes 4612
  39.7 22.2 %all-to-all-start = ((bf16[8,256,256]{2,1,0:T(8,128)(2,1)}), bf16[8,256,256]{2,1,0:T(8,128)(2,1)S(1)}, u32[]{:S(2)}, u32[]{:S(2)}) async-start(bf16[8,256,256]{2,1,0:T(8,128)(2,1)} %broadcast_in_dim.4), calls=%async_computation | async-start | bytes 2097152 | tf_op jit(solution)/shard_map/all_to_all | solution.py:30
  43.5 0.7 collective-permute-start.1
  63.1 6.8 %copy-start.8 = (f32[256,256]{1,0:T(8,128)S(1)}, f32[256,256]{1,0:T(8,128)}, u32[]{:S(2)}) copy-start(f32[256,256]{1,0:T(8,128)} %param.10) | copy-start | bytes 786436
  63.1 7.6 %copy-start.9 = (f32[256]{0:T(256)S(1)}, f32[256]{0:T(256)}, u32[]{:S(2)}) copy-start(f32[256]{0:T(256)} %param.13) | copy-start | bytes 3076
  63.1 49.1 %all-to-all-start.1 = ((bf16[8,256,384]{2,1,0:T(8,128)(2,1)}), bf16[8,256,384]{2,1,0:T(8,128)(2,1)S(1)}, u32[]{:S(2)}, u32[]{:S(2)}) async-start(bf16[8,256,384]{2,1,0:T(8,128)(2,1)} %broadcast_in_dim.5), calls=%async_computation.1 | async-start | bytes 3145728 | tf_op jit(solution)/shard_map/all_to_all | solution.py:30
  68.0 8.1 %collective-permute-start.2 = (bf16[8,256,256]{2,1,0:T(8,128)(2,1)S(1)}, bf16[8,256,256]{2,1,0:T(8,128)(2,1)}, u32[]{:S(2)}, u32[]{:S(2)}) collective-permute-start(bf16[8,256,256]{2,1,0:T(8,128)(2,1)S(1)} %all-to-all-done), channel_id=1, source_target_pairs={{0,1},{1,0},{2,3},{3,2},{4,5},{5,4},{6,7},{7,6},{8,9},{9,8},{10,11... | collective-permute-start | bytes 3145736 | tf_op jit(solution)/shard_map/ppermute | solution.py:19
  142.6 20.4 %collective-permute-start.4 = (bf16[8,256,384]{2,1,0:T(8,128)(2,1)S(1)}, bf16[8,256,384]{2,1,0:T(8,128)(2,1)}, u32[]{:S(2)}, u32[]{:S(2)}) collective-permute-start(bf16[8,256,384]{2,1,0:T(8,128)(2,1)S(1)} %all-to-all-done.1), channel_id=1, source_target_pairs={{0,1},{1,0},{2,3},{3,2},{4,5},{5,4},{6,7},{7,6},{8,9},{9,8},{10,11... | collective-permute-start | bytes 4718600 | tf_op jit(solution)/shard_map/ppermute | solution.py:19
  148.1 1.5 copy-start.1
  149.4 1.3 copy-start.3
  150.1 4.6 %copy-start.6 = (bf16[5120,256]{1,0:T(8,128)(2,1)S(1)}, bf16[5120,256]{1,0:T(8,128)(2,1)}, u32[]{:S(2)}) copy-start(bf16[5120,256]{1,0:T(8,128)(2,1)} %all-gather.7.cloned.1.call-done) | copy-start | bytes 7864324
  151.2 4.4 %copy-start = (bf16[512,1536]{1,0:T(8,128)(2,1)S(1)}, bf16[512,1536]{1,0:T(8,128)(2,1)}, u32[]{:S(2)}) copy-start(bf16[512,1536]{1,0:T(8,128)(2,1)} %reshape.144) | copy-start | bytes 4718596
  151.3 11.6 %collective-permute-start.3 = (bf16[256,256]{0,1:T(8,128)(2,1)S(1)}, bf16[256,256]{0,1:T(8,128)(2,1)S(1)}, u32[]{:S(2)}, u32[]{:S(2)}) collective-permute-start(bf16[256,256]{0,1:T(8,128)(2,1)S(1)} %select_convert_fusion.1), channel_id=1, source_target_pairs={{0,64},{64,0},{1,65},{65,1},{2,66},{66,2},{3,67},{67,3},{4,68},{68... | collective-permute-start | bytes 393224 | tf_op jit(solution)/shard_map/ppermute | solution.py:19
  155.7 7.2 %copy-start.7 = (f32[256,256]{0,1:T(8,128)S(1)}, f32[256,256]{0,1:T(8,128)}, u32[]{:S(2)}) copy-start(f32[256,256]{0,1:T(8,128)} %copy.47) | copy-start | bytes 786436
  169.0 10.7 %collective-permute-start.5 = (bf16[256,256]{0,1:T(8,128)(2,1)S(1)}, bf16[256,256]{0,1:T(8,128)(2,1)S(1)}, u32[]{:S(2)}, u32[]{:S(2)}) collective-permute-start(bf16[256,256]{0,1:T(8,128)(2,1)S(1)} %select_convert_fusion), channel_id=1, source_target_pairs={{0,64},{64,0},{1,65},{65,1},{2,66},{66,2},{3,67},{67,3},{4,68},{68... | collective-permute-start | bytes 393224 | tf_op jit(solution)/shard_map/ppermute | solution.py:19
  171.1 39.4 %copy-start.4 = (bf16[512,1024]{1,0:T(8,128)(2,1)S(1)}, bf16[512,1024]{1,0:T(8,128)(2,1)}, u32[]{:S(2)}) copy-start(bf16[512,1024]{1,0:T(8,128)(2,1)} %reshape.142) | copy-start | bytes 3145732
  198.5 12.5 %copy-start.2 = (bf16[512,1024]{1,0:T(8,128)(2,1)S(1)}, bf16[512,1024]{1,0:T(8,128)(2,1)}, u32[]{:S(2)}) copy-start(bf16[512,1024]{1,0:T(8,128)(2,1)} %reshape.139) | copy-start | bytes 3145732
  198.7 11.8 %collective-permute-start.6 = (bf16[256,256]{0,1:T(8,128)(2,1)S(1)}, bf16[256,256]{0,1:T(8,128)(2,1)S(1)}, u32[]{:S(2)}, u32[]{:S(2)}) collective-permute-start(bf16[256,256]{0,1:T(8,128)(2,1)S(1)} %get-tuple-element.38), channel_id=1, source_target_pairs={{0,64},{64,0},{1,65},{65,1},{2,66},{66,2},{3,67},{67,3},{4,68},{68... | collective-permute-start | bytes 393224 | tf_op jit(solution)/shard_map/ppermute | solution.py:19
  212.6 35.4 %all-to-all-start.2 = ((bf16[16,128,256]{2,1,0:T(8,128)(2,1)}), bf16[16,128,256]{2,1,0:T(8,128)(2,1)S(1)}, u32[]{:S(2)}, u32[]{:S(2)}) async-start(bf16[16,128,256]{2,1,0:T(8,128)(2,1)} %bitcast.38), calls=%async_computation.2 | async-start | bytes 2097152 | tf_op jit(solution)/shard_map/all_to_all | solution.py:156
Sparse Core Ops, SparseCore 0:
  11.2 131.3 all-gather.6

commit v4 on v3

--- a/solution.py
+++ b/solution.py
@@ -12,7 +12,7 @@
 TOKEN_AXES = ("zhigh", "pair", "y")
 GATHER_AXES = ("zhigh", "y")
 FEATURE_AXES = ("group", "xhigh", "xlow", "core")
-CHIP_AXES = ("group", "xhigh", "xlow")
+CHIP_AXES = ("xhigh", "group", "xlow")
 
 
 def swap(values, axis):
@@ -24,18 +24,13 @@
 
 
 def gather_features(values, after=None):
-    tokens, width = values.shape
     count = lax.axis_size(CHIP_AXES)
-    copies = jnp.broadcast_to(values[None], (count, tokens, width))
+    copies = jnp.broadcast_to(values[None], (count, *values.shape))
     line = lax.all_to_all(copies, CHIP_AXES, 0, 0, tiled=True)
     if after is not None:
         line, after = lax.optimization_barrier((line, after))
     other = swap(line, "core")
-    shape = (lax.axis_size("group"), 2, lax.axis_size("xlow"), tokens, width)
-    gathered = tuple(
-        part.reshape(shape).transpose(1, 3, 0, 2, 4).reshape(2 * tokens, -1)
-        for part in (line, other)
-    )
+    gathered = tuple(part.reshape(2, count // 2, *values.shape) for part in (line, other))
     return gathered, after
 
 
@@ -46,9 +41,11 @@
     )
 
 
-def product(pair, weight_pair):
-    return jnp.dot(pair[0], weight_pair[0], preferred_element_type=F32) + jnp.dot(
-        pair[1], weight_pair[1], preferred_element_type=F32
+def product(parts, weight_parts, block):
+    dims = (((0, 2), (0, 1)), ((), ()))
+    return sum(
+        lax.dot_general(part[block], weight, dims, preferred_element_type=F32)
+        for part, weight in zip(parts, weight_parts)
     )
 
 
@@ -87,29 +84,34 @@
     width = student_stream.shape[1]
     depth = out_weight.shape[0]
 
-    weights = lax.all_gather(
-        jnp.concatenate([out_weight, projection], axis=0), GATHER_AXES, axis=0
-    )
+    weights = jnp.concatenate([out_weight, projection], axis=0)
+    zhigh = lax.axis_index("zhigh")
+    weights = jnp.stack(both((weights, swap(weights, "zhigh")), zhigh), axis=0)
     context = turned(student_context)
     teacher_mean, _, teacher_square = moments(teacher_stream)
     table = gather_rows([teacher_mean, teacher_square])
-    context, table = lax.optimization_barrier((context, table))
+    context, weights, table = lax.optimization_barrier((context, weights, table))
+    weights = lax.all_gather(weights, "y", axis=0)
     mean, _, inv_std = combine(table[:, 0], table[:, 1], teacher_stream.shape[1])
     hidden = ((teacher_stream - mean[:, None]) * inv_std[:, None] * teacher_gain).astype(BF16)
     context, _ = gather_features(context)
     hidden, weights = gather_features(turned(hidden), weights)
 
-    weights = weights.reshape(groups, lanes, cores, 2, *weights.shape[1:])
-    weights = weights.transpose(2, 0, 1, 3, 4, 5)
-    out_full = both(weights[..., :depth, :].reshape(cores, -1, width), core)
-    projection_full = both(weights[..., depth:, :].reshape(cores, -1, width), core)
+    weights = weights.reshape(lanes, cores, 2, groups, *weights.shape[2:])
+    weights = weights.transpose(1, 3, 0, 2, 4, 5)
 
-    def shared(partial):
-        mine, other = both(partial.reshape(2, tokens, width), pair)
+    def weight_parts(part):
+        return both(part.reshape(cores, groups * lanes, -1, width), core)
+
+    out_full = weight_parts(weights[..., :depth, :])
+    projection_full = weight_parts(weights[..., depth:, :])
+
+    def shared(parts, weight):
+        mine, other = both([product(parts, weight, block) for block in range(2)], pair)
         return mine + swap(other.astype(BF16), "pair").astype(F32)
 
-    pre_norm = student_stream + shared(product(context, out_full))
-    target = shared(product(hidden, projection_full))
+    pre_norm = student_stream + shared(context, out_full)
+    target = shared(hidden, projection_full)
 
     block_mean, centered, square = moments(pre_norm)
     gain_square = student_gain * student_gain
@@ -143,13 +145,14 @@
     grad_pre = (
         inv_std[:, None] * (grad_norm - first_mean[:, None] - normalized * second_mean[:, None])
     ).astype(BF16)
-    grad_pre = jnp.concatenate(both((grad_pre, swap(grad_pre, "pair")), pair), axis=0)
-
+    grads = both((grad_pre, swap(grad_pre, "pair")), pair)
+    dims = (((1,), (0,)), ((), ()))
     partial = [
-        lax.dot_general(
-            half, grad_pre, (((0,), (0,)), ((), ())), preferred_element_type=F32
+        sum(
+            lax.dot_general(part[block], grads[block], dims, preferred_element_type=F32)
+            for block in range(2)
         ).astype(BF16)
-        for half in context
+        for part in context
     ]
     partial = jnp.stack(both(partial, core), axis=0)
     partial = partial.reshape(cores, groups, lanes, 2 * depth, width).transpose(1, 2, 0, 3, 4)

time: 256 us -> 212 us (0.83)
  the two profiles are of different devices: /device:TPU:8 before, /device:TPU:2 now
where the time goes in v4:
time: 212 us; the launch traced here: 211 us
  waiting for transfers between devices  88.1 us (42%)
  starting transfers between devices  47.3 us (22%)
  blocking collectives  38.6 us (18%)
  between operations  14.4 us (7%)
  matrix products  8.85 us (4%)
  other arithmetic  7.82 us (4%)
  local copies, waits for them, and re-layouts  5.93 us (3%)
    all_gather x2, blocking collectives, gather_rows(): return lax.all_gather(jnp.stack(rows, axis=0), FEATURE_AXES, axis=0)  38.6 us
    all_to_all x2, waiting for transfers between devices, gather_features(): line = lax.all_to_all(copies, CHIP_AXES, 0, 0, tiled=True)  33.7 us
    all_to_all x1, waiting for transfers between devices, shards(): lax.all_to_all(partial.reshape(-1, depth, width), GATHER_AXES, 0, 0, tile...  30.7 us
    ppermute x6, waiting for transfers between devices, swap(): return lax.ppermute(values, axis, [(0, 1), (1, 0)])  23 us
    ppermute x6, starting transfers between devices, swap(): return lax.ppermute(values, axis, [(0, 1), (1, 0)])  22 us
    all_to_all x2, starting transfers between devices, gather_features(): line = lax.all_to_all(copies, CHIP_AXES, 0, 0, tiled=True)  15.8 us
    all_to_all x1, starting transfers between devices, shards(): lax.all_to_all(partial.reshape(-1, depth, width), GATHER_AXES, 0, 0, tile...  7.21 us
    dot_general x8, matrix products, product(): lax.dot_general(part[block], weight, dims, preferred_element_type=F32)  5.38 us
  transfers between devices with their start and end apart: 12, of which 6 were waited for; matrix products, arithmetic and copies ran while one was open for 6% of the time, Pallas kernels for 0%

profile of v4, /device:TPU:2, one launch (start us, length us, event | category | flops | bytes accessed | tf_op | source)
XLA Modules:
  0.0 211.0 jit_solution(2058139939067473761)
XLA Ops:
  7.2 0.8 constant_dynamic-update-slice_fusion.1
  8.0 0.9 constant_dynamic-update-slice_fusion
  8.9 10.9 %collective-permute-start.1 = (bf16[320,256]{1,0:T(8,128)(2,1)S(1)}, bf16[320,256]{1,0:T(8,128)(2,1)S(1)}, u32[]{:S(2)}, u32[]{:S(2)}) collective-permute-start(bf16[320,256]{1,0:T(8,128)(2,1)S(1)} %constant_dynamic-update-slice_fusion), channel_id=1, source_target_pairs={{0,128},{128,0},{1,129},{129,1},{2,130},{130,2},{3,131},{131,3},{4... | collective-permute-start | bytes 491528 | tf_op jit(solution)/shard_map/ppermute | solution.py:19
  19.8 1.6 collective-permute-start
  21.4 1.1 reduce_sum.162
  22.5 1.2 multiply_reduce_fusion
  23.7 19.7 %all-gather.3 = f32[16,2,256]{2,1,0:T(2,128)S(1)} all-gather(f32[1,2,256]{2,1,0:T(2,128)S(1)} %maximum_bitcast_fusion), channel_id=2, replica_groups=mesh['group'=2,'zhigh'=2,'pair'=2,'y'=8,'xhigh'=2,'xlow'=2,'core'=2] {'g..., dimensions={0}, use_global_device_ids=true | all-gather | bytes 34816 | tf_op jit(solution)/shard_map/all_gather | solution.py:66
  43.4 0.8 pad_maximum_fusion.1
  44.2 1.1 broadcast_in_dim.4
  45.2 7.7 %all-to-all-start = ((bf16[8,256,256]{2,1,0:T(8,128)(2,1)}), bf16[8,256,256]{2,1,0:T(8,128)(2,1)S(1)}, u32[]{:S(2)}, u32[]{:S(2)}) async-start(bf16[8,256,256]{2,1,0:T(8,128)(2,1)} %broadcast_in_dim.4), calls=%async_computation | async-start | bytes 2097152 | tf_op jit(solution)/shard_map/all_to_all | solution.py:29
  52.9 0.7 all-gather.7.cloned.1.call-update
  53.8 0.1 multiply_convert_fusion
  53.9 0.7 collective-permute-start.2
  54.6 16.7 %all-to-all-done = bf16[8,256,256]{2,1,0:T(8,128)(2,1)S(1)} async-done(((bf16[8,256,256]{2,1,0:T(8,128)(2,1)}), bf16[8,256,256]{2,1,0:T(8,128)(2,1)S(1)}, u32[]{:S(2)}, u32[]{:S(2)}) %all-to-all-start) | async-done | bytes 1048608 | tf_op jit(solution)/shard_map/all_to_all | solution.py:29
  71.3 1.3 broadcast_in_dim.5
  72.6 8.1 %all-to-all-start.1 = ((bf16[8,256,384]{2,1,0:T(8,128)(2,1)}), bf16[8,256,384]{2,1,0:T(8,128)(2,1)S(1)}, u32[]{:S(2)}, u32[]{:S(2)}) async-start(bf16[8,256,384]{2,1,0:T(8,128)(2,1)} %broadcast_in_dim.5), calls=%async_computation.1 | async-start | bytes 3145728 | tf_op jit(solution)/shard_map/all_to_all | solution.py:29
  80.7 1.9 collective-permute-start.3
  82.8 0.6 broadcast_multiply_fusion
  83.4 17.0 %all-to-all-done.1 = bf16[8,256,384]{2,1,0:T(8,128)(2,1)S(1)} async-done(((bf16[8,256,384]{2,1,0:T(8,128)(2,1)}), bf16[8,256,384]{2,1,0:T(8,128)(2,1)S(1)}, u32[]{:S(2)}, u32[]{:S(2)}) %all-to-all-start.1) | async-done | bytes 1572896 | tf_op jit(solution)/shard_map/all_to_all | solution.py:29
  100.4 1.3 broadcast_select_fusion.4
  101.7 1.9 collective-permute-start.5
  103.6 0.3 convolution_bitcast_fusion.7
  104.0 0.3 convolution_bitcast_fusion.5
  104.4 1.5 fusion.4
  106.0 1.4 select_convert_fusion.1
  107.4 3.3 %collective-permute-start.4 = (bf16[256,256]{0,1:T(8,128)(2,1)S(1)}, bf16[256,256]{0,1:T(8,128)(2,1)S(1)}, u32[]{:S(2)}, u32[]{:S(2)}) collective-permute-start(bf16[256,256]{0,1:T(8,128)(2,1)S(1)} %get-tuple-element.61), channel_id=1, source_target_pairs={{0,64},{64,0},{1,65},{65,1},{2,66},{66,2},{3,67},{67,3},{4,68},{68... | collective-permute-start | bytes 393224 | tf_op jit(solution)/shard_map/ppermute | solution.py:19
  110.9 0.4 convolution_bitcast_fusion.3
  111.3 0.4 convolution_bitcast_fusion.1
  111.8 7.0 %collective-permute-done.4 = bf16[256,256]{0,1:T(8,128)(2,1)S(1)} collective-permute-done((bf16[256,256]{0,1:T(8,128)(2,1)S(1)}, bf16[256,256]{0,1:T(8,128)(2,1)S(1)}, u32[]{:S(2)}, u32[]{:S(2)}) %collective-permute-start.4) | collective-permute-done | bytes 131104 | tf_op jit(solution)/shard_map/ppermute | solution.py:19
  118.9 0.4 fusion.2
  119.4 0.5 select_convert_fusion
  119.8 1.9 collective-permute-start.6
  121.8 7.7 %collective-permute-done.6 = bf16[256,256]{0,1:T(8,128)(2,1)S(1)} collective-permute-done((bf16[256,256]{0,1:T(8,128)(2,1)S(1)}, bf16[256,256]{0,1:T(8,128)(2,1)S(1)}, u32[]{:S(2)}, u32[]{:S(2)}) %collective-permute-start.6) | collective-permute-done | bytes 131104 | tf_op jit(solution)/shard_map/ppermute | solution.py:19
  129.6 0.1 fusion.6
  129.8 0.6 stack_broadcast_in_dim.3
  130.5 18.9 %all-gather.4 = f32[16,7,256]{2,1,0:T(8,128)S(1)} all-gather(f32[1,7,256]{2,1,0:T(8,128)S(1)} %bitcast.164), channel_id=4, replica_groups=mesh['group'=2,'zhigh'=2,'pair'=2,'y'=8,'xhigh'=2,'xlow'=2,'core'=2] {'g..., dimensions={0}, use_global_device_ids=true | all-gather | bytes 121856 | tf_op jit(solution)/shard_map/all_gather | solution.py:66
  149.5 0.2 multiply_convert_fusion.1
  149.7 2.1 collective-permute-start.7
  151.8 8.2 %collective-permute-done.7 = bf16[256,256]{0,1:T(8,128)(2,1)S(1)} collective-permute-done((bf16[256,256]{0,1:T(8,128)(2,1)S(1)}, bf16[256,256]{0,1:T(8,128)(2,1)S(1)}, u32[]{:S(2)}, u32[]{:S(2)}) %collective-permute-start.7) | collective-permute-done | bytes 131104 | tf_op jit(solution)/shard_map/ppermute | solution.py:19
  160.0 0.3 fusion.10
  160.4 1.4 fusion.8
  161.8 1.4 fusion.1
  163.1 0.3 broadcast_select_fusion.3
  163.5 1.1 pad_maximum_fusion
  164.6 7.2 %all-to-all-start.2 = ((bf16[16,128,256]{2,1,0:T(8,128)(2,1)}), bf16[16,128,256]{2,1,0:T(8,128)(2,1)S(1)}, u32[]{:S(2)}, u32[]{:S(2)}) async-start(bf16[16,128,256]{2,1,0:T(8,128)(2,1)} %bitcast.44), calls=%async_computation.2 | async-start | bytes 2097152 | tf_op jit(solution)/shard_map/all_to_all | solution.py:159
  171.8 0.8 copy.140
  172.6 30.7 %all-to-all-done.2 = bf16[16,128,256]{2,1,0:T(8,128)(2,1)S(1)} async-done(((bf16[16,128,256]{2,1,0:T(8,128)(2,1)}), bf16[16,128,256]{2,1,0:T(8,128)(2,1)S(1)}, u32[]{:S(2)}, u32[]{:S(2)}) %all-to-all-start.2) | async-done | bytes 1048608 | tf_op jit(solution)/shard_map/all_to_all | solution.py:159
  203.3 0.8 convert_reduce_fusion
  (40 shorter events, 1.0 us)
Async XLA Ops:
  8.9 34.5 %collective-permute-start.1 = (bf16[320,256]{1,0:T(8,128)(2,1)S(1)}, bf16[320,256]{1,0:T(8,128)(2,1)S(1)}, u32[]{:S(2)}, u32[]{:S(2)}) collective-permute-start(bf16[320,256]{1,0:T(8,128)(2,1)S(1)} %constant_dynamic-update-slice_fusion), channel_id=1, source_target_pairs={{0,128},{128,0},{1,129},{129,1},{2,130},{130,2},{3,131},{131,3},{4... | collective-permute-start | bytes 491528 | tf_op jit(solution)/shard_map/ppermute | solution.py:19
  19.8 24.4 %collective-permute-start = (bf16[256,256]{1,0:T(8,128)(2,1)}, bf16[256,256]{1,0:T(8,128)(2,1)S(1)}, u32[]{:S(2)}, u32[]{:S(2)}) collective-permute-start(bf16[256,256]{1,0:T(8,128)(2,1)} %param.11), channel_id=1, source_target_pairs={{0,0},{4,64},{64,4},{68,68},{1,1},{5,65},{65,5},{69,69},{2,2},{6,6... | collective-permute-start | bytes 393224 | tf_op jit(solution)/shard_map/ppermute | solution.py:23
  45.2 8.5 %copy-start = (f32[256,384]{1,0:T(8,128)S(1)}, f32[256,384]{1,0:T(8,128)}, u32[]{:S(2)}) copy-start(f32[256,384]{1,0:T(8,128)} %param.7) | copy-start | bytes 1179652
  45.2 8.5 %copy-start.4 = (f32[384]{0:T(512)S(1)}, f32[384]{0:T(512)}, u32[]{:S(2)}) copy-start(f32[384]{0:T(512)} %param.8) | copy-start | bytes 4612
  45.2 26.1 %all-to-all-start = ((bf16[8,256,256]{2,1,0:T(8,128)(2,1)}), bf16[8,256,256]{2,1,0:T(8,128)(2,1)S(1)}, u32[]{:S(2)}, u32[]{:S(2)}) async-start(bf16[8,256,256]{2,1,0:T(8,128)(2,1)} %broadcast_in_dim.4), calls=%async_computation | async-start | bytes 2097152 | tf_op jit(solution)/shard_map/all_to_all | solution.py:29
  52.9 47.4 %all-gather.7.cloned.1.call-start = ((), (), s32[]{:S(2)}) async-start(), calls=%async_computation.3 | async-start | bytes 2949120 | tf_op jit(solution)/shard_map/all_gather | solution.py:94
  53.9 0.7 collective-permute-start.2
  72.6 10.1 %copy-start.2 = (f32[256,256]{1,0:T(8,128)S(1)}, f32[256,256]{1,0:T(8,128)}, u32[]{:S(2)}) copy-start(f32[256,256]{1,0:T(8,128)} %param.10) | copy-start | bytes 786436
  72.6 10.2 %copy-start.3 = (f32[256]{0:T(256)S(1)}, f32[256]{0:T(256)}, u32[]{:S(2)}) copy-start(f32[256]{0:T(256)} %param.13) | copy-start | bytes 3076
  72.6 27.8 %all-to-all-start.1 = ((bf16[8,256,384]{2,1,0:T(8,128)(2,1)}), bf16[8,256,384]{2,1,0:T(8,128)(2,1)S(1)}, u32[]{:S(2)}, u32[]{:S(2)}) async-start(bf16[8,256,384]{2,1,0:T(8,128)(2,1)} %broadcast_in_dim.5), calls=%async_computation.1 | async-start | bytes 3145728 | tf_op jit(solution)/shard_map/all_to_all | solution.py:29
  80.7 23.7 %collective-permute-start.3 = (bf16[8,256,256]{2,1,0:T(8,128)(2,1)S(1)}, bf16[8,256,256]{2,1,0:T(8,128)(2,1)}, u32[]{:S(2)}, u32[]{:S(2)}) collective-permute-start(bf16[8,256,256]{2,1,0:T(8,128)(2,1)S(1)} %all-to-all-done), channel_id=1, source_target_pairs={{0,1},{1,0},{2,3},{3,2},{4,5},{5,4},{6,7},{7,6},{8,9},{9,8},{10,11... | collective-permute-start | bytes 3145736 | tf_op jit(solution)/shard_map/ppermute | solution.py:19
  101.7 17.2 %collective-permute-start.5 = (bf16[8,256,384]{2,1,0:T(8,128)(2,1)S(1)}, bf16[8,256,384]{2,1,0:T(8,128)(2,1)S(1)}, u32[]{:S(2)}, u32[]{:S(2)}) collective-permute-start(bf16[8,256,384]{2,1,0:T(8,128)(2,1)S(1)} %all-to-all-done.1), channel_id=1, source_target_pairs={{0,1},{1,0},{2,3},{3,2},{4,5},{5,4},{6,7},{7,6},{8,9},{9,8},{10,11... | collective-permute-start | bytes 4718600 | tf_op jit(solution)/shard_map/ppermute | solution.py:19
  104.4 6.3 %copy-start.1 = (bf16[16,320,256]{2,1,0:T(8,128)(2,1)S(1)}, bf16[16,320,256]{2,1,0:T(8,128)(2,1)}, u32[]{:S(2)}) copy-start(bf16[16,320,256]{2,1,0:T(8,128)(2,1)} %all-gather.7.cloned.1.call-done) | copy-start | bytes 7864324
  107.4 11.5 %collective-permute-start.4 = (bf16[256,256]{0,1:T(8,128)(2,1)S(1)}, bf16[256,256]{0,1:T(8,128)(2,1)S(1)}, u32[]{:S(2)}, u32[]{:S(2)}) collective-permute-start(bf16[256,256]{0,1:T(8,128)(2,1)S(1)} %get-tuple-element.61), channel_id=1, source_target_pairs={{0,64},{64,0},{1,65},{65,1},{2,66},{66,2},{3,67},{67,3},{4,68},{68... | collective-permute-start | bytes 393224 | tf_op jit(solution)/shard_map/ppermute | solution.py:19
  119.8 9.7 %collective-permute-start.6 = (bf16[256,256]{0,1:T(8,128)(2,1)S(1)}, bf16[256,256]{0,1:T(8,128)(2,1)S(1)}, u32[]{:S(2)}, u32[]{:S(2)}) collective-permute-start(bf16[256,256]{0,1:T(8,128)(2,1)S(1)} %get-tuple-element.59), channel_id=1, source_target_pairs={{0,64},{64,0},{1,65},{65,1},{2,66},{66,2},{3,67},{67,3},{4,68},{68... | collective-permute-start | bytes 393224 | tf_op jit(solution)/shard_map/ppermute | solution.py:19
  149.7 10.3 %collective-permute-start.7 = (bf16[256,256]{0,1:T(8,128)(2,1)S(1)}, bf16[256,256]{0,1:T(8,128)(2,1)S(1)}, u32[]{:S(2)}, u32[]{:S(2)}) collective-permute-start(bf16[256,256]{0,1:T(8,128)(2,1)S(1)} %get-tuple-element.44), channel_id=1, source_target_pairs={{0,64},{64,0},{1,65},{65,1},{2,66},{66,2},{3,67},{67,3},{4,68},{68... | collective-permute-start | bytes 393224 | tf_op jit(solution)/shard_map/ppermute | solution.py:19
  164.6 38.8 %all-to-all-start.2 = ((bf16[16,128,256]{2,1,0:T(8,128)(2,1)}), bf16[16,128,256]{2,1,0:T(8,128)(2,1)S(1)}, u32[]{:S(2)}, u32[]{:S(2)}) async-start(bf16[16,128,256]{2,1,0:T(8,128)(2,1)} %bitcast.44), calls=%async_computation.2 | async-start | bytes 2097152 | tf_op jit(solution)/shard_map/all_to_all | solution.py:159
Sparse Core Ops, SparseCore 0:
  55.8 41.7 all-gather.6

commit v5 on v4

--- a/solution.py
+++ b/solution.py
@@ -23,15 +23,17 @@
     return lax.ppermute(values, ("pair", "xhigh"), [(0, 0), (1, 2), (2, 1), (3, 3)])
 
 
-def gather_features(values, after=None):
+def spread(values):
     count = lax.axis_size(CHIP_AXES)
     copies = jnp.broadcast_to(values[None], (count, *values.shape))
-    line = lax.all_to_all(copies, CHIP_AXES, 0, 0, tiled=True)
-    if after is not None:
-        line, after = lax.optimization_barrier((line, after))
-    other = swap(line, "core")
-    gathered = tuple(part.reshape(2, count // 2, *values.shape) for part in (line, other))
-    return gathered, after
+    return lax.all_to_all(copies, CHIP_AXES, 0, 0, tiled=True)
+
+
+def with_other_core(line):
+    return tuple(
+        part.reshape(2, line.shape[0] // 2, *line.shape[1:])
+        for part in (line, swap(line, "core"))
+    )
 
 
 def both(first, place):
@@ -84,21 +86,27 @@
     width = student_stream.shape[1]
     depth = out_weight.shape[0]
 
+    together = lax.optimization_barrier
     weights = jnp.concatenate([out_weight, projection], axis=0)
-    zhigh = lax.axis_index("zhigh")
-    weights = jnp.stack(both((weights, swap(weights, "zhigh")), zhigh), axis=0)
+    near = lax.all_gather(weights, "y", axis=0)
     context = turned(student_context)
-    teacher_mean, _, teacher_square = moments(teacher_stream)
-    table = gather_rows([teacher_mean, teacher_square])
-    context, weights, table = lax.optimization_barrier((context, weights, table))
-    weights = lax.all_gather(weights, "y", axis=0)
+    mean, _, square = moments(teacher_stream)
+    context, mean, square = together((context, mean, square))
+    context = spread(context)
+    table = gather_rows([mean, square])
+    weights, table = together((weights, table))
+    far = lax.all_gather(swap(weights, "zhigh"), "y", axis=0)
     mean, _, inv_std = combine(table[:, 0], table[:, 1], teacher_stream.shape[1])
     hidden = ((teacher_stream - mean[:, None]) * inv_std[:, None] * teacher_gain).astype(BF16)
-    context, _ = gather_features(context)
-    hidden, weights = gather_features(turned(hidden), weights)
+    hidden, context = together((hidden, context))
+    hidden, near = together((turned(hidden), near))
+    context = with_other_core(context)
+    hidden, far = together((spread(hidden), far))
+    hidden = with_other_core(hidden)
 
-    weights = weights.reshape(lanes, cores, 2, groups, *weights.shape[2:])
-    weights = weights.transpose(1, 3, 0, 2, 4, 5)
+    weights = jnp.stack(both((near, far), lax.axis_index("zhigh")), axis=0)
+    weights = weights.reshape(groups, lanes, cores, 2, *weights.shape[2:])
+    weights = weights.transpose(2, 0, 1, 3, 4, 5)
 
     def weight_parts(part):
         return both(part.reshape(cores, groups * lanes, -1, width), core)
@@ -106,12 +114,14 @@
     out_full = weight_parts(weights[..., :depth, :])
     projection_full = weight_parts(weights[..., depth:, :])
 
-    def shared(parts, weight):
-        mine, other = both([product(parts, weight, block) for block in range(2)], pair)
-        return mine + swap(other.astype(BF16), "pair").astype(F32)
-
-    pre_norm = student_stream + shared(context, out_full)
-    target = shared(hidden, projection_full)
+    branch, other_branch = both([product(context, out_full, block) for block in range(2)], pair)
+    target, other_target = both(
+        [product(hidden, projection_full, block) for block in range(2)], pair
+    )
+    sent = jnp.concatenate([other_branch.astype(BF16), other_target.astype(BF16)], axis=0)
+    received = swap(sent, "pair").astype(F32)
+    pre_norm = student_stream + (branch + received[:tokens])
+    target = target + received[tokens:]
 
     block_mean, centered, square = moments(pre_norm)
     gain_square = student_gain * student_gain

time: 212 us -> 260 us (1.23)
  the two profiles are of different devices: /device:TPU:2 before, /device:TPU:8 now
where the time goes in v5:
time: 260 us; the launch traced here: 259 us
  waiting for transfers between devices  116 us (45%)
  starting transfers between devices  59 us (23%)
  blocking collectives  46.3 us (18%)
  between operations  14.4 us (6%)
  matrix products  8.71 us (3%)
  other arithmetic  7.99 us (3%)
  local copies, waits for them, and re-layouts  7.09 us (3%)
    all_gather x2, blocking collectives, gather_rows(): return lax.all_gather(jnp.stack(rows, axis=0), FEATURE_AXES, axis=0)  46.3 us
    ppermute x5, waiting for transfers between devices, swap(): return lax.ppermute(values, axis, [(0, 1), (1, 0)])  43 us
    all_gather x1, waiting for transfers between devices, shards(): far = lax.all_gather(swap(weights, 'zhigh'), 'y', axis=0)  37 us
    all_to_all x1, waiting for transfers between devices, shards(): lax.all_to_all(partial.reshape(-1, depth, width), GATHER_AXES, 0, 0, tile...  28.9 us
    all_to_all x2, starting transfers between devices, spread(): return lax.all_to_all(copies, CHIP_AXES, 0, 0, tiled=True)  24.7 us
    ppermute x5, starting transfers between devices, swap(): return lax.ppermute(values, axis, [(0, 1), (1, 0)])  23.4 us
    all_to_all x1, starting transfers between devices, shards(): lax.all_to_all(partial.reshape(-1, depth, width), GATHER_AXES, 0, 0, tile...  8.53 us
    all_gather x1, waiting for transfers between devices, shards(): near = lax.all_gather(weights, 'y', axis=0)  6.57 us
  transfers between devices with their start and end apart: 12, of which 6 were waited for; matrix products, arithmetic and copies ran while one was open for 5% of the time, Pallas kernels for 0%

profile of v5, /device:TPU:8, one launch (start us, length us, event | category | flops | bytes accessed | tf_op | source)
XLA Modules:
  0.0 259.1 jit_solution(9798616540660654760)
XLA Ops:
  7.2 1.6 collective-permute-start
  8.8 0.8 constant_dynamic-update-slice_fusion.1
  9.6 0.9 constant_dynamic-update-slice_fusion
  10.5 0.7 copy-done.1
  11.2 1.1 reduce_sum.162
  12.3 1.2 multiply_reduce_fusion
  13.5 1.1 broadcast_in_dim.4
  14.6 11.4 %all-to-all-start = ((bf16[8,256,256]{2,1,0:T(8,128)(2,1)}), bf16[8,256,256]{2,1,0:T(8,128)(2,1)S(1)}, u32[]{:S(2)}, u32[]{:S(2)}) async-start(bf16[8,256,256]{2,1,0:T(8,128)(2,1)} %broadcast_in_dim.4), calls=%async_computation | async-start | bytes 2097152 | tf_op jit(solution)/shard_map/all_to_all | solution.py:29
  26.0 27.2 %all-gather.4 = f32[16,2,256]{2,1,0:T(2,128)S(1)} all-gather(f32[1,2,256]{2,1,0:T(2,128)S(1)} %maximum_bitcast_fusion.1), channel_id=2, replica_groups=mesh['group'=2,'zhigh'=2,'pair'=2,'y'=8,'xhigh'=2,'xlow'=2,'core'=2] {'g..., dimensions={0}, use_global_device_ids=true | all-gather | bytes 34816 | tf_op jit(solution)/shard_map/all_gather | solution.py:68
  53.5 0.7 collective-permute-start.1
  54.2 6.6 %all-gather.9.cloned.1.call-done = bf16[2560,256]{1,0:T(8,128)(2,1)} async-done(((bf16[320,256]{1,0:T(8,128)(2,1)}), bf16[2560,256]{1,0:T(8,128)(2,1)}) %all-gather.9.cloned.1.call-update) | async-done | bytes 1310736 | tf_op jit(solution)/shard_map/all_gather | solution.py:91
  60.8 1.3 broadcast_in_dim.5
  62.1 13.3 %all-to-all-start.1 = ((bf16[8,256,384]{2,1,0:T(8,128)(2,1)}), bf16[8,256,384]{2,1,0:T(8,128)(2,1)S(1)}, u32[]{:S(2)}, u32[]{:S(2)}) async-start(bf16[8,256,384]{2,1,0:T(8,128)(2,1)} %broadcast_in_dim.5), calls=%async_computation.1 | async-start | bytes 3145728 | tf_op jit(solution)/shard_map/all_to_all | solution.py:29
  75.4 9.7 %collective-permute-start.2 = (bf16[320,256]{1,0:T(8,128)(2,1)S(1)}, bf16[320,256]{1,0:T(8,128)(2,1)S(1)}, u32[]{:S(2)}, u32[]{:S(2)}) collective-permute-start(bf16[320,256]{1,0:T(8,128)(2,1)S(1)} %copy-done.2), channel_id=1, source_target_pairs={{0,128},{128,0},{1,129},{129,1},{2,130},{130,2},{3,131},{131,3},{4... | collective-permute-start | bytes 491528 | tf_op jit(solution)/shard_map/ppermute | solution.py:19
  85.1 24.4 %collective-permute-done.2 = bf16[320,256]{1,0:T(8,128)(2,1)S(1)} collective-permute-done((bf16[320,256]{1,0:T(8,128)(2,1)S(1)}, bf16[320,256]{1,0:T(8,128)(2,1)S(1)}, u32[]{:S(2)}, u32[]{:S(2)}) %collective-permute-start.2) | collective-permute-done | bytes 163872 | tf_op jit(solution)/shard_map/ppermute | solution.py:19
  109.5 0.7 copy-done.4
  110.2 1.9 collective-permute-start.3
  112.1 37.0 %all-gather.11.cloned.1.call-done = bf16[2560,256]{1,0:T(8,128)(2,1)} async-done(((bf16[320,256]{1,0:T(8,128)(2,1)}), bf16[2560,256]{1,0:T(8,128)(2,1)}) %all-gather.11.cloned.1.call-update) | async-done | bytes 1310736 | tf_op jit(solution)/shard_map/all_gather | solution.py:98
  149.1 1.9 collective-permute-start.4
  151.1 1.9 broadcast_select_fusion.1
  152.9 0.2 maximum_bitcast_fusion
  153.3 0.3 convolution_bitcast_fusion.7
  153.6 0.3 convolution_bitcast_fusion.5
  154.1 0.4 convolution_bitcast_fusion.3
  154.5 0.4 convolution_bitcast_fusion.1
  155.0 1.4 fusion.4
  156.4 1.4 select_convert_fusion.1
  157.8 0.4 fusion.3
  158.3 0.4 select_convert_fusion
  158.8 4.6 %collective-permute-start.5 = (bf16[512,256]{0,1:T(8,128)(2,1)S(1)}, bf16[512,256]{0,1:T(8,128)(2,1)S(1)}, u32[]{:S(2)}, u32[]{:S(2)}) collective-permute-start(bf16[512,256]{0,1:T(8,128)(2,1)S(1)} %pad_maximum_fusion.1), channel_id=1, source_target_pairs={{0,64},{64,0},{1,65},{65,1},{2,66},{66,2},{3,67},{67,3},{4,68},{68... | collective-permute-start | bytes 786440 | tf_op jit(solution)/shard_map/ppermute | solution.py:19
  163.6 0.6 broadcast_multiply_fusion
  164.2 11.8 %collective-permute-done.5 = bf16[512,256]{0,1:T(8,128)(2,1)S(1)} collective-permute-done((bf16[512,256]{0,1:T(8,128)(2,1)S(1)}, bf16[512,256]{0,1:T(8,128)(2,1)S(1)}, u32[]{:S(2)}, u32[]{:S(2)}) %collective-permute-start.5) | collective-permute-done | bytes 262176 | tf_op jit(solution)/shard_map/ppermute | solution.py:19
  176.0 0.1 multiply_reduce_fusion.4
  176.2 0.2 fusion.6
  176.4 0.6 stack_broadcast_in_dim.3
  177.0 19.1 %all-gather.5 = f32[16,7,256]{2,1,0:T(8,128)S(1)} all-gather(f32[1,7,256]{2,1,0:T(8,128)S(1)} %bitcast.164), channel_id=5, replica_groups=mesh['group'=2,'zhigh'=2,'pair'=2,'y'=8,'xhigh'=2,'xlow'=2,'core'=2] {'g..., dimensions={0}, use_global_device_ids=true | all-gather | bytes 121856 | tf_op jit(solution)/shard_map/all_gather | solution.py:68
  196.3 0.2 multiply_convert_fusion.1
  196.5 5.3 %collective-permute-start.6 = (bf16[256,256]{0,1:T(8,128)(2,1)S(1)}, bf16[256,256]{0,1:T(8,128)(2,1)S(1)}, u32[]{:S(2)}, u32[]{:S(2)}) collective-permute-start(bf16[256,256]{0,1:T(8,128)(2,1)S(1)} %get-tuple-element.56), channel_id=1, source_target_pairs={{0,64},{64,0},{1,65},{65,1},{2,66},{66,2},{3,67},{67,3},{4,68},{68... | collective-permute-start | bytes 393224 | tf_op jit(solution)/shard_map/ppermute | solution.py:19
  201.8 6.8 %collective-permute-done.6 = bf16[256,256]{0,1:T(8,128)(2,1)S(1)} collective-permute-done((bf16[256,256]{0,1:T(8,128)(2,1)S(1)}, bf16[256,256]{0,1:T(8,128)(2,1)S(1)}, u32[]{:S(2)}, u32[]{:S(2)}) %collective-permute-start.6) | collective-permute-done | bytes 131104 | tf_op jit(solution)/shard_map/ppermute | solution.py:19
  208.6 0.3 fusion.11
  208.9 1.4 fusion.9
  210.3 1.4 fusion.1
  211.7 0.3 broadcast_select_fusion.5
  212.1 1.1 pad_maximum_fusion
  213.1 8.5 %all-to-all-start.2 = ((bf16[16,128,256]{2,1,0:T(8,128)(2,1)}), bf16[16,128,256]{2,1,0:T(8,128)(2,1)S(1)}, u32[]{:S(2)}, u32[]{:S(2)}) async-start(bf16[16,128,256]{2,1,0:T(8,128)(2,1)} %bitcast.43), calls=%async_computation.2 | async-start | bytes 2097152 | tf_op jit(solution)/shard_map/all_to_all | solution.py:169
  221.7 0.8 copy.108
  222.5 28.9 %all-to-all-done.2 = bf16[16,128,256]{2,1,0:T(8,128)(2,1)S(1)} async-done(((bf16[16,128,256]{2,1,0:T(8,128)(2,1)}), bf16[16,128,256]{2,1,0:T(8,128)(2,1)S(1)}, u32[]{:S(2)}, u32[]{:S(2)}) %all-to-all-start.2) | async-done | bytes 1048608 | tf_op jit(solution)/shard_map/all_to_all | solution.py:169
  251.4 0.8 convert_reduce_fusion
  (42 shorter events, 1.0 us)
Async XLA Ops:
  7.2 53.6 %all-gather.9.cloned.1.call-start = ((), (), s32[]{:S(2)}) async-start(), calls=%async_computation.3 | async-start | bytes 1474560 | tf_op jit(solution)/shard_map/all_gather | solution.py:91
  7.2 6.3 %collective-permute-start = (bf16[256,256]{1,0:T(8,128)(2,1)}, bf16[256,256]{1,0:T(8,128)(2,1)S(1)}, u32[]{:S(2)}, u32[]{:S(2)}) collective-permute-start(bf16[256,256]{1,0:T(8,128)(2,1)} %param.11), channel_id=1, source_target_pairs={{0,0},{4,64},{64,4},{68,68},{1,1},{5,65},{65,5},{69,69},{2,2},{6,6... | collective-permute-start | bytes 393224 | tf_op jit(solution)/shard_map/ppermute | solution.py:23
  10.5 0.7 copy-start.1
  13.5 39.8 %copy-start = (f32[256,384]{1,0:T(8,128)S(1)}, f32[256,384]{1,0:T(8,128)}, u32[]{:S(2)}) copy-start(f32[256,384]{1,0:T(8,128)} %param.7) | copy-start | bytes 1179652
  13.5 39.8 %copy-start.6 = (f32[384]{0:T(512)S(1)}, f32[384]{0:T(512)}, u32[]{:S(2)}) copy-start(f32[384]{0:T(512)} %param.8) | copy-start | bytes 4612
  14.6 38.9 %all-to-all-start = ((bf16[8,256,256]{2,1,0:T(8,128)(2,1)}), bf16[8,256,256]{2,1,0:T(8,128)(2,1)S(1)}, u32[]{:S(2)}, u32[]{:S(2)}) async-start(bf16[8,256,256]{2,1,0:T(8,128)(2,1)} %broadcast_in_dim.4), calls=%async_computation | async-start | bytes 2097152 | tf_op jit(solution)/shard_map/all_to_all | solution.py:29
  53.5 0.7 collective-permute-start.1
  62.1 13.4 %copy-start.2 = (bf16[320,256]{1,0:T(8,128)(2,1)S(1)}, bf16[320,256]{1,0:T(8,128)(2,1)}, u32[]{:S(2)}) copy-start(bf16[320,256]{1,0:T(8,128)(2,1)} %copy-done.1) | copy-start | bytes 491524
  62.1 87.1 %all-to-all-start.1 = ((bf16[8,256,384]{2,1,0:T(8,128)(2,1)}), bf16[8,256,384]{2,1,0:T(8,128)(2,1)S(1)}, u32[]{:S(2)}, u32[]{:S(2)}) async-start(bf16[8,256,384]{2,1,0:T(8,128)(2,1)} %broadcast_in_dim.5), calls=%async_computation.1 | async-start | bytes 3145728 | tf_op jit(solution)/shard_map/all_to_all | solution.py:29
  75.4 73.8 %all-gather.11.cloned.1.call-start = ((), (), s32[]{:S(2)}) async-start(), calls=%async_computation.4 | async-start | bytes 1474560 | tf_op jit(solution)/shard_map/all_gather | solution.py:98
  75.4 34.1 %collective-permute-start.2 = (bf16[320,256]{1,0:T(8,128)(2,1)S(1)}, bf16[320,256]{1,0:T(8,128)(2,1)S(1)}, u32[]{:S(2)}, u32[]{:S(2)}) collective-permute-start(bf16[320,256]{1,0:T(8,128)(2,1)S(1)} %copy-done.2), channel_id=1, source_target_pairs={{0,128},{128,0},{1,129},{129,1},{2,130},{130,2},{3,131},{131,3},{4... | collective-permute-start | bytes 491528 | tf_op jit(solution)/shard_map/ppermute | solution.py:19
  109.5 0.7 copy-start.4
  110.2 44.8 %collective-permute-start.3 = (bf16[8,256,256]{2,1,0:T(8,128)(2,1)S(1)}, bf16[8,256,256]{2,1,0:T(8,128)(2,1)}, u32[]{:S(2)}, u32[]{:S(2)}) collective-permute-start(bf16[8,256,256]{2,1,0:T(8,128)(2,1)S(1)} %all-to-all-done), channel_id=1, source_target_pairs={{0,1},{1,0},{2,3},{3,2},{4,5},{5,4},{6,7},{7,6},{8,9},{9,8},{10,11... | collective-permute-start | bytes 3145736 | tf_op jit(solution)/shard_map/ppermute | solution.py:19
  149.1 8.7 %collective-permute-start.4 = (bf16[8,256,384]{2,1,0:T(8,128)(2,1)S(1)}, bf16[8,256,384]{2,1,0:T(8,128)(2,1)S(1)}, u32[]{:S(2)}, u32[]{:S(2)}) collective-permute-start(bf16[8,256,384]{2,1,0:T(8,128)(2,1)S(1)} %all-to-all-done.1), channel_id=1, source_target_pairs={{0,1},{1,0},{2,3},{3,2},{4,5},{5,4},{6,7},{7,6},{8,9},{9,8},{10,11... | collective-permute-start | bytes 4718600 | tf_op jit(solution)/shard_map/ppermute | solution.py:19
  158.3 5.1 %copy-start.3 = (f32[256,256]{1,0:T(8,128)S(1)}, f32[256,256]{1,0:T(8,128)}, u32[]{:S(2)}) copy-start(f32[256,256]{1,0:T(8,128)} %param.10) | copy-start | bytes 786436
  158.3 5.3 %copy-start.5 = (f32[256]{0:T(256)S(1)}, f32[256]{0:T(256)}, u32[]{:S(2)}) copy-start(f32[256]{0:T(256)} %param.13) | copy-start | bytes 3076
  158.8 17.2 %collective-permute-start.5 = (bf16[512,256]{0,1:T(8,128)(2,1)S(1)}, bf16[512,256]{0,1:T(8,128)(2,1)S(1)}, u32[]{:S(2)}, u32[]{:S(2)}) collective-permute-start(bf16[512,256]{0,1:T(8,128)(2,1)S(1)} %pad_maximum_fusion.1), channel_id=1, source_target_pairs={{0,64},{64,0},{1,65},{65,1},{2,66},{66,2},{3,67},{67,3},{4,68},{68... | collective-permute-start | bytes 786440 | tf_op jit(solution)/shard_map/ppermute | solution.py:19
  196.5 12.1 %collective-permute-start.6 = (bf16[256,256]{0,1:T(8,128)(2,1)S(1)}, bf16[256,256]{0,1:T(8,128)(2,1)S(1)}, u32[]{:S(2)}, u32[]{:S(2)}) collective-permute-start(bf16[256,256]{0,1:T(8,128)(2,1)S(1)} %get-tuple-element.56), channel_id=1, source_target_pairs={{0,64},{64,0},{1,65},{65,1},{2,66},{66,2},{3,67},{67,3},{4,68},{68... | collective-permute-start | bytes 393224 | tf_op jit(solution)/shard_map/ppermute | solution.py:19
  213.1 38.3 %all-to-all-start.2 = ((bf16[16,128,256]{2,1,0:T(8,128)(2,1)}), bf16[16,128,256]{2,1,0:T(8,128)(2,1)S(1)}, u32[]{:S(2)}, u32[]{:S(2)}) async-start(bf16[16,128,256]{2,1,0:T(8,128)(2,1)} %bitcast.43), calls=%async_computation.2 | async-start | bytes 2097152 | tf_op jit(solution)/shard_map/all_to_all | solution.py:169
Sparse Core Ops, SparseCore 0:
  11.3 49.3 all-gather.8
  110.3 38.7 all-gather.10

commit v6 on v5

v6 whole, which is shorter than its diff:
```python
import math

import jax
import jax.numpy as jnp
from jax import lax
from jax.sharding import Mesh, PartitionSpec as P

EPSILON = 1e-05
BF16 = jnp.bfloat16
F32 = jnp.float32

TOKEN_AXES = ("zhigh", "zlow", "y")
SPLIT_AXES = ("zhigh", "zlow")
FEATURE_AXES = ("group", "xhigh", "xlow", "core")
CHIP_AXES = ("xlow", "group", "xhigh")


def turned(values):
    sizes = [lax.axis_size(name) for name in ("group", "zhigh", "zlow", "xhigh")]
    pairs = [
        (((a * sizes[1] + b) * sizes[2] + c) * sizes[3] + d, ((b * sizes[1] + a) * sizes[2] + d) * sizes[3] + c)
        for a in range(sizes[0])
        for b in range(sizes[1])
        for c in range(sizes[2])
        for d in range(sizes[3])
    ]
    return lax.ppermute(values, ("group", "zhigh", "zlow", "xhigh"), pairs)


def spread(values, axes):
    copies = jnp.broadcast_to(values[None], (lax.axis_size(axes), *values.shape))
    return lax.all_to_all(copies, axes, 0, 0, tiled=True)


def with_other_core(line):
    other = lax.ppermute(line, "core", [(0, 1), (1, 0)])
    return tuple(
        part.reshape(lax.axis_size("xlow"), -1, line.shape[2]) for part in (line, other)
    )


def both(first, place):
    return (
        jnp.where(place == 0, first[0], first[1]),
        jnp.where(place == 0, first[1], first[0]),
    )


def product(parts, weight_parts):
    dims = (((0, 2), (0, 1)), ((), ()))
    return sum(
        lax.dot_general(part, weight, dims, preferred_element_type=F32)
        for part, weight in zip(parts, weight_parts)
    )


def moments(values):
    mean = jnp.mean(values, axis=1)
    centered = values - mean[:, None]
    return mean, centered, jnp.sum(centered * centered, axis=1)


def combine(means, squares, width):
    mean = jnp.mean(means, axis=0)
    shift = means - mean
    variance = jnp.mean(squares / width + shift * shift, axis=0)
    return mean, shift, lax.rsqrt(variance + EPSILON)


def gather_rows(rows):
    return lax.all_gather(jnp.stack(rows, axis=0), FEATURE_AXES, axis=0)


def shards(
    teacher_stream,
    teacher_gain,
    projection,
    student_stream,
    student_context,
    out_weight,
    student_gain,
):
    core = lax.axis_index("core")
    place = lax.axis_index(SPLIT_AXES)
    splits = lax.axis_size(SPLIT_AXES)
    lanes, cores = (lax.axis_size(name) for name in ("xlow", "core"))
    blocks = lax.axis_size(FEATURE_AXES)
    tokens = teacher_stream.shape[0]
    token_count = tokens * lax.axis_size(TOKEN_AXES)
    width = student_stream.shape[1]
    depth = out_weight.shape[0]

    weights = lax.all_gather(jnp.concatenate([out_weight, projection], axis=0), "y", axis=0)
    together = lax.optimization_barrier
    mean, _, square = moments(teacher_stream)
    context, mean, square = together((turned(student_context), mean, square))
    table = gather_rows([mean, square])
    context, table = together((context, table))
    context = spread(context, CHIP_AXES)
    mean, _, inv_std = combine(table[:, 0], table[:, 1], teacher_stream.shape[1])
    hidden = ((teacher_stream - mean[:, None]) * inv_std[:, None] * teacher_gain).astype(BF16)
    hidden, weights = together((turned(hidden), weights))
    hidden = with_other_core(spread(hidden, CHIP_AXES))
    context = with_other_core(context)

    weights = weights.reshape(lanes, cores, 2, *weights.shape[1:]).transpose(1, 0, 2, 3, 4)

    def weight_parts(part):
        return both(part.reshape(cores, lanes, -1, width), core)

    branch = product(context, weight_parts(weights[..., :depth, :])).reshape(splits, tokens, width)
    target = product(hidden, weight_parts(weights[..., depth:, :])).reshape(splits, tokens, width)
    sent = jnp.concatenate([branch.astype(BF16), target.astype(BF16)], axis=1)
    received = lax.all_to_all(sent, SPLIT_AXES, 0, 0, tiled=True).astype(F32)

    def whole(partial, others):
        return sum(
            jnp.where(block == place, partial[block], others[block]) for block in range(splits)
        )

    pre_norm = student_stream + whole(branch, received[:, :tokens])
    target = whole(target, received[:, tokens:])

    block_mean, centered, square = moments(pre_norm)
    gain_square = student_gain * student_gain
    weighted = centered * gain_square
    scaled_target = target * student_gain
    table = gather_rows(
        [
            block_mean,
            square,
            jnp.sum(weighted, axis=1),
            jnp.sum(weighted * centered, axis=1),
            jnp.sum(scaled_target, axis=1),
            jnp.sum(scaled_target * centered, axis=1),
            jnp.full((tokens,), jnp.sum(gain_square), F32),
        ]
    )
    mean, shift, inv_std = combine(table[:, 0], table[:, 1], width)
    gains = table[:, 6]
    linear = jnp.sum(table[:, 2] + shift * gains, axis=0)
    quadratic = jnp.sum(table[:, 3] + shift * (2.0 * table[:, 2] + shift * gains), axis=0)
    target_sum = jnp.sum(table[:, 4], axis=0)
    target_cross = jnp.sum(table[:, 5] + shift * table[:, 4], axis=0)
    count = width * blocks
    scale = 1.0 / math.sqrt(token_count)
    first_mean = (inv_std * linear - target_sum) * (scale / count)
    second_mean = (inv_std * inv_std * quadratic - inv_std * target_cross) * (scale / count)

    normalized = (pre_norm - mean[:, None]) * inv_std[:, None]
    student_out = normalized * student_gain
    grad_norm = (student_out - target) * scale * student_gain
    grad_pre = (
        inv_std[:, None] * (grad_norm - first_mean[:, None] - normalized * second_mean[:, None])
    ).astype(BF16)
    grads = spread(grad_pre, SPLIT_AXES).reshape(splits * tokens, width)
    dims = (((1,), (0,)), ((), ()))
    partial = [
        lax.dot_general(part, grads, dims, preferred_element_type=F32).astype(BF16)
        for part in context
    ]
    partial = jnp.stack(both(partial, core), axis=0)
    partial = partial.reshape(cores, lanes, 2 * depth, width).transpose(1, 0, 2, 3)
    parts = lax.all_to_all(partial.reshape(-1, depth, width), "y", 0, 0, tiled=True)
    weight_grad = jnp.sum(parts.astype(F32), axis=0)
    return (student_out, weight_grad)


def solution(mesh):
    groups, token_blocks, columns = (mesh.shape[name] for name in ("group", "dp", "tensor"))
    cores, xhigh = 2, 2
    zhigh, zlow = groups, xhigh
    fine = Mesh(
        mesh.devices.reshape(
            groups, zhigh, zlow, token_blocks // (zhigh * zlow), xhigh, columns // (xhigh * cores), cores
        ),
        ("group", "zhigh", "zlow", "y", "xhigh", "xlow", "core"),
    )
    split = P(TOKEN_AXES, FEATURE_AXES)
    return jax.shard_map(
        shards,
        mesh=fine,
        in_specs=(
            split,
            P(FEATURE_AXES),
            split,
            split,
            split,
            split,
            P(FEATURE_AXES),
        ),
        out_specs=(split, split),
        check_vma=False,
    )
```

time: 260 us -> 216 us (0.83)
  the two profiles are of different devices: /device:TPU:8 before, /device:TPU:64 now
where the time goes in v6:
time: 216 us; the launch traced here: 215 us
  blocking collectives  77.9 us (36%)
  waiting for transfers between devices  58.5 us (27%)
  starting transfers between devices  41.4 us (19%)
  between operations  14.3 us (7%)
  matrix products  8.88 us (4%)
  other arithmetic  8.52 us (4%)
  local copies, waits for them, and re-layouts  5.53 us (3%)
    all_gather x2, blocking collectives, gather_rows(): return lax.all_gather(jnp.stack(rows, axis=0), FEATURE_AXES, axis=0)  34.4 us
    all_to_all x1, waiting for transfers between devices, shards(): received = lax.all_to_all(sent, SPLIT_AXES, 0, 0, tiled=True).astype(F32)  27.8 us
    all_to_all x2, waiting for transfers between devices, spread(): return lax.all_to_all(copies, axes, 0, 0, tiled=True)  24.1 us
    all_to_all x1, blocking collectives, shards(): lax.all_to_all(partial.reshape(-1, depth, width), 'y', 0, 0, tiled=True)  23.6 us
    all_to_all x1, blocking collectives, spread(): return lax.all_to_all(copies, axes, 0, 0, tiled=True)  19.9 us
    all_to_all x2, starting transfers between devices, spread(): return lax.all_to_all(copies, axes, 0, 0, tiled=True)  18.6 us
    ppermute x2, starting transfers between devices, turned(): return lax.ppermute(values, ('group', 'zhigh', 'zlow', 'xhigh'), pairs)  15 us
    dot_general x4, matrix products, product(): lax.dot_general(part, weight, dims, preferred_element_type=F32)  6.68 us
  transfers between devices with their start and end apart: 8, of which 5 were waited for; matrix products, arithmetic and copies ran while one was open for 5% of the time, Pallas kernels for 0%

profile of v6, /device:TPU:64, one launch (start us, length us, event | category | flops | bytes accessed | tf_op | source)
XLA Modules:
  0.0 215.1 jit_solution(17990985440006419241)
XLA Ops:
  7.2 0.0 all-gather.7.cloned.1.call-start
  7.2 9.1 %collective-permute-start = (bf16[256,256]{1,0:T(8,128)(2,1)}, bf16[256,256]{1,0:T(8,128)(2,1)S(1)}, u32[]{:S(2)}, u32[]{:S(2)}) collective-permute-start(bf16[256,256]{1,0:T(8,128)(2,1)} %param.11), channel_id=1, source_target_pairs={{0,0},{4,64},{64,4},{68,68},{128,256},{132,320},{192,260},{196,324... | collective-permute-start | bytes 393224 | tf_op jit(solution)/shard_map/ppermute | solution.py:27
  16.3 1.6 pad_maximum_fusion.1
  17.9 0.0 all-gather.7.cloned.1.call-update
  17.9 1.1 reduce_sum.162
  19.0 1.2 multiply_reduce_fusion
  20.2 0.0 collective-permute-done
  20.3 17.8 %all-gather.3 = f32[16,2,256]{2,1,0:T(2,128)S(1)} all-gather(f32[1,2,256]{2,1,0:T(2,128)S(1)} %maximum_bitcast_fusion.1), channel_id=2, replica_groups=mesh['group'=2,'zhigh'=2,'zlow'=2,'y'=8,'xhigh'=2,'xlow'=2,'core'=2] {'g..., dimensions={0}, use_global_device_ids=true | all-gather | bytes 34816 | tf_op jit(solution)/shard_map/all_gather | solution.py:71
  38.1 1.1 broadcast_in_dim.6
  39.1 7.6 %all-to-all-start = ((bf16[8,256,256]{2,1,0:T(8,128)(2,1)}), bf16[8,256,256]{2,1,0:T(8,128)(2,1)S(1)}, u32[]{:S(2)}, u32[]{:S(2)}) async-start(bf16[8,256,256]{2,1,0:T(8,128)(2,1)} %broadcast_in_dim.6), calls=%async_computation | async-start | bytes 2097152 | tf_op jit(solution)/shard_map/all_to_all | solution.py:32
  46.9 0.1 multiply_convert_fusion
  47.0 5.9 %collective-permute-start.1 = (bf16[256,384]{1,0:T(8,128)(2,1)S(1)}, bf16[256,384]{1,0:T(8,128)(2,1)S(1)}, u32[]{:S(2)}, u32[]{:S(2)}) collective-permute-start(bf16[256,384]{1,0:T(8,128)(2,1)S(1)} %multiply_convert_fusion), channel_id=1, source_target_pairs={{0,0},{4,64},{64,4},{68,68},{128,256},{132,320},{192,260},{196,324... | collective-permute-start | bytes 589832 | tf_op jit(solution)/shard_map/ppermute | solution.py:27
  52.9 6.0 %collective-permute-done.1 = bf16[256,384]{1,0:T(8,128)(2,1)S(1)} collective-permute-done((bf16[256,384]{1,0:T(8,128)(2,1)S(1)}, bf16[256,384]{1,0:T(8,128)(2,1)S(1)}, u32[]{:S(2)}, u32[]{:S(2)}) %collective-permute-start.1) | collective-permute-done | bytes 196640 | tf_op jit(solution)/shard_map/ppermute | solution.py:27
  58.9 0.6 all-gather.7.cloned.1.call-done
  59.5 4.3 %all-to-all-done = bf16[8,256,256]{2,1,0:T(8,128)(2,1)S(1)} async-done(((bf16[8,256,256]{2,1,0:T(8,128)(2,1)}), bf16[8,256,256]{2,1,0:T(8,128)(2,1)S(1)}, u32[]{:S(2)}, u32[]{:S(2)}) %all-to-all-start) | async-done | bytes 1048608 | tf_op jit(solution)/shard_map/all_to_all | solution.py:32
  63.8 1.3 broadcast_in_dim.7
  65.1 11.0 %all-to-all-start.1 = ((bf16[8,256,384]{2,1,0:T(8,128)(2,1)}), bf16[8,256,384]{2,1,0:T(8,128)(2,1)S(1)}, u32[]{:S(2)}, u32[]{:S(2)}) async-start(bf16[8,256,384]{2,1,0:T(8,128)(2,1)} %broadcast_in_dim.7), calls=%async_computation.1 | async-start | bytes 3145728 | tf_op jit(solution)/shard_map/all_to_all | solution.py:32
  76.1 1.9 collective-permute-start.2
  78.0 19.8 %all-to-all-done.1 = bf16[8,256,384]{2,1,0:T(8,128)(2,1)S(1)} async-done(((bf16[8,256,384]{2,1,0:T(8,128)(2,1)}), bf16[8,256,384]{2,1,0:T(8,128)(2,1)S(1)}, u32[]{:S(2)}, u32[]{:S(2)}) %all-to-all-start.1) | async-done | bytes 1572896 | tf_op jit(solution)/shard_map/all_to_all | solution.py:32
  97.8 1.9 collective-permute-start.3
  99.7 1.4 copy.100
  101.2 0.4 convolution_bitcast_fusion.3
  101.6 0.1 broadcast_select_fusion
  101.7 0.0 collective-permute-done.2
  101.7 2.6 %fusion.35 = (bf16[1024,256]{1,0:T(8,128)(2,1)S(1)}, f32[1024,256]{1,0:T(8,128)}) fusion(f32[1024,256]{1,0:T(8,128)S(1)} %convolution_bitcast_fusion.3, bf16[2,1024,256]{2,1,0:T(8,128)(2,1)} %bitcast.10, bf16[2,256,256]{2,1,0:T(8,128)(2,1)S(1)} %bitcast.200), kind=kOutput, calls=%fused_computation.91 | convolution fusion | flops 268959744 | bytes 3932160 | tf_op jit(solution)/shard_map/dot_general | solution.py:52
  104.4 0.6 convolution_bitcast_fusion.1
  104.9 0.0 collective-permute-done.3
  104.9 3.0 %fusion.34 = (bf16[1024,256]{1,0:T(8,128)(2,1)S(1)}, f32[1024,256]{1,0:T(8,128)}) fusion(f32[1024,256]{1,0:T(8,128)S(1)} %convolution_bitcast_fusion.1, bf16[2,1024,384]{2,1,0:T(8,128)(2,1)} %bitcast.17, bf16[2,384,256]{2,1,0:T(8,128)(2,1)S(1)} %bitcast.196), kind=kOutput, calls=%fused_computation.90 | convolution fusion | flops 403177472 | bytes 4587520 | tf_op jit(solution)/shard_map/dot_general | solution.py:52
  108.0 1.0 pad_maximum_fusion
  109.0 4.0 %all-to-all-start.2 = ((bf16[4,512,256]{2,1,0:T(8,128)(2,1)}), bf16[4,512,256]{2,1,0:T(8,128)(2,1)S(1)}, u32[]{:S(2)}, u32[]{:S(2)}) async-start(bf16[4,512,256]{2,1,0:T(8,128)(2,1)} %pad_maximum_fusion), calls=%async_computation.2 | async-start | bytes 2097152 | tf_op jit(solution)/shard_map/all_to_all | solution.py:114
  113.0 0.0 copy-done.4
  113.0 0.6 broadcast_multiply_fusion
  113.6 27.8 %all-to-all-done.2 = bf16[4,512,256]{2,1,0:T(8,128)(2,1)S(1)} async-done(((bf16[4,512,256]{2,1,0:T(8,128)(2,1)}), bf16[4,512,256]{2,1,0:T(8,128)(2,1)S(1)}, u32[]{:S(2)}, u32[]{:S(2)}) %all-to-all-start.2) | async-done | bytes 1048608 | tf_op jit(solution)/shard_map/all_to_all | solution.py:114
  141.4 0.2 convert_element_type.35
  141.6 0.2 fusion.32
  141.8 1.0 copy-done.1
  142.8 0.2 multiply_reduce_fusion.4
  143.0 0.3 fusion.2
  143.3 0.7 stack_broadcast_in_dim.3
  144.0 16.6 %all-gather.4 = f32[16,7,256]{2,1,0:T(8,128)S(1)} all-gather(f32[1,7,256]{2,1,0:T(8,128)S(1)} %bitcast.203), channel_id=4, replica_groups=mesh['group'=2,'zhigh'=2,'zlow'=2,'y'=8,'xhigh'=2,'xlow'=2,'core'=2] {'g..., dimensions={0}, use_global_device_ids=true | all-gather | bytes 121856 | tf_op jit(solution)/shard_map/all_gather | solution.py:71
  160.7 0.1 slice_reduce_fusion.1
  160.8 0.9 multiply_convert_fusion.1
  161.8 19.9 %all_to_all.25 = bf16[4,256,256]{2,1,0:T(8,128)(2,1)S(1)} all-to-all(bf16[4,256,256]{2,1,0:T(8,128)(2,1)S(1)} %broadcast_in_dim.8), channel_id=1, replica_groups=mesh['group'=2,'zhigh'=2,'zlow'=2,'y'=8,'xhigh'=2,'xlow'=2,'core'=2] {'z..., dimensions={0} | all-to-all | bytes 1048576 | tf_op jit(solution)/shard_map/all_to_all | solution.py:32
  181.7 0.5 convolution_convert_fusion.1
  182.2 1.7 select_bitcast_fusion.1
  183.9 0.1 maximum_bitcast_fusion
  184.0 23.6 %all_to_all.26 = bf16[8,128,256]{2,1,0:T(8,128)(2,1)S(1)} all-to-all(bf16[8,128,256]{2,1,0:T(8,128)(2,1)S(1)} %bitcast.195), channel_id=1, replica_groups=mesh['group'=2,'zhigh'=2,'zlow'=2,'y'=8,'xhigh'=2,'xlow'=2,'core'=2] {'y'}, dimensions={0} | all-to-all | bytes 1048576 | tf_op jit(solution)/shard_map/all_to_all | solution.py:164
  207.5 0.7 convert_reduce_fusion
  (26 shorter events, 0.3 us)
Async XLA Ops:
  7.2 52.3 %all-gather.7.cloned.1.call-start = ((), (), s32[]{:S(2)}) async-start(), calls=%async_computation.5 | async-start | bytes 1474560 | tf_op jit(solution)/shard_map/all_gather | solution.py:93
  7.2 13.0 %collective-permute-start = (bf16[256,256]{1,0:T(8,128)(2,1)}, bf16[256,256]{1,0:T(8,128)(2,1)S(1)}, u32[]{:S(2)}, u32[]{:S(2)}) collective-permute-start(bf16[256,256]{1,0:T(8,128)(2,1)} %param.11), channel_id=1, source_target_pairs={{0,0},{4,64},{64,4},{68,68},{128,256},{132,320},{192,260},{196,324... | collective-permute-start | bytes 393224 | tf_op jit(solution)/shard_map/ppermute | solution.py:27
  38.1 8.8 %copy-start.2 = (f32[256,384]{1,0:T(8,128)S(1)}, f32[256,384]{1,0:T(8,128)}, u32[]{:S(2)}) copy-start(f32[256,384]{1,0:T(8,128)} %param.7) | copy-start | bytes 1179652
  38.1 8.8 %copy-start.5 = (f32[384]{0:T(512)S(1)}, f32[384]{0:T(512)}, u32[]{:S(2)}) copy-start(f32[384]{0:T(512)} %param.8) | copy-start | bytes 4612
  39.1 24.7 %all-to-all-start = ((bf16[8,256,256]{2,1,0:T(8,128)(2,1)}), bf16[8,256,256]{2,1,0:T(8,128)(2,1)S(1)}, u32[]{:S(2)}, u32[]{:S(2)}) async-start(bf16[8,256,256]{2,1,0:T(8,128)(2,1)} %broadcast_in_dim.6), calls=%async_computation | async-start | bytes 2097152 | tf_op jit(solution)/shard_map/all_to_all | solution.py:32
  47.0 11.9 %collective-permute-start.1 = (bf16[256,384]{1,0:T(8,128)(2,1)S(1)}, bf16[256,384]{1,0:T(8,128)(2,1)S(1)}, u32[]{:S(2)}, u32[]{:S(2)}) collective-permute-start(bf16[256,384]{1,0:T(8,128)(2,1)S(1)} %multiply_convert_fusion), channel_id=1, source_target_pairs={{0,0},{4,64},{64,4},{68,68},{128,256},{132,320},{192,260},{196,324... | collective-permute-start | bytes 589832 | tf_op jit(solution)/shard_map/ppermute | solution.py:27
  65.1 32.7 %all-to-all-start.1 = ((bf16[8,256,384]{2,1,0:T(8,128)(2,1)}), bf16[8,256,384]{2,1,0:T(8,128)(2,1)S(1)}, u32[]{:S(2)}, u32[]{:S(2)}) async-start(bf16[8,256,384]{2,1,0:T(8,128)(2,1)} %broadcast_in_dim.7), calls=%async_computation.1 | async-start | bytes 3145728 | tf_op jit(solution)/shard_map/all_to_all | solution.py:32
  76.1 25.6 %collective-permute-start.2 = (bf16[8,256,256]{2,1,0:T(8,128)(2,1)S(1)}, bf16[8,256,256]{2,1,0:T(8,128)(2,1)}, u32[]{:S(2)}, u32[]{:S(2)}) collective-permute-start(bf16[8,256,256]{2,1,0:T(8,128)(2,1)S(1)} %all-to-all-done), channel_id=1, source_target_pairs={{0,1},{1,0},{2,3},{3,2},{4,5},{5,4},{6,7},{7,6},{8,9},{9,8},{10,11... | collective-permute-start | bytes 3145736 | tf_op jit(solution)/shard_map/ppermute | solution.py:36
  97.8 7.1 %collective-permute-start.3 = (bf16[8,256,384]{2,1,0:T(8,128)(2,1)S(1)}, bf16[8,256,384]{2,1,0:T(8,128)(2,1)}, u32[]{:S(2)}, u32[]{:S(2)}) collective-permute-start(bf16[8,256,384]{2,1,0:T(8,128)(2,1)S(1)} %all-to-all-done.1), channel_id=1, source_target_pairs={{0,1},{1,0},{2,3},{3,2},{4,5},{5,4},{6,7},{7,6},{8,9},{9,8},{10,11... | collective-permute-start | bytes 4718600 | tf_op jit(solution)/shard_map/ppermute | solution.py:36
  109.0 4.0 %copy-start.4 = (f32[256]{0:T(256)S(1)}, f32[256]{0:T(256)}, u32[]{:S(2)}) copy-start(f32[256]{0:T(256)} %param.13) | copy-start | bytes 3076
  109.0 32.4 %all-to-all-start.2 = ((bf16[4,512,256]{2,1,0:T(8,128)(2,1)}), bf16[4,512,256]{2,1,0:T(8,128)(2,1)S(1)}, u32[]{:S(2)}, u32[]{:S(2)}) async-start(bf16[4,512,256]{2,1,0:T(8,128)(2,1)} %pad_maximum_fusion), calls=%async_computation.2 | async-start | bytes 2097152 | tf_op jit(solution)/shard_map/all_to_all | solution.py:114
  113.6 28.0 %copy-start = (f32[1024,256]{1,0:T(8,128)S(1)}, f32[1024,256]{1,0:T(8,128)}, u32[]{:S(2)}) copy-start(f32[1024,256]{1,0:T(8,128)} %get-tuple-element.54) | copy-start | bytes 3145732
  113.6 28.0 %copy-start.3 = (f32[256,256]{1,0:T(8,128)S(1)}, f32[256,256]{1,0:T(8,128)}, u32[]{:S(2)}) copy-start(f32[256,256]{1,0:T(8,128)} %param.10) | copy-start | bytes 786436
  141.6 1.2 copy-start.1
Sparse Core Ops, SparseCore 0:
  18.0 41.4 all-gather.6

commit v7 on v6

--- a/solution.py
+++ b/solution.py
@@ -30,6 +30,47 @@
 def spread(values, axes):
     copies = jnp.broadcast_to(values[None], (lax.axis_size(axes), *values.shape))
     return lax.all_to_all(copies, axes, 0, 0, tiled=True)
+
+
+def group_pair(values):
+    other = lax.ppermute(values, "group", [(0, 1), (1, 0)])
+    return jnp.stack(both((values, other), lax.axis_index("group")), axis=0)
+
+
+def ring(values):
+    axes = ("xhigh", "xlow")
+    count = lax.axis_size(axes)
+    place = lax.axis_index(axes)
+    if count == 2:
+        lines = both((values, lax.ppermute(values, axes, [(0, 1), (1, 0)])), place)
+    else:
+        ahead = [(i, (i + 1) % count) for i in range(count)]
+        back = [(i, (i - 1) % count) for i in range(count)]
+        previous = lax.ppermute(values, axes, ahead)
+        following = lax.ppermute(values, axes, back)
+        opposite = jnp.stack(
+            [lax.ppermute(previous[0], axes, ahead), lax.ppermute(following[1], axes, back)],
+            axis=0,
+        )
+        pieces = [values, previous, opposite, following]
+        lines = [lax.select_n((place - j) & (count - 1), *pieces) for j in range(count)]
+    lanes = lax.axis_size("xlow")
+    line = jnp.stack(
+        [jnp.stack(lines[low::lanes], axis=1) for low in range(lanes)], axis=0
+    )
+    return line.reshape(-1, *values.shape[1:])
+
+
+def scatter(parts, axes):
+    count = lax.axis_size(axes)
+    place = lax.axis_index(axes)
+    total = sum(jnp.where(block == place, parts[block], 0.0) for block in range(count))
+    sent = parts.astype(BF16)
+    for step in (1, count - 1, 2):
+        chunk = lax.dynamic_index_in_dim(sent, (place + step) & (count - 1), 0, keepdims=False)
+        pairs = [(i, (i + step) % count) for i in range(count)]
+        total = total + lax.ppermute(chunk, axes, pairs).astype(F32)
+    return total
 
 
 def with_other_core(line):
@@ -93,14 +134,13 @@
     weights = lax.all_gather(jnp.concatenate([out_weight, projection], axis=0), "y", axis=0)
     together = lax.optimization_barrier
     mean, _, square = moments(teacher_stream)
-    context, mean, square = together((turned(student_context), mean, square))
+    context = group_pair(turned(student_context))
     table = gather_rows([mean, square])
-    context, table = together((context, table))
-    context = spread(context, CHIP_AXES)
     mean, _, inv_std = combine(table[:, 0], table[:, 1], teacher_stream.shape[1])
     hidden = ((teacher_stream - mean[:, None]) * inv_std[:, None] * teacher_gain).astype(BF16)
-    hidden, weights = together((turned(hidden), weights))
-    hidden = with_other_core(spread(hidden, CHIP_AXES))
+    context, hidden = together((context, turned(hidden)))
+    hidden = spread(hidden, CHIP_AXES)
+    context, weights = together((ring(context), weights))
     context = with_other_core(context)
 
     weights = weights.reshape(lanes, cores, 2, *weights.shape[1:]).transpose(1, 0, 2, 3, 4)
@@ -109,17 +149,15 @@
         return both(part.reshape(cores, lanes, -1, width), core)
 
     branch = product(context, weight_parts(weights[..., :depth, :])).reshape(splits, tokens, width)
+    hidden, _ = together((hidden, branch))
+    pre_norm = student_stream + scatter(branch, SPLIT_AXES)
+    hidden = with_other_core(hidden)
     target = product(hidden, weight_parts(weights[..., depth:, :])).reshape(splits, tokens, width)
-    sent = jnp.concatenate([branch.astype(BF16), target.astype(BF16)], axis=1)
-    received = lax.all_to_all(sent, SPLIT_AXES, 0, 0, tiled=True).astype(F32)
-
-    def whole(partial, others):
-        return sum(
-            jnp.where(block == place, partial[block], others[block]) for block in range(splits)
-        )
-
-    pre_norm = student_stream + whole(branch, received[:, :tokens])
-    target = whole(target, received[:, tokens:])
+    pre_norm, target = together((pre_norm, target))
+    received = lax.all_to_all(target.astype(BF16), SPLIT_AXES, 0, 0, tiled=True).astype(F32)
+    target = sum(
+        jnp.where(block == place, target[block], received[block]) for block in range(splits)
+    )
 
     block_mean, centered, square = moments(pre_norm)
     gain_square = student_gain * student_gain

time: 216 us -> 225 us (1.042)
  starting transfers between devices: 41.4 us -> 60.5 us
  waiting for transfers between devices: 58.5 us -> 44 us
  blocking collectives: 77.9 us -> 83.4 us
    ppermute x0 -> x8, starting transfers between devices: none -> 32.4 us  [the longest x3 13.9 us: scatter(): total = total + lax.ppermute(chunk, axes, pairs).astype(F32)]
    all_to_all x2 -> x1, waiting for transfers between devices: 24.1 us -> 0.01 us  [spread(): return lax.all_to_all(copies, axes, 0, 0, tiled=True)]
    ppermute x0 -> x8, waiting for transfers between devices: none -> 21.5 us  [the longest x1 16 us: ring(): lax.ppermute(following[1], axes, back)]
    all_to_all x1, waiting for transfers between devices: 27.8 us -> 13.5 us  [shards(): lax.all_to_all(target.astype(BF16), SPLIT_AXES, 0, 0, tiled=True)]
    all_to_all x2 -> x1, starting transfers between devices: 18.6 us -> 6.82 us  [spread(): return lax.all_to_all(copies, axes, 0, 0, tiled=True)]
    all_gather x2, blocking collectives: 34.4 us -> 40.3 us  [gather_rows(): return lax.all_gather(jnp.stack(rows, axis=0), FEATURE_AXES, axis=0)]
    ppermute x2, starting transfers between devices: 15 us -> 12.1 us  [turned(): return lax.ppermute(values, ('group', 'zhigh', 'zlow', 'xhigh'), pairs)]
    ppermute x2, waiting for transfers between devices: 5.99 us -> 8.67 us  [turned(): return lax.ppermute(values, ('group', 'zhigh', 'zlow', 'xhigh'), pairs)]
  transfers between devices with their start and end apart: 8 -> 15, of which waited for: 5 -> 6; matrix products, arithmetic and copies ran while one was open for 5% -> 6% of each run, Pallas kernels for 0% -> 0%
where the time goes in v7:
time: 225 us; the launch traced here: 224 us
  blocking collectives  83.4 us (37%)
  starting transfers between devices  60.5 us (27%)
  waiting for transfers between devices  44 us (20%)
  between operations  14.5 us (6%)
  other arithmetic  10.4 us (5%)
  matrix products  6.84 us (3%)
  local copies, waits for them, and re-layouts  4.09 us (2%)
    all_gather x2, blocking collectives, gather_rows(): return lax.all_gather(jnp.stack(rows, axis=0), FEATURE_AXES, axis=0)  40.3 us
    all_to_all x1, blocking collectives, shards(): lax.all_to_all(partial.reshape(-1, depth, width), 'y', 0, 0, tiled=True)  23.8 us
    all_to_all x1, blocking collectives, spread(): return lax.all_to_all(copies, axes, 0, 0, tiled=True)  19.3 us
    ppermute x1, waiting for transfers between devices, ring(): lax.ppermute(following[1], axes, back)  16 us
    ppermute x3, starting transfers between devices, scatter(): total = total + lax.ppermute(chunk, axes, pairs).astype(F32)  13.9 us
    all_to_all x1, waiting for transfers between devices, shards(): lax.all_to_all(target.astype(BF16), SPLIT_AXES, 0, 0, tiled=True)  13.5 us
    ppermute x2, starting transfers between devices, turned(): return lax.ppermute(values, ('group', 'zhigh', 'zlow', 'xhigh'), pairs)  12.1 us
    ppermute x2, waiting for transfers between devices, turned(): return lax.ppermute(values, ('group', 'zhigh', 'zlow', 'xhigh'), pairs)  8.67 us
  transfers between devices with their start and end apart: 15, of which 6 were waited for; matrix products, arithmetic and copies ran while one was open for 6% of the time, Pallas kernels for 0%

profile of v7, /device:TPU:64, one launch (start us, length us, event | category | flops | bytes accessed | tf_op | source)
XLA Modules:
  0.0 223.8 jit_solution(3706842385555088126)
XLA Ops:
  7.2 9.2 %collective-permute-start = (bf16[256,256]{1,0:T(8,128)(2,1)}, bf16[256,256]{1,0:T(8,128)(2,1)S(1)}, u32[]{:S(2)}, u32[]{:S(2)}) collective-permute-start(bf16[256,256]{1,0:T(8,128)(2,1)} %param.11), channel_id=1, source_target_pairs={{0,0},{4,64},{64,4},{68,68},{128,256},{132,320},{192,260},{196,324... | collective-permute-start | bytes 393224 | tf_op jit(solution)/shard_map/ppermute | solution.py:27
  16.5 1.6 pad_maximum_fusion.3
  18.1 1.1 reduce_sum.162
  19.2 1.2 multiply_reduce_fusion
  20.4 17.8 %all-gather.3 = f32[16,2,256]{2,1,0:T(2,128)S(1)} all-gather(f32[1,2,256]{2,1,0:T(2,128)S(1)} %maximum_bitcast_fusion.3), channel_id=2, replica_groups=mesh['group'=2,'zhigh'=2,'zlow'=2,'y'=8,'xhigh'=2,'xlow'=2,'core'=2] {'g..., dimensions={0}, use_global_device_ids=true | all-gather | bytes 34816 | tf_op jit(solution)/shard_map/all_gather | solution.py:112
  38.3 6.1 %collective-permute-start.1 = (bf16[256,256]{1,0:T(8,128)(2,1)S(1)}, bf16[256,256]{1,0:T(8,128)(2,1)S(1)}, u32[]{:S(2)}, u32[]{:S(2)}) collective-permute-start(bf16[256,256]{1,0:T(8,128)(2,1)S(1)} %collective-permute-done), channel_id=1, source_target_pairs={{0,256},{256,0},{1,257},{257,1},{2,258},{258,2},{3,259},{259,3},{4... | collective-permute-start | bytes 393224 | tf_op jit(solution)/shard_map/ppermute | solution.py:36
  44.4 0.8 multiply_convert_fusion
  45.2 2.8 %collective-permute-start.2 = (bf16[256,384]{1,0:T(8,128)(2,1)S(1)}, bf16[256,384]{1,0:T(8,128)(2,1)S(1)}, u32[]{:S(2)}, u32[]{:S(2)}) collective-permute-start(bf16[256,384]{1,0:T(8,128)(2,1)S(1)} %multiply_convert_fusion), channel_id=1, source_target_pairs={{0,0},{4,64},{64,4},{68,68},{128,256},{132,320},{192,260},{196,324... | collective-permute-start | bytes 589832 | tf_op jit(solution)/shard_map/ppermute | solution.py:27
  48.1 0.3 collective-permute-done.1
  48.4 8.7 %collective-permute-done.2 = bf16[256,384]{1,0:T(8,128)(2,1)S(1)} collective-permute-done((bf16[256,384]{1,0:T(8,128)(2,1)S(1)}, bf16[256,384]{1,0:T(8,128)(2,1)S(1)}, u32[]{:S(2)}, u32[]{:S(2)}) %collective-permute-start.2) | collective-permute-done | bytes 196640 | tf_op jit(solution)/shard_map/ppermute | solution.py:27
  57.1 2.3 %collective-permute-start.5 = (bf16[2,256,256]{2,1,0:T(8,128)(2,1)S(1)}, bf16[2,256,256]{2,1,0:T(8,128)(2,1)S(1)}, u32[]{:S(2)}, u32[]{:S(2)}) collective-permute-start(bf16[2,256,256]{2,1,0:T(8,128)(2,1)S(1)} %pad_maximum_fusion.1), channel_id=1, source_target_pairs={{0,6},{2,0},{4,2},{6,4},{1,7},{3,1},{5,3},{7,5},{8,14},{10,8},{12,... | collective-permute-start | bytes 786440 | tf_op jit(solution)/shard_map/ppermute | solution.py:50
  59.4 3.5 %collective-permute-start.3 = (bf16[2,256,256]{2,1,0:T(8,128)(2,1)S(1)}, bf16[2,256,256]{2,1,0:T(8,128)(2,1)S(1)}, u32[]{:S(2)}, u32[]{:S(2)}) collective-permute-start(bf16[2,256,256]{2,1,0:T(8,128)(2,1)S(1)} %pad_maximum_fusion.1), channel_id=1, source_target_pairs={{0,2},{2,4},{4,6},{6,0},{1,3},{3,5},{5,7},{7,1},{8,10},{10,12},{12... | collective-permute-start | bytes 786440 | tf_op jit(solution)/shard_map/ppermute | solution.py:49
  62.9 1.3 broadcast_in_dim.12
  64.2 6.8 %all-to-all-start = ((bf16[8,256,384]{2,1,0:T(8,128)(2,1)}), bf16[8,256,384]{2,1,0:T(8,128)(2,1)S(1)}, u32[]{:S(2)}, u32[]{:S(2)}) async-start(bf16[8,256,384]{2,1,0:T(8,128)(2,1)} %broadcast_in_dim.12), calls=%async_computation | async-start | bytes 3145728 | tf_op jit(solution)/shard_map/all_to_all | solution.py:32
  71.1 4.6 %collective-permute-start.6 = (bf16[256,256]{1,0:T(8,128)(2,1)S(1)}, bf16[256,256]{1,0:T(8,128)(2,1)S(1)}, u32[]{:S(2)}, u32[]{:S(2)}) collective-permute-start(bf16[256,256]{1,0:T(8,128)(2,1)S(1)} %slice_bitcast_fusion), channel_id=1, source_target_pairs={{0,6},{2,0},{4,2},{6,4},{1,7},{3,1},{5,3},{7,5},{8,14},{10,8},{12,... | collective-permute-start | bytes 393224 | tf_op jit(solution)/shard_map/ppermute | solution.py:52
  75.7 1.9 collective-permute-start.4
  77.6 16.0 %collective-permute-done.6 = bf16[256,256]{1,0:T(8,128)(2,1)S(1)} collective-permute-done((bf16[256,256]{1,0:T(8,128)(2,1)S(1)}, bf16[256,256]{1,0:T(8,128)(2,1)S(1)}, u32[]{:S(2)}, u32[]{:S(2)}) %collective-permute-start.6) | collective-permute-done | bytes 131104 | tf_op jit(solution)/shard_map/ppermute | solution.py:52
  94.0 1.9 collective-permute-start.7
  95.9 1.4 copy.114
  97.4 0.4 convolution_bitcast_fusion.3
  97.8 0.6 copy-done
  98.4 0.3 collective-permute-done.7
  98.7 1.7 fusion.1
  100.3 2.1 collective-permute-start.11
  102.5 1.2 broadcast_select_fusion
  103.8 5.1 %collective-permute-start.8 = (bf16[256,256]{1,0:T(8,128)(2,1)S(1)}, bf16[256,256]{1,0:T(8,128)(2,1)S(1)}, u32[]{:S(2)}, u32[]{:S(2)}) collective-permute-start(bf16[256,256]{1,0:T(8,128)(2,1)S(1)} %get-tuple-element.39), channel_id=1, source_target_pairs={{0,64},{64,128},{128,192},{192,0},{1,65},{65,129},{129,193},{193,1... | collective-permute-start | bytes 393224 | tf_op jit(solution)/shard_map/ppermute | solution.py:72
  108.9 3.6 %collective-permute-start.10 = (bf16[256,256]{1,0:T(8,128)(2,1)S(1)}, bf16[256,256]{1,0:T(8,128)(2,1)S(1)}, u32[]{:S(2)}, u32[]{:S(2)}) collective-permute-start(bf16[256,256]{1,0:T(8,128)(2,1)S(1)} %get-tuple-element.40), channel_id=1, source_target_pairs={{0,128},{64,192},{128,0},{192,64},{1,129},{65,193},{129,1},{193,65... | collective-permute-start | bytes 393224 | tf_op jit(solution)/shard_map/ppermute | solution.py:72
  112.6 5.2 %collective-permute-start.9 = (bf16[256,256]{1,0:T(8,128)(2,1)S(1)}, bf16[256,256]{1,0:T(8,128)(2,1)S(1)}, u32[]{:S(2)}, u32[]{:S(2)}) collective-permute-start(bf16[256,256]{1,0:T(8,128)(2,1)S(1)} %get-tuple-element.41), channel_id=1, source_target_pairs={{0,192},{64,0},{128,64},{192,128},{1,193},{65,1},{129,65},{193,129... | collective-permute-start | bytes 393224 | tf_op jit(solution)/shard_map/ppermute | solution.py:72
  117.8 0.6 convolution_bitcast_fusion.1
  118.4 5.2 %collective-permute-done.10 = bf16[256,256]{1,0:T(8,128)(2,1)S(1)} collective-permute-done((bf16[256,256]{1,0:T(8,128)(2,1)S(1)}, bf16[256,256]{1,0:T(8,128)(2,1)S(1)}, u32[]{:S(2)}, u32[]{:S(2)}) %collective-permute-start.10) | collective-permute-done | bytes 131104 | tf_op jit(solution)/shard_map/ppermute | solution.py:72
  123.6 0.1 fusion.11
  123.7 2.0 fusion
  125.7 0.8 convert_element_type.38
  126.5 5.1 %all-to-all-start.1 = ((bf16[4,256,256]{2,1,0:T(8,128)(2,1)}), bf16[4,256,256]{2,1,0:T(8,128)(2,1)S(1)}, u32[]{:S(2)}, u32[]{:S(2)}) async-start(bf16[4,256,256]{2,1,0:T(8,128)(2,1)} %convert_element_type.38), calls=%async_computation.1 | async-start | bytes 1048576 | tf_op jit(solution)/shard_map/all_to_all | solution.py:157
  131.6 0.6 broadcast_multiply_fusion
  132.2 0.1 reduce_sum.166
  132.4 13.5 %all-to-all-done.1 = bf16[4,256,256]{2,1,0:T(8,128)(2,1)S(1)} async-done(((bf16[4,256,256]{2,1,0:T(8,128)(2,1)}), bf16[4,256,256]{2,1,0:T(8,128)(2,1)S(1)}, u32[]{:S(2)}, u32[]{:S(2)}) %all-to-all-start.1) | async-done | bytes 524320 | tf_op jit(solution)/shard_map/all_to_all | solution.py:157
  146.0 0.2 multiply_reduce_fusion.4
  146.1 0.3 fusion.2
  146.4 0.7 stack_broadcast_in_dim.3
  147.1 22.5 %all-gather.4 = f32[16,7,256]{2,1,0:T(8,128)S(1)} all-gather(f32[1,7,256]{2,1,0:T(8,128)S(1)} %bitcast.181), channel_id=4, replica_groups=mesh['group'=2,'zhigh'=2,'zlow'=2,'y'=8,'xhigh'=2,'xlow'=2,'core'=2] {'g..., dimensions={0}, use_global_device_ids=true | all-gather | bytes 121856 | tf_op jit(solution)/shard_map/all_gather | solution.py:112
  169.6 0.1 slice_reduce_fusion
  169.8 0.9 multiply_convert_fusion.1
  170.7 19.3 %all_to_all.20 = bf16[4,256,256]{2,1,0:T(8,128)(2,1)S(1)} all-to-all(bf16[4,256,256]{2,1,0:T(8,128)(2,1)S(1)} %broadcast_in_dim.13), channel_id=1, replica_groups=mesh['group'=2,'zhigh'=2,'zlow'=2,'y'=8,'xhigh'=2,'xlow'=2,'core'=2] {'z..., dimensions={0} | all-to-all | bytes 1048576 | tf_op jit(solution)/shard_map/all_to_all | solution.py:32
  190.0 0.5 convolution_convert_fusion.1
  190.5 1.7 select_bitcast_fusion.1
  192.3 23.8 %all_to_all.21 = bf16[8,128,256]{2,1,0:T(8,128)(2,1)S(1)} all-to-all(bf16[8,128,256]{2,1,0:T(8,128)(2,1)S(1)} %bitcast.169), channel_id=1, replica_groups=mesh['group'=2,'zhigh'=2,'zlow'=2,'y'=8,'xhigh'=2,'xlow'=2,'core'=2] {'y'}, dimensions={0} | all-to-all | bytes 1048576 | tf_op jit(solution)/shard_map/all_to_all | solution.py:202
  216.2 0.7 convert_reduce_fusion
  (48 shorter events, 1.0 us)
Async XLA Ops:
  7.2 37.2 %copy-start.3 = (f32[256,384]{1,0:T(8,128)S(1)}, f32[256,384]{1,0:T(8,128)}, u32[]{:S(2)}) copy-start(f32[256,384]{1,0:T(8,128)} %param.7) | copy-start | bytes 1179652
  7.2 86.8 %all-gather.7.cloned.1.call-start = ((), (), s32[]{:S(2)}) async-start(), calls=%async_computation.4 | async-start | bytes 1474560 | tf_op jit(solution)/shard_map/all_gather | solution.py:134
  7.2 31.1 %collective-permute-start = (bf16[256,256]{1,0:T(8,128)(2,1)}, bf16[256,256]{1,0:T(8,128)(2,1)S(1)}, u32[]{:S(2)}, u32[]{:S(2)}) collective-permute-start(bf16[256,256]{1,0:T(8,128)(2,1)} %param.11), channel_id=1, source_target_pairs={{0,0},{4,64},{64,4},{68,68},{128,256},{132,320},{192,260},{196,324... | collective-permute-start | bytes 393224 | tf_op jit(solution)/shard_map/ppermute | solution.py:27
  38.3 10.1 %collective-permute-start.1 = (bf16[256,256]{1,0:T(8,128)(2,1)S(1)}, bf16[256,256]{1,0:T(8,128)(2,1)S(1)}, u32[]{:S(2)}, u32[]{:S(2)}) collective-permute-start(bf16[256,256]{1,0:T(8,128)(2,1)S(1)} %collective-permute-done), channel_id=1, source_target_pairs={{0,256},{256,0},{1,257},{257,1},{2,258},{258,2},{3,259},{259,3},{4... | collective-permute-start | bytes 393224 | tf_op jit(solution)/shard_map/ppermute | solution.py:36
  45.2 11.9 %collective-permute-start.2 = (bf16[256,384]{1,0:T(8,128)(2,1)S(1)}, bf16[256,384]{1,0:T(8,128)(2,1)S(1)}, u32[]{:S(2)}, u32[]{:S(2)}) collective-permute-start(bf16[256,384]{1,0:T(8,128)(2,1)S(1)} %multiply_convert_fusion), channel_id=1, source_target_pairs={{0,0},{4,64},{64,4},{68,68},{128,256},{132,320},{192,260},{196,324... | collective-permute-start | bytes 589832 | tf_op jit(solution)/shard_map/ppermute | solution.py:27
  57.1 14.0 %collective-permute-start.5 = (bf16[2,256,256]{2,1,0:T(8,128)(2,1)S(1)}, bf16[2,256,256]{2,1,0:T(8,128)(2,1)S(1)}, u32[]{:S(2)}, u32[]{:S(2)}) collective-permute-start(bf16[2,256,256]{2,1,0:T(8,128)(2,1)S(1)} %pad_maximum_fusion.1), channel_id=1, source_target_pairs={{0,6},{2,0},{4,2},{6,4},{1,7},{3,1},{5,3},{7,5},{8,14},{10,8},{12,... | collective-permute-start | bytes 786440 | tf_op jit(solution)/shard_map/ppermute | solution.py:50
  59.4 16.3 %collective-permute-start.3 = (bf16[2,256,256]{2,1,0:T(8,128)(2,1)S(1)}, bf16[2,256,256]{2,1,0:T(8,128)(2,1)S(1)}, u32[]{:S(2)}, u32[]{:S(2)}) collective-permute-start(bf16[2,256,256]{2,1,0:T(8,128)(2,1)S(1)} %pad_maximum_fusion.1), channel_id=1, source_target_pairs={{0,2},{2,4},{4,6},{6,0},{1,3},{3,5},{5,7},{7,1},{8,10},{10,12},{12... | collective-permute-start | bytes 786440 | tf_op jit(solution)/shard_map/ppermute | solution.py:49
  64.2 36.1 %all-to-all-start = ((bf16[8,256,384]{2,1,0:T(8,128)(2,1)}), bf16[8,256,384]{2,1,0:T(8,128)(2,1)S(1)}, u32[]{:S(2)}, u32[]{:S(2)}) async-start(bf16[8,256,384]{2,1,0:T(8,128)(2,1)} %broadcast_in_dim.12), calls=%async_computation | async-start | bytes 3145728 | tf_op jit(solution)/shard_map/all_to_all | solution.py:32
  71.1 22.6 %collective-permute-start.6 = (bf16[256,256]{1,0:T(8,128)(2,1)S(1)}, bf16[256,256]{1,0:T(8,128)(2,1)S(1)}, u32[]{:S(2)}, u32[]{:S(2)}) collective-permute-start(bf16[256,256]{1,0:T(8,128)(2,1)S(1)} %slice_bitcast_fusion), channel_id=1, source_target_pairs={{0,6},{2,0},{4,2},{6,4},{1,7},{3,1},{5,3},{7,5},{8,14},{10,8},{12,... | collective-permute-start | bytes 393224 | tf_op jit(solution)/shard_map/ppermute | solution.py:52
  75.7 18.0 %collective-permute-start.4 = (bf16[256,256]{1,0:T(8,128)(2,1)S(1)}, bf16[256,256]{1,0:T(8,128)(2,1)S(1)}, u32[]{:S(2)}, u32[]{:S(2)}) collective-permute-start(bf16[256,256]{1,0:T(8,128)(2,1)S(1)} %slice_bitcast_fusion.1), channel_id=1, source_target_pairs={{0,2},{2,4},{4,6},{6,0},{1,3},{3,5},{5,7},{7,1},{8,10},{10,12},{12... | collective-permute-start | bytes 393224 | tf_op jit(solution)/shard_map/ppermute | solution.py:52
  94.0 3.4 %copy-start.1 = (bf16[2,2,2,256,256]{4,3,2,1,0:T(8,128)(2,1)}, bf16[2,2,2,256,256]{4,3,2,1,0:T(8,128)(2,1)S(1)}, u32[]{:S(2)}) copy-start(bf16[2,2,2,256,256]{4,3,2,1,0:T(8,128)(2,1)S(1)} %pad_maximum_fusion) | copy-start | bytes 3145732
  94.0 4.7 %collective-permute-start.7 = (bf16[8,256,256]{2,1,0:T(8,128)(2,1)S(1)}, bf16[8,256,256]{2,1,0:T(8,128)(2,1)}, u32[]{:S(2)}, u32[]{:S(2)}) collective-permute-start(bf16[8,256,256]{2,1,0:T(8,128)(2,1)S(1)} %bitcast.166), channel_id=1, source_target_pairs={{0,1},{1,0},{2,3},{3,2},{4,5},{5,4},{6,7},{7,6},{8,9},{9,8},{10,11... | collective-permute-start | bytes 3145736 | tf_op jit(solution)/shard_map/ppermute | solution.py:77
  97.3 1.1 copy-start
  100.3 23.3 %collective-permute-start.11 = (bf16[8,256,384]{2,1,0:T(8,128)(2,1)S(1)}, bf16[8,256,384]{2,1,0:T(8,128)(2,1)}, u32[]{:S(2)}, u32[]{:S(2)}) collective-permute-start(bf16[8,256,384]{2,1,0:T(8,128)(2,1)S(1)} %all-to-all-done), channel_id=1, source_target_pairs={{0,1},{1,0},{2,3},{3,2},{4,5},{5,4},{6,7},{7,6},{8,9},{9,8},{10,11... | collective-permute-start | bytes 4718600 | tf_op jit(solution)/shard_map/ppermute | solution.py:77
  103.8 19.8 %copy-start.4 = (f32[256,256]{1,0:T(8,128)S(1)}, f32[256,256]{1,0:T(8,128)}, u32[]{:S(2)}) copy-start(f32[256,256]{1,0:T(8,128)} %param.10) | copy-start | bytes 786436
  103.8 14.6 %collective-permute-start.8 = (bf16[256,256]{1,0:T(8,128)(2,1)S(1)}, bf16[256,256]{1,0:T(8,128)(2,1)S(1)}, u32[]{:S(2)}, u32[]{:S(2)}) collective-permute-start(bf16[256,256]{1,0:T(8,128)(2,1)S(1)} %get-tuple-element.39), channel_id=1, source_target_pairs={{0,64},{64,128},{128,192},{192,0},{1,65},{65,129},{129,193},{193,1... | collective-permute-start | bytes 393224 | tf_op jit(solution)/shard_map/ppermute | solution.py:72
  108.9 14.6 %collective-permute-start.10 = (bf16[256,256]{1,0:T(8,128)(2,1)S(1)}, bf16[256,256]{1,0:T(8,128)(2,1)S(1)}, u32[]{:S(2)}, u32[]{:S(2)}) collective-permute-start(bf16[256,256]{1,0:T(8,128)(2,1)S(1)} %get-tuple-element.40), channel_id=1, source_target_pairs={{0,128},{64,192},{128,0},{192,64},{1,129},{65,193},{129,1},{193,65... | collective-permute-start | bytes 393224 | tf_op jit(solution)/shard_map/ppermute | solution.py:72
  112.6 11.0 %collective-permute-start.9 = (bf16[256,256]{1,0:T(8,128)(2,1)S(1)}, bf16[256,256]{1,0:T(8,128)(2,1)S(1)}, u32[]{:S(2)}, u32[]{:S(2)}) collective-permute-start(bf16[256,256]{1,0:T(8,128)(2,1)S(1)} %get-tuple-element.41), channel_id=1, source_target_pairs={{0,192},{64,0},{128,64},{192,128},{1,193},{65,1},{129,65},{193,129... | collective-permute-start | bytes 393224 | tf_op jit(solution)/shard_map/ppermute | solution.py:72
  125.7 6.0 %copy-start.5 = (f32[256]{0:T(256)S(1)}, f32[256]{0:T(256)}, u32[]{:S(2)}) copy-start(f32[256]{0:T(256)} %param.13) | copy-start | bytes 3076
  126.5 19.3 %all-to-all-start.1 = ((bf16[4,256,256]{2,1,0:T(8,128)(2,1)}), bf16[4,256,256]{2,1,0:T(8,128)(2,1)S(1)}, u32[]{:S(2)}, u32[]{:S(2)}) async-start(bf16[4,256,256]{2,1,0:T(8,128)(2,1)} %convert_element_type.38), calls=%async_computation.1 | async-start | bytes 1048576 | tf_op jit(solution)/shard_map/all_to_all | solution.py:157
  147.1 42.9 %copy-start.2 = (bf16[2,2,2,256,256]{4,3,2,1,0:T(8,128)(2,1)S(1)}, bf16[2,2,2,256,256]{4,3,2,1,0:T(8,128)(2,1)}, u32[]{:S(2)}) copy-start(bf16[2,2,2,256,256]{4,3,2,1,0:T(8,128)(2,1)} %copy-done.1) | copy-start | bytes 3145732
Sparse Core Ops, SparseCore 0:
  18.2 41.4 all-gather.6

commit v8 on v6

--- a/solution.py
+++ b/solution.py
@@ -92,34 +92,30 @@
 
     weights = lax.all_gather(jnp.concatenate([out_weight, projection], axis=0), "y", axis=0)
     together = lax.optimization_barrier
+    context = lax.all_gather(turned(student_context), FEATURE_AXES, axis=0)
     mean, _, square = moments(teacher_stream)
-    context, mean, square = together((turned(student_context), mean, square))
     table = gather_rows([mean, square])
-    context, table = together((context, table))
-    context = spread(context, CHIP_AXES)
     mean, _, inv_std = combine(table[:, 0], table[:, 1], teacher_stream.shape[1])
     hidden = ((teacher_stream - mean[:, None]) * inv_std[:, None] * teacher_gain).astype(BF16)
-    hidden, weights = together((turned(hidden), weights))
-    hidden = with_other_core(spread(hidden, CHIP_AXES))
-    context = with_other_core(context)
+    hidden, weights = together((spread(turned(hidden), CHIP_AXES), weights))
+    hidden = with_other_core(hidden)
 
-    weights = weights.reshape(lanes, cores, 2, *weights.shape[1:]).transpose(1, 0, 2, 3, 4)
+    out_full = weights[:, :depth].reshape(lanes * cores, -1, width)
+    projection_full = weights[:, depth:].reshape(lanes, cores, -1, width).transpose(1, 0, 2, 3)
+    target = product(hidden, both(projection_full, core))
 
-    def weight_parts(part):
-        return both(part.reshape(cores, lanes, -1, width), core)
-
-    branch = product(context, weight_parts(weights[..., :depth, :])).reshape(splits, tokens, width)
-    target = product(hidden, weight_parts(weights[..., depth:, :])).reshape(splits, tokens, width)
-    sent = jnp.concatenate([branch.astype(BF16), target.astype(BF16)], axis=1)
-    received = lax.all_to_all(sent, SPLIT_AXES, 0, 0, tiled=True).astype(F32)
-
-    def whole(partial, others):
+    def whole(partial):
+        partial = partial.reshape(splits, tokens, width)
+        others = lax.all_to_all(partial.astype(BF16), SPLIT_AXES, 0, 0, tiled=True).astype(F32)
         return sum(
             jnp.where(block == place, partial[block], others[block]) for block in range(splits)
         )
 
-    pre_norm = student_stream + whole(branch, received[:, :tokens])
-    target = whole(target, received[:, tokens:])
+    target = whole(target)
+    context, target = together((context, target))
+    context = context.reshape(splits, lanes * cores, tokens, width).transpose(1, 0, 2, 3)
+    context = context.reshape(lanes * cores, splits * tokens, width)
+    pre_norm = student_stream + whole(product([context], [out_full]))
 
     block_mean, centered, square = moments(pre_norm)
     gain_square = student_gain * student_gain
@@ -155,12 +151,7 @@
     ).astype(BF16)
     grads = spread(grad_pre, SPLIT_AXES).reshape(splits * tokens, width)
     dims = (((1,), (0,)), ((), ()))
-    partial = [
-        lax.dot_general(part, grads, dims, preferred_element_type=F32).astype(BF16)
-        for part in context
-    ]
-    partial = jnp.stack(both(partial, core), axis=0)
-    partial = partial.reshape(cores, lanes, 2 * depth, width).transpose(1, 0, 2, 3)
+    partial = lax.dot_general(context, grads, dims, preferred_element_type=F32).astype(BF16)
     parts = lax.all_to_all(partial.reshape(-1, depth, width), "y", 0, 0, tiled=True)
     weight_grad = jnp.sum(parts.astype(F32), axis=0)
     return (student_out, weight_grad)

time: 216 us -> 225 us (1.042)
  the two profiles are of different devices: /device:TPU:64 before, /device:TPU:8 now
where the time goes in v8:
time: 225 us; the launch traced here: 224 us
  blocking collectives  82 us (36%)
  waiting for transfers between devices  72.9 us (32%)
  starting transfers between devices  36.3 us (16%)
  between operations  14.2 us (6%)
  other arithmetic  8.04 us (4%)
  local copies, waits for them, and re-layouts  6.67 us (3%)
  matrix products  4.24 us (2%)
    all_gather x2, blocking collectives, gather_rows(): return lax.all_gather(jnp.stack(rows, axis=0), FEATURE_AXES, axis=0)  40.8 us
    all_to_all x2, waiting for transfers between devices, whole(): lax.all_to_all(partial.astype(BF16), SPLIT_AXES, 0, 0, tiled=True)  30.4 us
    all_to_all x1, waiting for transfers between devices, spread(): return lax.all_to_all(copies, axes, 0, 0, tiled=True)  23.7 us
    all_to_all x1, blocking collectives, shards(): lax.all_to_all(partial.reshape(-1, depth, width), 'y', 0, 0, tiled=True)  21.9 us
    all_to_all x1, starting transfers between devices, spread(): return lax.all_to_all(copies, axes, 0, 0, tiled=True)  20 us
    all_to_all x1, blocking collectives, spread(): return lax.all_to_all(copies, axes, 0, 0, tiled=True)  19.3 us
    all_gather x1, waiting for transfers between devices, shards(): context = lax.all_gather(turned(student_context), FEATURE_AXES, axis=0)  16.5 us
    all_to_all x2, starting transfers between devices, whole(): lax.all_to_all(partial.astype(BF16), SPLIT_AXES, 0, 0, tiled=True)  12.9 us
  transfers between devices with their start and end apart: 8, of which 6 were waited for; matrix products, arithmetic and copies ran while one was open for 4% of the time, Pallas kernels for 0%

profile of v8, /device:TPU:8, one launch (start us, length us, event | category | flops | bytes accessed | tf_op | source)
XLA Modules:
  0.0 224.4 jit_solution(5755208477881907723)
XLA Ops:
  7.2 0.0 copy-start
  7.2 0.0 all-gather.11.cloned.1.call-start
  7.2 1.6 pad_maximum_fusion
  8.8 0.0 all-gather.11.cloned.1.call-update
  8.9 1.1 reduce_sum.162
  10.0 1.2 multiply_reduce_fusion
  11.2 20.6 %all-gather.4 = f32[16,2,256]{2,1,0:T(2,128)S(1)} all-gather(f32[1,2,256]{2,1,0:T(2,128)S(1)} %maximum_bitcast_fusion), channel_id=3, replica_groups=mesh['group'=2,'zhigh'=2,'zlow'=2,'y'=8,'xhigh'=2,'xlow'=2,'core'=2] {'g..., dimensions={0}, use_global_device_ids=true | all-gather | bytes 34816 | tf_op jit(solution)/shard_map/all_gather | solution.py:71
  31.8 0.8 multiply_convert_fusion
  32.7 0.7 collective-permute-start.1
  33.3 0.0 collective-permute-done.1
  33.4 1.3 broadcast_in_dim.4
  34.6 20.0 %all-to-all-start = ((bf16[8,256,384]{2,1,0:T(8,128)(2,1)}), bf16[8,256,384]{2,1,0:T(8,128)(2,1)S(1)}, u32[]{:S(2)}, u32[]{:S(2)}) async-start(bf16[8,256,384]{2,1,0:T(8,128)(2,1)} %broadcast_in_dim.4), calls=%async_computation | async-start | bytes 3145728 | tf_op jit(solution)/shard_map/all_to_all | solution.py:32
  54.7 0.0 all-gather.9.cloned.1.call-start
  54.7 0.7 collective-permute-start
  55.4 0.0 collective-permute-done
  55.4 0.0 copy-start.3
  55.4 0.6 copy-done.3
  56.1 0.0 all-gather.9.cloned.1.call-update
  56.1 0.6 all-gather.11.cloned.1.call-done
  56.6 23.7 %all-to-all-done = bf16[8,256,384]{2,1,0:T(8,128)(2,1)S(1)} async-done(((bf16[8,256,384]{2,1,0:T(8,128)(2,1)}), bf16[8,256,384]{2,1,0:T(8,128)(2,1)S(1)}, u32[]{:S(2)}, u32[]{:S(2)}) %all-to-all-start) | async-done | bytes 1572896 | tf_op jit(solution)/shard_map/all_to_all | solution.py:32
  80.4 1.9 collective-permute-start.2
  82.3 1.2 slice.101
  83.5 0.6 convolution_bitcast_fusion.3
  84.1 1.6 collective-permute-done.2
  85.7 1.4 fusion.46
  87.1 7.0 %all-to-all-start.1 = ((bf16[4,256,256]{2,1,0:T(8,128)(2,1)}), bf16[4,256,256]{2,1,0:T(8,128)(2,1)S(1)}, u32[]{:S(2)}, u32[]{:S(2)}) async-start(bf16[4,256,256]{2,1,0:T(8,128)(2,1)} %bitcast.15), calls=%async_computation.1 | async-start | bytes 1048576 | tf_op jit(solution)/shard_map/all_to_all | solution.py:109
  94.0 1.1 slice.112
  95.1 15.9 %all-to-all-done.1 = bf16[4,256,256]{2,1,0:T(8,128)(2,1)S(1)} async-done(((bf16[4,256,256]{2,1,0:T(8,128)(2,1)}), bf16[4,256,256]{2,1,0:T(8,128)(2,1)S(1)}, u32[]{:S(2)}, u32[]{:S(2)}) %all-to-all-start.1) | async-done | bytes 524320 | tf_op jit(solution)/shard_map/all_to_all | solution.py:109
  111.0 0.1 convert_element_type.33
  111.1 0.1 fusion.23
  111.3 16.5 %all-gather.9.cloned.1.call-done = bf16[4096,256]{1,0:T(8,128)(2,1)} async-done(((bf16[256,256]{1,0:T(8,128)(2,1)}), bf16[4096,256]{1,0:T(8,128)(2,1)}) %all-gather.9.cloned.1.call-update) | async-done | bytes 2097168 | tf_op jit(solution)/shard_map/all_gather | solution.py:95
  127.8 1.7 copy.26
  129.5 0.0 copy-start.4
  129.5 1.5 fusion.47
  131.1 6.0 %all-to-all-start.2 = ((bf16[4,256,256]{2,1,0:T(8,128)(2,1)}), bf16[4,256,256]{2,1,0:T(8,128)(2,1)S(1)}, u32[]{:S(2)}, u32[]{:S(2)}) async-start(bf16[4,256,256]{2,1,0:T(8,128)(2,1)} %bitcast.25), calls=%async_computation.2 | async-start | bytes 1048576 | tf_op jit(solution)/shard_map/all_to_all | solution.py:109
  137.0 0.6 broadcast_multiply_fusion
  137.6 14.5 %all-to-all-done.2 = bf16[4,256,256]{2,1,0:T(8,128)(2,1)S(1)} async-done(((bf16[4,256,256]{2,1,0:T(8,128)(2,1)}), bf16[4,256,256]{2,1,0:T(8,128)(2,1)S(1)}, u32[]{:S(2)}, u32[]{:S(2)}) %all-to-all-start.2) | async-done | bytes 524320 | tf_op jit(solution)/shard_map/all_to_all | solution.py:109
  152.1 0.1 convert_element_type.36
  152.2 0.2 fusion.44
  152.4 0.3 fusion.13
  152.8 0.7 stack_broadcast_in_dim.3
  153.5 20.3 %all-gather.5 = f32[16,7,256]{2,1,0:T(8,128)S(1)} all-gather(f32[1,7,256]{2,1,0:T(8,128)S(1)} %bitcast.193), channel_id=5, replica_groups=mesh['group'=2,'zhigh'=2,'zlow'=2,'y'=8,'xhigh'=2,'xlow'=2,'core'=2] {'g..., dimensions={0}, use_global_device_ids=true | all-gather | bytes 121856 | tf_op jit(solution)/shard_map/all_gather | solution.py:71
  173.8 0.1 slice_reduce_fusion
  173.9 0.9 multiply_convert_fusion.1
  174.8 19.3 %all_to_all.25 = bf16[4,256,256]{2,1,0:T(8,128)(2,1)S(1)} all-to-all(bf16[4,256,256]{2,1,0:T(8,128)(2,1)S(1)} %broadcast_in_dim.5), channel_id=1, replica_groups=mesh['group'=2,'zhigh'=2,'zlow'=2,'y'=8,'xhigh'=2,'xlow'=2,'core'=2] {'z..., dimensions={0} | all-to-all | bytes 1048576 | tf_op jit(solution)/shard_map/all_to_all | solution.py:32
  194.2 0.8 fusion.1
  194.9 21.9 %all_to_all.26 = bf16[8,128,256]{2,1,0:T(8,128)(2,1)S(1)} all-to-all(bf16[8,128,256]{2,1,0:T(8,128)(2,1)S(1)} %bitcast.192), channel_id=1, replica_groups=mesh['group'=2,'zhigh'=2,'zlow'=2,'y'=8,'xhigh'=2,'xlow'=2,'core'=2] {'y'}, dimensions={0} | all-to-all | bytes 1048576 | tf_op jit(solution)/shard_map/all_to_all | solution.py:155
  216.8 0.7 convert_reduce_fusion
  (20 shorter events, 0.2 us)
Async XLA Ops:
  7.2 24.7 %copy-start = (f32[256,384]{1,0:T(8,128)S(1)}, f32[256,384]{1,0:T(8,128)}, u32[]{:S(2)}) copy-start(f32[256,384]{1,0:T(8,128)} %param.7) | copy-start | bytes 1179652
  7.2 49.5 %all-gather.11.cloned.1.call-start = ((), (), s32[]{:S(2)}) async-start(), calls=%async_computation.6 | async-start | bytes 1474560 | tf_op jit(solution)/shard_map/all_gather | solution.py:93
  32.7 0.7 collective-permute-start.1
  34.6 20.1 %copy-start.5 = (bf16[256,256]{1,0:T(8,128)(2,1)S(1)}, bf16[256,256]{1,0:T(8,128)(2,1)}, u32[]{:S(2)}) copy-start(bf16[256,256]{1,0:T(8,128)(2,1)} %param.11) | copy-start | bytes 393220
  34.6 45.7 %all-to-all-start = ((bf16[8,256,384]{2,1,0:T(8,128)(2,1)}), bf16[8,256,384]{2,1,0:T(8,128)(2,1)S(1)}, u32[]{:S(2)}, u32[]{:S(2)}) async-start(bf16[8,256,384]{2,1,0:T(8,128)(2,1)} %broadcast_in_dim.4), calls=%async_computation | async-start | bytes 3145728 | tf_op jit(solution)/shard_map/all_to_all | solution.py:32
  54.7 73.1 %all-gather.9.cloned.1.call-start = ((), (), s32[]{:S(2)}) async-start(), calls=%async_computation.5 | async-start | bytes 2228224 | tf_op jit(solution)/shard_map/all_gather | solution.py:95
  54.7 0.7 collective-permute-start
  55.4 0.7 copy-start.3
  80.4 5.3 %collective-permute-start.2 = (bf16[8,256,384]{2,1,0:T(8,128)(2,1)S(1)}, bf16[8,256,384]{2,1,0:T(8,128)(2,1)S(1)}, u32[]{:S(2)}, u32[]{:S(2)}) collective-permute-start(bf16[8,256,384]{2,1,0:T(8,128)(2,1)S(1)} %all-to-all-done), channel_id=1, source_target_pairs={{0,1},{1,0},{2,3},{3,2},{4,5},{5,4},{6,7},{7,6},{8,9},{9,8},{10,11... | collective-permute-start | bytes 4718600 | tf_op jit(solution)/shard_map/ppermute | solution.py:36
  87.1 24.0 %all-to-all-start.1 = ((bf16[4,256,256]{2,1,0:T(8,128)(2,1)}), bf16[4,256,256]{2,1,0:T(8,128)(2,1)S(1)}, u32[]{:S(2)}, u32[]{:S(2)}) async-start(bf16[4,256,256]{2,1,0:T(8,128)(2,1)} %bitcast.15), calls=%async_computation.1 | async-start | bytes 1048576 | tf_op jit(solution)/shard_map/all_to_all | solution.py:109
  129.5 7.5 %copy-start.4 = (f32[256]{0:T(256)S(1)}, f32[256]{0:T(256)}, u32[]{:S(2)}) copy-start(f32[256]{0:T(256)} %param.13) | copy-start | bytes 3076
  131.1 21.2 %copy-start.2 = (f32[256,256]{1,0:T(8,128)S(1)}, f32[256,256]{1,0:T(8,128)}, u32[]{:S(2)}) copy-start(f32[256,256]{1,0:T(8,128)} %param.10) | copy-start | bytes 786436
  131.1 21.1 %all-to-all-start.2 = ((bf16[4,256,256]{2,1,0:T(8,128)(2,1)}), bf16[4,256,256]{2,1,0:T(8,128)(2,1)S(1)}, u32[]{:S(2)}, u32[]{:S(2)}) async-start(bf16[4,256,256]{2,1,0:T(8,128)(2,1)} %bitcast.25), calls=%async_computation.2 | async-start | bytes 1048576 | tf_op jit(solution)/shard_map/all_to_all | solution.py:109
  153.5 40.7 %copy-start.1 = (bf16[4096,256]{1,0:T(8,128)(2,1)S(1)}, bf16[4096,256]{1,0:T(8,128)(2,1)}, u32[]{:S(2)}) copy-start(bf16[4096,256]{1,0:T(8,128)(2,1)} %all-gather.9.cloned.1.call-done) | copy-start | bytes 6291460
Sparse Core Ops, SparseCore 0:
  10.7 45.9 all-gather.10
  59.4 68.3 all-gather.8

commit v9 on v2

--- a/solution.py
+++ b/solution.py
@@ -31,14 +31,15 @@
     return jnp.concatenate([keep, swap(give, "row")], axis=0)
 
 
-def gather_features(values):
+def spread(values):
     axes = ("group", "x")
-    count = lax.axis_size(axes)
-    copies = jnp.broadcast_to(values[None], (count, *values.shape))
-    line = lax.all_to_all(copies, axes, 0, 0, tiled=True)
-    other = swap(line, "core")
+    copies = jnp.broadcast_to(values[None], (lax.axis_size(axes), *values.shape))
+    return lax.all_to_all(copies, axes, 0, 0, tiled=True)
+
+
+def with_other_core(line):
     return tuple(
-        part.transpose(1, 0, 2).reshape(values.shape[0], -1) for part in (line, other)
+        part.transpose(1, 0, 2).reshape(line.shape[1], -1) for part in (line, swap(line, "core"))
     )
 
 
@@ -98,18 +99,19 @@
     out_full = both(weights[:, :, :, :depth].reshape(cores, -1, width), core)
     projection_full = both(weights[:, :, :, depth:].reshape(cores, -1, width), core)
 
-    context = gather_features(split_tokens(student_context, row))
-
+    together = lax.optimization_barrier
+    context = split_tokens(student_context, row)
     teacher_mean, _, teacher_square = moments(teacher_stream)
     table = gather_rows([teacher_mean, teacher_square])
     mean, _, inv_std = combine(table[:, 0], table[:, 1], teacher_stream.shape[1])
     hidden = ((teacher_stream - mean[:, None]) * inv_std[:, None] * teacher_gain).astype(BF16)
-    hidden = gather_features(split_tokens(hidden, row))
-
+    hidden, context = together((spread(split_tokens(hidden, row)), context))
+    hidden = with_other_core(hidden)
+    target = product(hidden, projection_full)
+    target = target[:tokens] + swap(target[tokens:].astype(BF16), "row").astype(F32)
+    context = with_other_core(spread(context))
     branch = product(context, out_full)
     pre_norm = student_stream + (branch[:tokens] + swap(branch[tokens:].astype(BF16), "row").astype(F32))
-    target = product(hidden, projection_full)
-    target = target[:tokens] + swap(target[tokens:].astype(BF16), "row").astype(F32)
 
     block_mean, centered, square = moments(pre_norm)
     gain_square = student_gain * student_gain

time: 205 us -> 211 us (1.029)
  the two profiles are of different devices: /device:TPU:24 before, /device:TPU:25 now
where the time goes in v9:
time: 211 us
  waiting for transfers between devices  77.2 us (37%)
  starting transfers between devices  56.5 us (27%)
  blocking collectives  41.5 us (20%)
  between operations  14.3 us (7%)
  other arithmetic  9.56 us (5%)
  local copies, waits for them, and re-layouts  5.98 us (3%)
  matrix products  5.58 us (3%)
    all_gather x2, blocking collectives, gather_rows(): return lax.all_gather(jnp.stack(rows, axis=0), FEATURE_AXES, axis=0)  41.5 us
    all_to_all x1, waiting for transfers between devices, shards(): lax.all_to_all(partial.reshape(blocks, depth, width), GATHER_AXES, 0, 0,...  34.1 us
    ppermute x7, starting transfers between devices, swap(): return lax.ppermute(values, axis, [(0, 1), (1, 0)])  29.4 us
    all_to_all x2, waiting for transfers between devices, spread(): return lax.all_to_all(copies, axes, 0, 0, tiled=True)  26.4 us
    all_to_all x1, starting transfers between devices, shards(): lax.all_to_all(partial.reshape(blocks, depth, width), GATHER_AXES, 0, 0,...  18.3 us
    ppermute x7, waiting for transfers between devices, swap(): return lax.ppermute(values, axis, [(0, 1), (1, 0)])  16.7 us
    all_to_all x2, starting transfers between devices, spread(): return lax.all_to_all(copies, axes, 0, 0, tiled=True)  8.73 us
  transfers between devices with their start and end apart: 11, of which 8 were waited for; matrix products, arithmetic and copies ran while one was open for 6% of the time, Pallas kernels for 0%

profile of v9, /device:TPU:25, one launch (start us, length us, event | category | flops | bytes accessed | tf_op | source)
XLA Modules:
  0.0 210.6 jit_solution(4551042482468268846)
XLA Ops:
  7.2 1.6 pad_maximum_fusion.5
  8.9 1.1 reduce_sum.162
  10.0 1.2 multiply_reduce_fusion
  11.2 21.1 %all-gather.3 = f32[16,2,256]{2,1,0:T(2,128)S(1)} all-gather(f32[1,2,256]{2,1,0:T(2,128)S(1)} %maximum_bitcast_fusion), channel_id=2, replica_groups=mesh['group'=2,'zhigh'=4,'yhigh'=4,'row'=2,'x'=4,'core'=2] {'group','x',..., dimensions={0}, use_global_device_ids=true | all-gather | bytes 34816 | tf_op jit(solution)/shard_map/all_gather | solution.py:73
  32.3 0.8 multiply_convert_fusion
  33.2 0.1 broadcast_select_fusion.7
  33.3 2.1 collective-permute-start
  35.4 6.4 %collective-permute-done = bf16[256,192]{1,0:T(8,128)(2,1)S(1)} collective-permute-done((bf16[256,192]{1,0:T(8,128)(2,1)S(1)}, bf16[256,192]{1,0:T(8,128)(2,1)S(1)}, u32[]{:S(2)}, u32[]{:S(2)}) %collective-permute-start) | collective-permute-done | bytes 98336 | tf_op jit(solution)/shard_map/ppermute | solution.py:18
  41.8 0.1 copy.32
  41.9 1.3 broadcast_in_dim.4
  43.2 3.7 %all-to-all-start = ((bf16[8,512,192]{1,2,0:T(8,128)(2,1)}), bf16[8,512,192]{1,2,0:T(8,128)(2,1)S(1)}, u32[]{:S(2)}, u32[]{:S(2)}) async-start(bf16[8,512,192]{1,2,0:T(8,128)(2,1)} %broadcast_in_dim.4), calls=%async_computation | async-start | bytes 3145728 | tf_op jit(solution)/shard_map/all_to_all | solution.py:37
  47.0 2.4 %collective-permute-start.1 = (bf16[256,128]{1,0:T(8,128)(2,1)S(1)}, bf16[256,128]{1,0:T(8,128)(2,1)S(1)}, u32[]{:S(2)}, u32[]{:S(2)}) collective-permute-start(bf16[256,128]{1,0:T(8,128)(2,1)S(1)} %get-tuple-element.45), channel_id=1, source_target_pairs={{0,8},{8,0},{1,9},{9,1},{2,10},{10,2},{3,11},{11,3},{4,12},{12,4},... | collective-permute-start | bytes 196616 | tf_op jit(solution)/shard_map/ppermute | solution.py:18
  49.4 2.9 %collective-permute-done.1 = bf16[256,128]{1,0:T(8,128)(2,1)S(1)} collective-permute-done((bf16[256,128]{1,0:T(8,128)(2,1)S(1)}, bf16[256,128]{1,0:T(8,128)(2,1)S(1)}, u32[]{:S(2)}, u32[]{:S(2)}) %collective-permute-start.1) | collective-permute-done | bytes 65568 | tf_op jit(solution)/shard_map/ppermute | solution.py:18
  52.3 21.7 %all-to-all-done = bf16[8,512,192]{1,2,0:T(8,128)(2,1)S(1)} async-done(((bf16[8,512,192]{1,2,0:T(8,128)(2,1)}), bf16[8,512,192]{1,2,0:T(8,128)(2,1)S(1)}, u32[]{:S(2)}, u32[]{:S(2)}) %all-to-all-start) | async-done | bytes 1572896 | tf_op jit(solution)/shard_map/all_to_all | solution.py:37
  74.0 0.1 copy.33
  74.1 1.1 broadcast_in_dim.5
  75.2 0.3 copy-done.2
  75.4 5.0 %all-to-all-start.1 = ((bf16[8,512,128]{1,2,0:T(8,128)(2,1)}), bf16[8,512,128]{1,2,0:T(8,128)(2,1)S(1)}, u32[]{:S(2)}, u32[]{:S(2)}) async-start(bf16[8,512,128]{1,2,0:T(8,128)(2,1)} %broadcast_in_dim.5), calls=%async_computation.1 | async-start | bytes 2097152 | tf_op jit(solution)/shard_map/all_to_all | solution.py:37
  80.5 0.1 copy.34
  80.6 9.7 %collective-permute-start.4 = (bf16[8,512,192]{1,2,0:T(8,128)(2,1)}, bf16[8,512,192]{1,2,0:T(8,128)(2,1)S(1)}, u32[]{:S(2)}, u32[]{:S(2)}) collective-permute-start(bf16[8,512,192]{1,2,0:T(8,128)(2,1)} %copy-done.2), channel_id=1, source_target_pairs={{0,1},{1,0},{2,3},{3,2},{4,5},{5,4},{6,7},{7,6},{8,9},{9,8},{10,11... | collective-permute-start | bytes 4718600 | tf_op jit(solution)/shard_map/ppermute | solution.py:18
  90.3 0.6 broadcast_multiply_fusion
  90.9 4.7 %all-to-all-done.1 = bf16[8,512,128]{1,2,0:T(8,128)(2,1)S(1)} async-done(((bf16[8,512,128]{1,2,0:T(8,128)(2,1)}), bf16[8,512,128]{1,2,0:T(8,128)(2,1)S(1)}, u32[]{:S(2)}, u32[]{:S(2)}) %all-to-all-start.1) | async-done | bytes 1048608 | tf_op jit(solution)/shard_map/all_to_all | solution.py:37
  95.6 6.7 %collective-permute-start.2 = (bf16[8,512,128]{1,2,0:T(8,128)(2,1)S(1)}, bf16[8,512,128]{1,2,0:T(8,128)(2,1)}, u32[]{:S(2)}, u32[]{:S(2)}) collective-permute-start(bf16[8,512,128]{1,2,0:T(8,128)(2,1)S(1)} %all-to-all-done.1), channel_id=1, source_target_pairs={{0,1},{1,0},{2,3},{3,2},{4,5},{5,4},{6,7},{7,6},{8,9},{9,8},{10,11... | collective-permute-start | bytes 3145736 | tf_op jit(solution)/shard_map/ppermute | solution.py:18
  102.4 1.4 broadcast_select_fusion.4
  103.9 0.5 fusion.20
  104.4 0.1 copy-done.1
  104.5 0.1 broadcast_select_fusion
  104.6 1.3 copy-done.3
  105.9 0.6 fusion.21
  106.5 1.7 convolution_add_fusion
  108.3 2.4 %collective-permute-start.3 = (bf16[256,256]{0,1:T(8,128)(2,1)S(1)}, bf16[256,256]{0,1:T(8,128)(2,1)S(1)}, u32[]{:S(2)}, u32[]{:S(2)}) collective-permute-start(bf16[256,256]{0,1:T(8,128)(2,1)S(1)} %slice.157), channel_id=1, source_target_pairs={{0,8},{8,0},{1,9},{9,1},{2,10},{10,2},{3,11},{11,3},{4,12},{12,4},... | collective-permute-start | bytes 393224 | tf_op jit(solution)/shard_map/ppermute | solution.py:18
  110.7 0.6 convolution_add_fusion.1
  111.3 2.9 %collective-permute-start.5 = (bf16[256,256]{0,1:T(8,128)(2,1)S(1)}, bf16[256,256]{0,1:T(8,128)(2,1)S(1)}, u32[]{:S(2)}, u32[]{:S(2)}) collective-permute-start(bf16[256,256]{0,1:T(8,128)(2,1)S(1)} %slice.156), channel_id=1, source_target_pairs={{0,8},{8,0},{1,9},{9,1},{2,10},{10,2},{3,11},{11,3},{4,12},{12,4},... | collective-permute-start | bytes 393224 | tf_op jit(solution)/shard_map/ppermute | solution.py:18
  114.2 1.0 collective-permute-done.3
  115.4 2.7 %collective-permute-done.5 = bf16[256,256]{0,1:T(8,128)(2,1)S(1)} collective-permute-done((bf16[256,256]{0,1:T(8,128)(2,1)S(1)}, bf16[256,256]{0,1:T(8,128)(2,1)S(1)}, u32[]{:S(2)}, u32[]{:S(2)}) %collective-permute-start.5) | collective-permute-done | bytes 131104 | tf_op jit(solution)/shard_map/ppermute | solution.py:18
  118.0 0.2 multiply_reduce_fusion.2
  118.2 0.6 stack_broadcast_in_dim.3
  118.9 20.4 %all-gather.4 = f32[16,7,256]{2,1,0:T(8,128)S(1)} all-gather(f32[1,7,256]{2,1,0:T(8,128)S(1)} %bitcast.125), channel_id=4, replica_groups=mesh['group'=2,'zhigh'=4,'yhigh'=4,'row'=2,'x'=4,'core'=2] {'group','x',..., dimensions={0}, use_global_device_ids=true | all-gather | bytes 121856 | tf_op jit(solution)/shard_map/all_gather | solution.py:73
  139.5 0.2 multiply_convert_fusion.1
  139.6 3.2 %collective-permute-start.6 = (bf16[256,256]{0,1:T(8,128)(2,1)S(1)}, bf16[256,256]{0,1:T(8,128)(2,1)S(1)}, u32[]{:S(2)}, u32[]{:S(2)}) collective-permute-start(bf16[256,256]{0,1:T(8,128)(2,1)S(1)} %get-tuple-element.33), channel_id=1, source_target_pairs={{0,8},{8,0},{1,9},{9,1},{2,10},{10,2},{3,11},{11,3},{4,12},{12,4},... | collective-permute-start | bytes 393224 | tf_op jit(solution)/shard_map/ppermute | solution.py:18
  142.8 3.7 %collective-permute-done.6 = bf16[256,256]{0,1:T(8,128)(2,1)S(1)} collective-permute-done((bf16[256,256]{0,1:T(8,128)(2,1)S(1)}, bf16[256,256]{0,1:T(8,128)(2,1)S(1)}, u32[]{:S(2)}, u32[]{:S(2)}) %collective-permute-start.6) | collective-permute-done | bytes 131104 | tf_op jit(solution)/shard_map/ppermute | solution.py:18
  146.5 1.7 convolution_convert_fusion
  148.2 0.5 broadcast_select_fusion.3
  148.6 1.1 pad_maximum_fusion
  149.7 18.3 %all-to-all-start.2 = ((bf16[16,128,256]{2,1,0:T(8,128)(2,1)}), bf16[16,128,256]{2,1,0:T(8,128)(2,1)S(1)}, u32[]{:S(2)}, u32[]{:S(2)}) async-start(bf16[16,128,256]{2,1,0:T(8,128)(2,1)} %bitcast.39), calls=%async_computation.2 | async-start | bytes 2097152 | tf_op jit(solution)/shard_map/all_to_all | solution.py:158
  168.0 0.8 copy.43
  168.9 34.1 %all-to-all-done.2 = bf16[16,128,256]{2,1,0:T(8,128)(2,1)S(1)} async-done(((bf16[16,128,256]{2,1,0:T(8,128)(2,1)}), bf16[16,128,256]{2,1,0:T(8,128)(2,1)S(1)}, u32[]{:S(2)}, u32[]{:S(2)}) %all-to-all-start.2) | async-done | bytes 1048608 | tf_op jit(solution)/shard_map/all_to_all | solution.py:158
  203.0 0.8 convert_reduce_fusion
  (34 shorter events, 0.6 us)
Async XLA Ops:
  7.2 25.2 %copy-start = (f32[256,384]{1,0:T(8,128)S(1)}, f32[256,384]{1,0:T(8,128)}, u32[]{:S(2)}) copy-start(f32[256,384]{1,0:T(8,128)} %param.7) | copy-start | bytes 1179652
  7.2 95.2 %all-gather.7.cloned.1.call-start = ((), (), s32[]{:S(2)}) async-start(), calls=%async_computation.3 | async-start | bytes 2785280 | tf_op jit(solution)/shard_map/all_gather | solution.py:93
  33.3 8.5 %collective-permute-start = (bf16[256,192]{1,0:T(8,128)(2,1)S(1)}, bf16[256,192]{1,0:T(8,128)(2,1)S(1)}, u32[]{:S(2)}, u32[]{:S(2)}) collective-permute-start(bf16[256,192]{1,0:T(8,128)(2,1)S(1)} %get-tuple-element.36), channel_id=1, source_target_pairs={{0,8},{8,0},{1,9},{9,1},{2,10},{10,2},{3,11},{11,3},{4,12},{12,4},... | collective-permute-start | bytes 294920 | tf_op jit(solution)/shard_map/ppermute | solution.py:18
  43.2 3.7 %copy-start.5 = (bf16[256,256]{1,0:T(8,128)(2,1)S(1)}, bf16[256,256]{1,0:T(8,128)(2,1)}, u32[]{:S(2)}) copy-start(bf16[256,256]{1,0:T(8,128)(2,1)} %param.11) | copy-start | bytes 393220
  43.2 30.7 %all-to-all-start = ((bf16[8,512,192]{1,2,0:T(8,128)(2,1)}), bf16[8,512,192]{1,2,0:T(8,128)(2,1)S(1)}, u32[]{:S(2)}, u32[]{:S(2)}) async-start(bf16[8,512,192]{1,2,0:T(8,128)(2,1)} %broadcast_in_dim.4), calls=%async_computation | async-start | bytes 3145728 | tf_op jit(solution)/shard_map/all_to_all | solution.py:37
  47.0 5.3 %collective-permute-start.1 = (bf16[256,128]{1,0:T(8,128)(2,1)S(1)}, bf16[256,128]{1,0:T(8,128)(2,1)S(1)}, u32[]{:S(2)}, u32[]{:S(2)}) collective-permute-start(bf16[256,128]{1,0:T(8,128)(2,1)S(1)} %get-tuple-element.45), channel_id=1, source_target_pairs={{0,8},{8,0},{1,9},{9,1},{2,10},{10,2},{3,11},{11,3},{4,12},{12,4},... | collective-permute-start | bytes 196616 | tf_op jit(solution)/shard_map/ppermute | solution.py:18
  74.0 1.5 copy-start.2
  74.1 6.4 %copy-start.4 = (f32[256,256]{1,0:T(8,128)S(1)}, f32[256,256]{1,0:T(8,128)}, u32[]{:S(2)}) copy-start(f32[256,256]{1,0:T(8,128)} %param.10) | copy-start | bytes 786436
  75.2 15.2 %copy-start.6 = (f32[256]{0:T(256)S(1)}, f32[256]{0:T(256)}, u32[]{:S(2)}) copy-start(f32[256]{0:T(256)} %param.13) | copy-start | bytes 3076
  75.4 20.2 %all-to-all-start.1 = ((bf16[8,512,128]{1,2,0:T(8,128)(2,1)}), bf16[8,512,128]{1,2,0:T(8,128)(2,1)S(1)}, u32[]{:S(2)}, u32[]{:S(2)}) async-start(bf16[8,512,128]{1,2,0:T(8,128)(2,1)} %broadcast_in_dim.5), calls=%async_computation.1 | async-start | bytes 2097152 | tf_op jit(solution)/shard_map/all_to_all | solution.py:37
  80.6 30.1 %collective-permute-start.4 = (bf16[8,512,192]{1,2,0:T(8,128)(2,1)}, bf16[8,512,192]{1,2,0:T(8,128)(2,1)S(1)}, u32[]{:S(2)}, u32[]{:S(2)}) collective-permute-start(bf16[8,512,192]{1,2,0:T(8,128)(2,1)} %copy-done.2), channel_id=1, source_target_pairs={{0,1},{1,0},{2,3},{3,2},{4,5},{5,4},{6,7},{7,6},{8,9},{9,8},{10,11... | collective-permute-start | bytes 4718600 | tf_op jit(solution)/shard_map/ppermute | solution.py:18
  95.6 10.9 %collective-permute-start.2 = (bf16[8,512,128]{1,2,0:T(8,128)(2,1)S(1)}, bf16[8,512,128]{1,2,0:T(8,128)(2,1)}, u32[]{:S(2)}, u32[]{:S(2)}) collective-permute-start(bf16[8,512,128]{1,2,0:T(8,128)(2,1)S(1)} %all-to-all-done.1), channel_id=1, source_target_pairs={{0,1},{1,0},{2,3},{3,2},{4,5},{5,4},{6,7},{7,6},{8,9},{9,8},{10,11... | collective-permute-start | bytes 3145736 | tf_op jit(solution)/shard_map/ppermute | solution.py:18
  102.4 2.1 copy-start.1
  104.5 1.4 copy-start.3
  108.3 7.0 %collective-permute-start.3 = (bf16[256,256]{0,1:T(8,128)(2,1)S(1)}, bf16[256,256]{0,1:T(8,128)(2,1)S(1)}, u32[]{:S(2)}, u32[]{:S(2)}) collective-permute-start(bf16[256,256]{0,1:T(8,128)(2,1)S(1)} %slice.157), channel_id=1, source_target_pairs={{0,8},{8,0},{1,9},{9,1},{2,10},{10,2},{3,11},{11,3},{4,12},{12,4},... | collective-permute-start | bytes 393224 | tf_op jit(solution)/shard_map/ppermute | solution.py:18
  111.3 6.7 %collective-permute-start.5 = (bf16[256,256]{0,1:T(8,128)(2,1)S(1)}, bf16[256,256]{0,1:T(8,128)(2,1)S(1)}, u32[]{:S(2)}, u32[]{:S(2)}) collective-permute-start(bf16[256,256]{0,1:T(8,128)(2,1)S(1)} %slice.156), channel_id=1, source_target_pairs={{0,8},{8,0},{1,9},{9,1},{2,10},{10,2},{3,11},{11,3},{4,12},{12,4},... | collective-permute-start | bytes 393224 | tf_op jit(solution)/shard_map/ppermute | solution.py:18
  139.6 6.8 %collective-permute-start.6 = (bf16[256,256]{0,1:T(8,128)(2,1)S(1)}, bf16[256,256]{0,1:T(8,128)(2,1)S(1)}, u32[]{:S(2)}, u32[]{:S(2)}) collective-permute-start(bf16[256,256]{0,1:T(8,128)(2,1)S(1)} %get-tuple-element.33), channel_id=1, source_target_pairs={{0,8},{8,0},{1,9},{9,1},{2,10},{10,2},{3,11},{11,3},{4,12},{12,4},... | collective-permute-start | bytes 393224 | tf_op jit(solution)/shard_map/ppermute | solution.py:18
  149.7 53.3 %all-to-all-start.2 = ((bf16[16,128,256]{2,1,0:T(8,128)(2,1)}), bf16[16,128,256]{2,1,0:T(8,128)(2,1)S(1)}, u32[]{:S(2)}, u32[]{:S(2)}) async-start(bf16[16,128,256]{2,1,0:T(8,128)(2,1)} %bitcast.39), calls=%async_computation.2 | async-start | bytes 2097152 | tf_op jit(solution)/shard_map/all_to_all | solution.py:158
Sparse Core Ops, SparseCore 0:
  11.6 83.9 all-gather.6

commit v10 on v2

--- a/solution.py
+++ b/solution.py
@@ -153,8 +153,10 @@
     ]
     partial = jnp.stack(both(partial, core), axis=0)
     partial = partial.reshape(cores, groups, lanes, depth, width).transpose(1, 2, 0, 3, 4)
-    parts = lax.all_to_all(partial.reshape(blocks, depth, width), GATHER_AXES, 0, 0, tiled=True)
-    weight_grad = jnp.sum(parts.astype(F32), axis=0)
+    partial = partial.reshape(lax.axis_size("zhigh"), lax.axis_size("yhigh"), depth, width)
+    parts = lax.all_to_all(partial.transpose(1, 0, 2, 3), "yhigh", 0, 0, tiled=True)
+    parts = lax.all_to_all(jnp.sum(parts.astype(F32), axis=0), "zhigh", 0, 0, tiled=True)
+    weight_grad = jnp.sum(parts, axis=0)
     return (student_out, weight_grad)
 
 

time: 205 us -> 215 us (1.049)
  the two profiles are of different devices: /device:TPU:24 before, /device:TPU:8 now
where the time goes in v10:
time: 215 us; the launch traced here: 214 us
  blocking collectives  76.2 us (35%)
  waiting for transfers between devices  64 us (30%)
  starting transfers between devices  39.4 us (18%)
  between operations  14.4 us (7%)
  other arithmetic  8.42 us (4%)
  matrix products  7.15 us (3%)
  local copies, waits for them, and re-layouts  4.4 us (2%)
    all_gather x2, blocking collectives, gather_rows(): return lax.all_gather(jnp.stack(rows, axis=0), FEATURE_AXES, axis=0)  42.1 us
    all_to_all x2, waiting for transfers between devices, gather_features(): line = lax.all_to_all(copies, axes, 0, 0, tiled=True)  37.2 us
    all_to_all x1, blocking collectives, shards(): lax.all_to_all(partial.transpose(1, 0, 2, 3), 'yhigh', 0, 0, tiled=True)  34.1 us
    ppermute x7, starting transfers between devices, swap(): return lax.ppermute(values, axis, [(0, 1), (1, 0)])  23.9 us
    all_to_all x1, waiting for transfers between devices, shards(): lax.all_to_all(jnp.sum(parts.astype(F32), axis=0), 'zhigh', 0, 0, tiled=T...  14 us
    ppermute x7, waiting for transfers between devices, swap(): return lax.ppermute(values, axis, [(0, 1), (1, 0)])  12.8 us
    all_to_all x2, starting transfers between devices, gather_features(): line = lax.all_to_all(copies, axes, 0, 0, tiled=True)  8.11 us
    all_to_all x1, starting transfers between devices, shards(): lax.all_to_all(jnp.sum(parts.astype(F32), axis=0), 'zhigh', 0, 0, tiled=T...  7.38 us
  transfers between devices with their start and end apart: 11, of which 5 were waited for; matrix products, arithmetic and copies ran while one was open for 7% of the time, Pallas kernels for 0%

profile of v10, /device:TPU:8, one launch (start us, length us, event | category | flops | bytes accessed | tf_op | source)
XLA Modules:
  0.0 214.0 jit_solution(10254555639785414187)
XLA Ops:
  7.2 0.9 broadcast_select_fusion.9
  8.1 7.7 %collective-permute-start = (bf16[256,128]{1,0:T(8,128)(2,1)S(1)}, bf16[256,128]{1,0:T(8,128)(2,1)S(1)}, u32[]{:S(2)}, u32[]{:S(2)}) collective-permute-start(bf16[256,128]{1,0:T(8,128)(2,1)S(1)} %get-tuple-element.43), channel_id=1, source_target_pairs={{0,8},{8,0},{1,9},{9,1},{2,10},{10,2},{3,11},{11,3},{4,12},{12,4},... | collective-permute-start | bytes 196616 | tf_op jit(solution)/shard_map/ppermute | solution.py:18
  15.8 1.6 pad_maximum_fusion.5
  17.4 1.1 reduce_sum.175
  18.6 0.1 copy.45
  18.7 1.1 broadcast_in_dim.4
  19.8 3.7 %all-to-all-start = ((bf16[8,512,128]{1,2,0:T(8,128)(2,1)}), bf16[8,512,128]{1,2,0:T(8,128)(2,1)S(1)}, u32[]{:S(2)}, u32[]{:S(2)}) async-start(bf16[8,512,128]{1,2,0:T(8,128)(2,1)} %broadcast_in_dim.4), calls=%async_computation | async-start | bytes 2097152 | tf_op jit(solution)/shard_map/all_to_all | solution.py:38
  23.5 0.2 multiply_reduce_fusion
  23.7 23.4 %all-gather.3 = f32[16,2,256]{2,1,0:T(2,128)S(1)} all-gather(f32[1,2,256]{2,1,0:T(2,128)S(1)} %maximum_bitcast_fusion), channel_id=3, replica_groups=mesh['group'=2,'zhigh'=4,'yhigh'=4,'row'=2,'x'=4,'core'=2] {'group','x',..., dimensions={0}, use_global_device_ids=true | all-gather | bytes 34816 | tf_op jit(solution)/shard_map/all_gather | solution.py:72
  47.2 0.1 multiply_convert_fusion
  47.3 0.1 broadcast_select_fusion.7
  47.4 3.1 %collective-permute-start.3 = (bf16[256,192]{1,0:T(8,128)(2,1)S(1)}, bf16[256,192]{1,0:T(8,128)(2,1)S(1)}, u32[]{:S(2)}, u32[]{:S(2)}) collective-permute-start(bf16[256,192]{1,0:T(8,128)(2,1)S(1)} %get-tuple-element.34), channel_id=1, source_target_pairs={{0,8},{8,0},{1,9},{9,1},{2,10},{10,2},{3,11},{11,3},{4,12},{12,4},... | collective-permute-start | bytes 294920 | tf_op jit(solution)/shard_map/ppermute | solution.py:18
  50.5 4.5 %collective-permute-done.3 = bf16[256,192]{1,0:T(8,128)(2,1)S(1)} collective-permute-done((bf16[256,192]{1,0:T(8,128)(2,1)S(1)}, bf16[256,192]{1,0:T(8,128)(2,1)S(1)}, u32[]{:S(2)}, u32[]{:S(2)}) %collective-permute-start.3) | collective-permute-done | bytes 98336 | tf_op jit(solution)/shard_map/ppermute | solution.py:18
  55.1 0.1 copy.48
  55.3 1.3 broadcast_in_dim.5
  56.6 4.4 %all-to-all-start.1 = ((bf16[8,512,192]{1,2,0:T(8,128)(2,1)}), bf16[8,512,192]{1,2,0:T(8,128)(2,1)}, u32[]{:S(2)}, u32[]{:S(2)}) async-start(bf16[8,512,192]{1,2,0:T(8,128)(2,1)} %broadcast_in_dim.5), calls=%async_computation.1 | async-start | bytes 3145728 | tf_op jit(solution)/shard_map/all_to_all | solution.py:38
  61.0 1.9 collective-permute-start.1
  62.9 0.1 copy.46
  63.1 37.2 %all-to-all-done.1 = bf16[8,512,192]{1,2,0:T(8,128)(2,1)} async-done(((bf16[8,512,192]{1,2,0:T(8,128)(2,1)}), bf16[8,512,192]{1,2,0:T(8,128)(2,1)}, u32[]{:S(2)}, u32[]{:S(2)}) %all-to-all-start.1) | async-done | bytes 1572896 | tf_op jit(solution)/shard_map/all_to_all | solution.py:38
  100.3 1.9 collective-permute-start.4
  102.2 0.6 broadcast_multiply_fusion
  102.8 1.3 broadcast_select_fusion.4
  104.1 0.5 fusion.20
  104.6 1.9 convolution_add_fusion
  106.5 2.5 %collective-permute-start.2 = (bf16[256,256]{0,1:T(8,128)(2,1)S(1)}, bf16[256,256]{0,1:T(8,128)(2,1)S(1)}, u32[]{:S(2)}, u32[]{:S(2)}) collective-permute-start(bf16[256,256]{0,1:T(8,128)(2,1)S(1)} %slice.157), channel_id=1, source_target_pairs={{0,8},{8,0},{1,9},{9,1},{2,10},{10,2},{3,11},{11,3},{4,12},{12,4},... | collective-permute-start | bytes 393224 | tf_op jit(solution)/shard_map/ppermute | solution.py:18
  109.0 0.1 broadcast_select_fusion
  109.1 2.0 fusion.21
  111.2 0.6 convolution_add_fusion.1
  111.8 3.4 %collective-permute-start.5 = (bf16[256,256]{0,1:T(8,128)(2,1)S(1)}, bf16[256,256]{0,1:T(8,128)(2,1)S(1)}, u32[]{:S(2)}, u32[]{:S(2)}) collective-permute-start(bf16[256,256]{0,1:T(8,128)(2,1)S(1)} %slice.156), channel_id=1, source_target_pairs={{0,8},{8,0},{1,9},{9,1},{2,10},{10,2},{3,11},{11,3},{4,12},{12,4},... | collective-permute-start | bytes 393224 | tf_op jit(solution)/shard_map/ppermute | solution.py:18
  115.2 0.1 fusion.18
  115.3 4.0 %collective-permute-done.5 = bf16[256,256]{0,1:T(8,128)(2,1)S(1)} collective-permute-done((bf16[256,256]{0,1:T(8,128)(2,1)S(1)}, bf16[256,256]{0,1:T(8,128)(2,1)S(1)}, u32[]{:S(2)}, u32[]{:S(2)}) %collective-permute-start.5) | collective-permute-done | bytes 131104 | tf_op jit(solution)/shard_map/ppermute | solution.py:18
  119.3 0.2 multiply_reduce_fusion.2
  119.5 0.6 stack_broadcast_in_dim.3
  120.2 18.7 %all-gather.4 = f32[16,7,256]{2,1,0:T(8,128)S(1)} all-gather(f32[1,7,256]{2,1,0:T(8,128)S(1)} %bitcast.127), channel_id=4, replica_groups=mesh['group'=2,'zhigh'=4,'yhigh'=4,'row'=2,'x'=4,'core'=2] {'group','x',..., dimensions={0}, use_global_device_ids=true | all-gather | bytes 121856 | tf_op jit(solution)/shard_map/all_gather | solution.py:72
  138.9 0.1 slice_reduce_fusion
  139.1 0.2 multiply_convert_fusion.1
  139.2 3.4 %collective-permute-start.6 = (bf16[256,256]{0,1:T(8,128)(2,1)S(1)}, bf16[256,256]{0,1:T(8,128)(2,1)S(1)}, u32[]{:S(2)}, u32[]{:S(2)}) collective-permute-start(bf16[256,256]{0,1:T(8,128)(2,1)S(1)} %get-tuple-element.31), channel_id=1, source_target_pairs={{0,8},{8,0},{1,9},{9,1},{2,10},{10,2},{3,11},{11,3},{4,12},{12,4},... | collective-permute-start | bytes 393224 | tf_op jit(solution)/shard_map/ppermute | solution.py:18
  142.6 4.2 %collective-permute-done.6 = bf16[256,256]{0,1:T(8,128)(2,1)S(1)} collective-permute-done((bf16[256,256]{0,1:T(8,128)(2,1)S(1)}, bf16[256,256]{0,1:T(8,128)(2,1)S(1)}, u32[]{:S(2)}, u32[]{:S(2)}) %collective-permute-start.6) | collective-permute-done | bytes 131104 | tf_op jit(solution)/shard_map/ppermute | solution.py:18
  146.9 1.7 convolution_convert_fusion
  148.6 0.5 broadcast_select_fusion.3
  149.1 0.1 pad_maximum_fusion
  149.2 0.1 copy.57
  149.2 34.1 %all_to_all.20 = bf16[4,4,128,256]{3,2,1,0:T(8,128)(2,1)S(1)} all-to-all(bf16[4,4,128,256]{3,2,1,0:T(8,128)(2,1)S(1)} %copy.57), channel_id=1, replica_groups=mesh['group'=2,'zhigh'=4,'yhigh'=4,'row'=2,'x'=4,'core'=2] {'yhigh'}, dimensions={0} | all-to-all | bytes 2097152 | tf_op jit(solution)/shard_map/all_to_all | solution.py:157
  183.3 0.9 convert_reduce_fusion
  184.3 7.4 %all-to-all-start.3 = ((f32[4,128,256]{2,1,0:T(8,128)}), f32[4,128,256]{2,1,0:T(8,128)S(1)}, u32[]{:S(2)}, u32[]{:S(2)}) async-start(f32[4,128,256]{2,1,0:T(8,128)} %convert_reduce_fusion), calls=%async_computation.3 | async-start | bytes 1048576 | tf_op jit(solution)/shard_map/all_to_all | solution.py:158
  191.7 0.8 copy.58
  192.5 14.0 %all-to-all-done.3 = f32[4,128,256]{2,1,0:T(8,128)S(1)} async-done(((f32[4,128,256]{2,1,0:T(8,128)}), f32[4,128,256]{2,1,0:T(8,128)S(1)}, u32[]{:S(2)}, u32[]{:S(2)}) %all-to-all-start.3) | async-done | bytes 524320 | tf_op jit(solution)/shard_map/all_to_all | solution.py:158
  206.5 0.7 reduce_sum.189
  (33 shorter events, 0.4 us)
Async XLA Ops:
  7.2 95.6 %all-gather.7.cloned.1.call-start = ((), (), s32[]{:S(2)}) async-start(), calls=%async_computation.4 | async-start | bytes 2785280 | tf_op jit(solution)/shard_map/all_gather | solution.py:92
  8.1 10.5 %collective-permute-start = (bf16[256,128]{1,0:T(8,128)(2,1)S(1)}, bf16[256,128]{1,0:T(8,128)(2,1)S(1)}, u32[]{:S(2)}, u32[]{:S(2)}) collective-permute-start(bf16[256,128]{1,0:T(8,128)(2,1)S(1)} %get-tuple-element.43), channel_id=1, source_target_pairs={{0,8},{8,0},{1,9},{9,1},{2,10},{10,2},{3,11},{11,3},{4,12},{12,4},... | collective-permute-start | bytes 196616 | tf_op jit(solution)/shard_map/ppermute | solution.py:18
  18.7 4.8 %copy-start = (f32[256,384]{1,0:T(8,128)S(1)}, f32[256,384]{1,0:T(8,128)}, u32[]{:S(2)}) copy-start(f32[256,384]{1,0:T(8,128)} %param.7) | copy-start | bytes 1179652
  19.8 27.4 %copy-start.4 = (f32[384]{0:T(512)S(1)}, f32[384]{0:T(512)}, u32[]{:S(2)}) copy-start(f32[384]{0:T(512)} %param.8) | copy-start | bytes 4612
  19.8 35.4 %all-to-all-start = ((bf16[8,512,128]{1,2,0:T(8,128)(2,1)}), bf16[8,512,128]{1,2,0:T(8,128)(2,1)S(1)}, u32[]{:S(2)}, u32[]{:S(2)}) async-start(bf16[8,512,128]{1,2,0:T(8,128)(2,1)} %broadcast_in_dim.4), calls=%async_computation | async-start | bytes 2097152 | tf_op jit(solution)/shard_map/all_to_all | solution.py:38
  47.4 7.6 %collective-permute-start.3 = (bf16[256,192]{1,0:T(8,128)(2,1)S(1)}, bf16[256,192]{1,0:T(8,128)(2,1)S(1)}, u32[]{:S(2)}, u32[]{:S(2)}) collective-permute-start(bf16[256,192]{1,0:T(8,128)(2,1)S(1)} %get-tuple-element.34), channel_id=1, source_target_pairs={{0,8},{8,0},{1,9},{9,1},{2,10},{10,2},{3,11},{11,3},{4,12},{12,4},... | collective-permute-start | bytes 294920 | tf_op jit(solution)/shard_map/ppermute | solution.py:18
  56.6 6.4 %copy-start.2 = (f32[256,256]{1,0:T(8,128)S(1)}, f32[256,256]{1,0:T(8,128)}, u32[]{:S(2)}) copy-start(f32[256,256]{1,0:T(8,128)} %param.10) | copy-start | bytes 786436
  56.6 45.6 %copy-start.3 = (f32[256]{0:T(256)S(1)}, f32[256]{0:T(256)}, u32[]{:S(2)}) copy-start(f32[256]{0:T(256)} %param.13) | copy-start | bytes 3076
  56.6 43.7 %all-to-all-start.1 = ((bf16[8,512,192]{1,2,0:T(8,128)(2,1)}), bf16[8,512,192]{1,2,0:T(8,128)(2,1)}, u32[]{:S(2)}, u32[]{:S(2)}) async-start(bf16[8,512,192]{1,2,0:T(8,128)(2,1)} %broadcast_in_dim.5), calls=%async_computation.1 | async-start | bytes 3145728 | tf_op jit(solution)/shard_map/all_to_all | solution.py:38
  61.0 43.6 %collective-permute-start.1 = (bf16[8,512,128]{1,2,0:T(8,128)(2,1)S(1)}, bf16[8,512,128]{1,2,0:T(8,128)(2,1)}, u32[]{:S(2)}, u32[]{:S(2)}) collective-permute-start(bf16[8,512,128]{1,2,0:T(8,128)(2,1)S(1)} %all-to-all-done), channel_id=1, source_target_pairs={{0,1},{1,0},{2,3},{3,2},{4,5},{5,4},{6,7},{7,6},{8,9},{9,8},{10,11... | collective-permute-start | bytes 3145736 | tf_op jit(solution)/shard_map/ppermute | solution.py:18
  100.3 10.9 %collective-permute-start.4 = (bf16[8,512,192]{1,2,0:T(8,128)(2,1)}, bf16[8,512,192]{1,2,0:T(8,128)(2,1)S(1)}, u32[]{:S(2)}, u32[]{:S(2)}) collective-permute-start(bf16[8,512,192]{1,2,0:T(8,128)(2,1)} %all-to-all-done.1), channel_id=1, source_target_pairs={{0,1},{1,0},{2,3},{3,2},{4,5},{5,4},{6,7},{7,6},{8,9},{9,8},{10,11... | collective-permute-start | bytes 4718600 | tf_op jit(solution)/shard_map/ppermute | solution.py:18
  104.6 4.4 %copy-start.1 = (bf16[5120,256]{1,0:T(8,128)(2,1)S(1)}, bf16[5120,256]{1,0:T(8,128)(2,1)}, u32[]{:S(2)}) copy-start(bf16[5120,256]{1,0:T(8,128)(2,1)} %all-gather.7.cloned.1.call-done) | copy-start | bytes 7864324
  106.5 8.7 %collective-permute-start.2 = (bf16[256,256]{0,1:T(8,128)(2,1)S(1)}, bf16[256,256]{0,1:T(8,128)(2,1)S(1)}, u32[]{:S(2)}, u32[]{:S(2)}) collective-permute-start(bf16[256,256]{0,1:T(8,128)(2,1)S(1)} %slice.157), channel_id=1, source_target_pairs={{0,8},{8,0},{1,9},{9,1},{2,10},{10,2},{3,11},{11,3},{4,12},{12,4},... | collective-permute-start | bytes 393224 | tf_op jit(solution)/shard_map/ppermute | solution.py:18
  111.8 7.5 %collective-permute-start.5 = (bf16[256,256]{0,1:T(8,128)(2,1)S(1)}, bf16[256,256]{0,1:T(8,128)(2,1)S(1)}, u32[]{:S(2)}, u32[]{:S(2)}) collective-permute-start(bf16[256,256]{0,1:T(8,128)(2,1)S(1)} %slice.156), channel_id=1, source_target_pairs={{0,8},{8,0},{1,9},{9,1},{2,10},{10,2},{3,11},{11,3},{4,12},{12,4},... | collective-permute-start | bytes 393224 | tf_op jit(solution)/shard_map/ppermute | solution.py:18
  139.2 7.6 %collective-permute-start.6 = (bf16[256,256]{0,1:T(8,128)(2,1)S(1)}, bf16[256,256]{0,1:T(8,128)(2,1)S(1)}, u32[]{:S(2)}, u32[]{:S(2)}) collective-permute-start(bf16[256,256]{0,1:T(8,128)(2,1)S(1)} %get-tuple-element.31), channel_id=1, source_target_pairs={{0,8},{8,0},{1,9},{9,1},{2,10},{10,2},{3,11},{11,3},{4,12},{12,4},... | collective-permute-start | bytes 393224 | tf_op jit(solution)/shard_map/ppermute | solution.py:18
  184.3 22.2 %all-to-all-start.3 = ((f32[4,128,256]{2,1,0:T(8,128)}), f32[4,128,256]{2,1,0:T(8,128)S(1)}, u32[]{:S(2)}, u32[]{:S(2)}) async-start(f32[4,128,256]{2,1,0:T(8,128)} %convert_reduce_fusion), calls=%async_computation.3 | async-start | bytes 1048576 | tf_op jit(solution)/shard_map/all_to_all | solution.py:158
Sparse Core Ops, SparseCore 0:
  17.6 77.4 all-gather.6

commit v11 on v2

--- a/solution.py
+++ b/solution.py
@@ -107,9 +107,11 @@
     hidden = gather_features(split_tokens(hidden, row))
 
     branch = product(context, out_full)
-    pre_norm = student_stream + (branch[:tokens] + swap(branch[tokens:].astype(BF16), "row").astype(F32))
     target = product(hidden, projection_full)
-    target = target[:tokens] + swap(target[tokens:].astype(BF16), "row").astype(F32)
+    sent = jnp.concatenate([branch[tokens:].astype(BF16), target[tokens:].astype(BF16)], axis=0)
+    received = swap(sent, "row").astype(F32)
+    pre_norm = student_stream + (branch[:tokens] + received[:tokens])
+    target = target[:tokens] + received[tokens:]
 
     block_mean, centered, square = moments(pre_norm)
     gain_square = student_gain * student_gain

time: 205 us -> 212 us (1.034)
  the two profiles are of different devices: /device:TPU:24 before, /device:TPU:80 now
where the time goes in v11:
time: 212 us
  waiting for transfers between devices  88.2 us (42%)
  starting transfers between devices  51.6 us (24%)
  blocking collectives  35.8 us (17%)
  between operations  14.4 us (7%)
  other arithmetic  11 us (5%)
  matrix products  5.62 us (3%)
  local copies, waits for them, and re-layouts  5.01 us (2%)
    all_gather x2, blocking collectives, gather_rows(): return lax.all_gather(jnp.stack(rows, axis=0), FEATURE_AXES, axis=0)  35.8 us
    all_to_all x2, waiting for transfers between devices, gather_features(): line = lax.all_to_all(copies, axes, 0, 0, tiled=True)  35.3 us
    all_to_all x1, waiting for transfers between devices, shards(): lax.all_to_all(partial.reshape(blocks, depth, width), GATHER_AXES, 0, 0,...  34.3 us
    all_to_all x1, starting transfers between devices, shards(): lax.all_to_all(partial.reshape(blocks, depth, width), GATHER_AXES, 0, 0,...  19.7 us
    ppermute x6, waiting for transfers between devices, swap(): return lax.ppermute(values, axis, [(0, 1), (1, 0)])  18.6 us
    ppermute x6, starting transfers between devices, swap(): return lax.ppermute(values, axis, [(0, 1), (1, 0)])  17.8 us
    all_to_all x2, starting transfers between devices, gather_features(): line = lax.all_to_all(copies, axes, 0, 0, tiled=True)  14 us
  transfers between devices with their start and end apart: 10, of which 7 were waited for; matrix products, arithmetic and copies ran while one was open for 6% of the time, Pallas kernels for 0%

profile of v11, /device:TPU:80, one launch (start us, length us, event | category | flops | bytes accessed | tf_op | source)
XLA Modules:
  0.0 211.5 jit_solution(4798548696087869156)
XLA Ops:
  7.2 1.6 pad_maximum_fusion.6
  8.9 1.1 reduce_sum.162
  10.0 1.2 multiply_reduce_fusion
  11.2 17.8 %all-gather.3 = f32[16,2,256]{2,1,0:T(2,128)S(1)} all-gather(f32[1,2,256]{2,1,0:T(2,128)S(1)} %maximum_bitcast_fusion), channel_id=3, replica_groups=mesh['group'=2,'zhigh'=4,'yhigh'=4,'row'=2,'x'=4,'core'=2] {'group','x',..., dimensions={0}, use_global_device_ids=true | all-gather | bytes 34816 | tf_op jit(solution)/shard_map/all_gather | solution.py:72
  29.1 0.8 multiply_convert_fusion
  30.0 0.1 broadcast_select_fusion.7
  30.1 3.5 %collective-permute-start.2 = (bf16[256,192]{1,0:T(8,128)(2,1)S(1)}, bf16[256,192]{1,0:T(8,128)(2,1)S(1)}, u32[]{:S(2)}, u32[]{:S(2)}) collective-permute-start(bf16[256,192]{1,0:T(8,128)(2,1)S(1)} %get-tuple-element.32), channel_id=1, source_target_pairs={{0,8},{8,0},{1,9},{9,1},{2,10},{10,2},{3,11},{11,3},{4,12},{12,4},... | collective-permute-start | bytes 294920 | tf_op jit(solution)/shard_map/ppermute | solution.py:18
  33.6 5.5 %collective-permute-done.2 = bf16[256,192]{1,0:T(8,128)(2,1)S(1)} collective-permute-done((bf16[256,192]{1,0:T(8,128)(2,1)S(1)}, bf16[256,192]{1,0:T(8,128)(2,1)S(1)}, u32[]{:S(2)}, u32[]{:S(2)}) %collective-permute-start.2) | collective-permute-done | bytes 98336 | tf_op jit(solution)/shard_map/ppermute | solution.py:18
  39.1 0.1 copy.37
  39.2 1.3 broadcast_in_dim.5
  40.5 6.1 %all-to-all-start.1 = ((bf16[8,512,192]{1,2,0:T(8,128)(2,1)}), bf16[8,512,192]{1,2,0:T(8,128)(2,1)S(1)}, u32[]{:S(2)}, u32[]{:S(2)}) async-start(bf16[8,512,192]{1,2,0:T(8,128)(2,1)} %broadcast_in_dim.5), calls=%async_computation.1 | async-start | bytes 3145728 | tf_op jit(solution)/shard_map/all_to_all | solution.py:38
  46.6 3.8 %collective-permute-start = (bf16[256,128]{1,0:T(8,128)(2,1)S(1)}, bf16[256,128]{1,0:T(8,128)(2,1)S(1)}, u32[]{:S(2)}, u32[]{:S(2)}) collective-permute-start(bf16[256,128]{1,0:T(8,128)(2,1)S(1)} %get-tuple-element.41), channel_id=1, source_target_pairs={{0,8},{8,0},{1,9},{9,1},{2,10},{10,2},{3,11},{11,3},{4,12},{12,4},... | collective-permute-start | bytes 196616 | tf_op jit(solution)/shard_map/ppermute | solution.py:18
  50.4 2.3 %collective-permute-done = bf16[256,128]{1,0:T(8,128)(2,1)S(1)} collective-permute-done((bf16[256,128]{1,0:T(8,128)(2,1)S(1)}, bf16[256,128]{1,0:T(8,128)(2,1)S(1)}, u32[]{:S(2)}, u32[]{:S(2)}) %collective-permute-start) | collective-permute-done | bytes 65568 | tf_op jit(solution)/shard_map/ppermute | solution.py:18
  52.8 0.1 copy.35
  52.9 24.2 %all-to-all-done.1 = bf16[8,512,192]{1,2,0:T(8,128)(2,1)S(1)} async-done(((bf16[8,512,192]{1,2,0:T(8,128)(2,1)}), bf16[8,512,192]{1,2,0:T(8,128)(2,1)S(1)}, u32[]{:S(2)}, u32[]{:S(2)}) %all-to-all-start.1) | async-done | bytes 1572896 | tf_op jit(solution)/shard_map/all_to_all | solution.py:38
  77.1 1.2 broadcast_in_dim.4
  78.3 0.4 copy-done.1
  78.7 7.9 %all-to-all-start = ((bf16[8,512,128]{1,2,0:T(8,128)(2,1)}), bf16[8,512,128]{1,2,0:T(8,128)(2,1)S(1)}, u32[]{:S(2)}, u32[]{:S(2)}) async-start(bf16[8,512,128]{1,2,0:T(8,128)(2,1)} %broadcast_in_dim.4), calls=%async_computation | async-start | bytes 2097152 | tf_op jit(solution)/shard_map/all_to_all | solution.py:38
  86.6 1.9 collective-permute-start.3
  88.5 11.0 %all-to-all-done = bf16[8,512,128]{1,2,0:T(8,128)(2,1)S(1)} async-done(((bf16[8,512,128]{1,2,0:T(8,128)(2,1)}), bf16[8,512,128]{1,2,0:T(8,128)(2,1)S(1)}, u32[]{:S(2)}, u32[]{:S(2)}) %all-to-all-start) | async-done | bytes 1048608 | tf_op jit(solution)/shard_map/all_to_all | solution.py:38
  99.5 1.9 collective-permute-start.1
  101.5 1.6 broadcast_select_fusion
  103.1 0.3 copy-done.2
  103.4 0.6 fusion.21
  104.0 0.6 convolution_add_fusion.1
  104.7 1.3 broadcast_select_fusion.4
  105.9 0.5 fusion.20
  106.5 1.8 convolution_add_fusion
  108.3 3.5 %collective-permute-start.4 = (bf16[512,256]{0,1:T(8,128)(2,1)S(1)}, bf16[512,256]{0,1:T(8,128)(2,1)S(1)}, u32[]{:S(2)}, u32[]{:S(2)}) collective-permute-start(bf16[512,256]{0,1:T(8,128)(2,1)S(1)} %pad_maximum_fusion.2), channel_id=1, source_target_pairs={{0,8},{8,0},{1,9},{9,1},{2,10},{10,2},{3,11},{11,3},{4,12},{12,4},... | collective-permute-start | bytes 786440 | tf_op jit(solution)/shard_map/ppermute | solution.py:18
  111.8 0.1 copy.40
  112.0 0.6 broadcast_multiply_fusion
  112.6 6.3 %collective-permute-done.4 = bf16[512,256]{0,1:T(8,128)(2,1)S(1)} collective-permute-done((bf16[512,256]{0,1:T(8,128)(2,1)S(1)}, bf16[512,256]{0,1:T(8,128)(2,1)S(1)}, u32[]{:S(2)}, u32[]{:S(2)}) %collective-permute-start.4) | collective-permute-done | bytes 262176 | tf_op jit(solution)/shard_map/ppermute | solution.py:18
  118.9 0.1 convert_element_type.21
  118.9 0.1 fusion.18
  119.0 0.2 multiply_reduce_fusion.2
  119.2 0.6 stack_broadcast_in_dim.3
  119.9 17.9 %all-gather.4 = f32[16,7,256]{2,1,0:T(8,128)S(1)} all-gather(f32[1,7,256]{2,1,0:T(8,128)S(1)} %bitcast.125), channel_id=4, replica_groups=mesh['group'=2,'zhigh'=4,'yhigh'=4,'row'=2,'x'=4,'core'=2] {'group','x',..., dimensions={0}, use_global_device_ids=true | all-gather | bytes 121856 | tf_op jit(solution)/shard_map/all_gather | solution.py:72
  137.8 0.1 slice_reduce_fusion
  138.0 0.2 multiply_convert_fusion.1
  138.1 3.1 %collective-permute-start.5 = (bf16[256,256]{0,1:T(8,128)(2,1)S(1)}, bf16[256,256]{0,1:T(8,128)(2,1)S(1)}, u32[]{:S(2)}, u32[]{:S(2)}) collective-permute-start(bf16[256,256]{0,1:T(8,128)(2,1)S(1)} %get-tuple-element.29), channel_id=1, source_target_pairs={{0,8},{8,0},{1,9},{9,1},{2,10},{10,2},{3,11},{11,3},{4,12},{12,4},... | collective-permute-start | bytes 393224 | tf_op jit(solution)/shard_map/ppermute | solution.py:18
  141.3 4.5 %collective-permute-done.5 = bf16[256,256]{0,1:T(8,128)(2,1)S(1)} collective-permute-done((bf16[256,256]{0,1:T(8,128)(2,1)S(1)}, bf16[256,256]{0,1:T(8,128)(2,1)S(1)}, u32[]{:S(2)}, u32[]{:S(2)}) %collective-permute-start.5) | collective-permute-done | bytes 131104 | tf_op jit(solution)/shard_map/ppermute | solution.py:18
  145.8 1.7 convolution_convert_fusion
  147.5 0.5 broadcast_select_fusion.3
  147.9 1.1 pad_maximum_fusion
  149.0 19.7 %all-to-all-start.2 = ((bf16[16,128,256]{2,1,0:T(8,128)(2,1)}), bf16[16,128,256]{2,1,0:T(8,128)(2,1)S(1)}, u32[]{:S(2)}, u32[]{:S(2)}) async-start(bf16[16,128,256]{2,1,0:T(8,128)(2,1)} %bitcast.39), calls=%async_computation.2 | async-start | bytes 2097152 | tf_op jit(solution)/shard_map/all_to_all | solution.py:158
  168.8 0.8 copy.49
  169.6 34.3 %all-to-all-done.2 = bf16[16,128,256]{2,1,0:T(8,128)(2,1)S(1)} async-done(((bf16[16,128,256]{2,1,0:T(8,128)(2,1)}), bf16[16,128,256]{2,1,0:T(8,128)(2,1)S(1)}, u32[]{:S(2)}, u32[]{:S(2)}) %all-to-all-start.2) | async-done | bytes 1048608 | tf_op jit(solution)/shard_map/all_to_all | solution.py:158
  203.9 0.8 convert_reduce_fusion
  (32 shorter events, 0.4 us)
Async XLA Ops:
  7.2 22.0 %copy-start = (f32[256,384]{1,0:T(8,128)S(1)}, f32[256,384]{1,0:T(8,128)}, u32[]{:S(2)}) copy-start(f32[256,384]{1,0:T(8,128)} %param.7) | copy-start | bytes 1179652
  7.2 94.3 %all-gather.7.cloned.1.call-start = ((), (), s32[]{:S(2)}) async-start(), calls=%async_computation.3 | async-start | bytes 2785280 | tf_op jit(solution)/shard_map/all_gather | solution.py:92
  30.1 9.0 %collective-permute-start.2 = (bf16[256,192]{1,0:T(8,128)(2,1)S(1)}, bf16[256,192]{1,0:T(8,128)(2,1)S(1)}, u32[]{:S(2)}, u32[]{:S(2)}) collective-permute-start(bf16[256,192]{1,0:T(8,128)(2,1)S(1)} %get-tuple-element.32), channel_id=1, source_target_pairs={{0,8},{8,0},{1,9},{9,1},{2,10},{10,2},{3,11},{11,3},{4,12},{12,4},... | collective-permute-start | bytes 294920 | tf_op jit(solution)/shard_map/ppermute | solution.py:18
  40.5 6.1 %copy-start.4 = (bf16[256,256]{1,0:T(8,128)(2,1)S(1)}, bf16[256,256]{1,0:T(8,128)(2,1)}, u32[]{:S(2)}) copy-start(bf16[256,256]{1,0:T(8,128)(2,1)} %param.11) | copy-start | bytes 393220
  40.5 36.6 %all-to-all-start.1 = ((bf16[8,512,192]{1,2,0:T(8,128)(2,1)}), bf16[8,512,192]{1,2,0:T(8,128)(2,1)S(1)}, u32[]{:S(2)}, u32[]{:S(2)}) async-start(bf16[8,512,192]{1,2,0:T(8,128)(2,1)} %broadcast_in_dim.5), calls=%async_computation.1 | async-start | bytes 3145728 | tf_op jit(solution)/shard_map/all_to_all | solution.py:38
  46.6 6.2 %collective-permute-start = (bf16[256,128]{1,0:T(8,128)(2,1)S(1)}, bf16[256,128]{1,0:T(8,128)(2,1)S(1)}, u32[]{:S(2)}, u32[]{:S(2)}) collective-permute-start(bf16[256,128]{1,0:T(8,128)(2,1)S(1)} %get-tuple-element.41), channel_id=1, source_target_pairs={{0,8},{8,0},{1,9},{9,1},{2,10},{10,2},{3,11},{11,3},{4,12},{12,4},... | collective-permute-start | bytes 196616 | tf_op jit(solution)/shard_map/ppermute | solution.py:18
  77.1 1.5 copy-start.1
  78.7 20.9 %all-to-all-start = ((bf16[8,512,128]{1,2,0:T(8,128)(2,1)}), bf16[8,512,128]{1,2,0:T(8,128)(2,1)S(1)}, u32[]{:S(2)}, u32[]{:S(2)}) async-start(bf16[8,512,128]{1,2,0:T(8,128)(2,1)} %broadcast_in_dim.4), calls=%async_computation | async-start | bytes 2097152 | tf_op jit(solution)/shard_map/all_to_all | solution.py:38
  86.6 17.4 %collective-permute-start.3 = (bf16[8,512,192]{1,2,0:T(8,128)(2,1)}, bf16[8,512,192]{1,2,0:T(8,128)(2,1)S(1)}, u32[]{:S(2)}, u32[]{:S(2)}) collective-permute-start(bf16[8,512,192]{1,2,0:T(8,128)(2,1)} %copy-done.1), channel_id=1, source_target_pairs={{0,1},{1,0},{2,3},{3,2},{4,5},{5,4},{6,7},{7,6},{8,9},{9,8},{10,11... | collective-permute-start | bytes 4718600 | tf_op jit(solution)/shard_map/ppermute | solution.py:18
  99.5 6.9 %collective-permute-start.1 = (bf16[8,512,128]{1,2,0:T(8,128)(2,1)S(1)}, bf16[8,512,128]{1,2,0:T(8,128)(2,1)}, u32[]{:S(2)}, u32[]{:S(2)}) collective-permute-start(bf16[8,512,128]{1,2,0:T(8,128)(2,1)S(1)} %all-to-all-done), channel_id=1, source_target_pairs={{0,1},{1,0},{2,3},{3,2},{4,5},{5,4},{6,7},{7,6},{8,9},{9,8},{10,11... | collective-permute-start | bytes 3145736 | tf_op jit(solution)/shard_map/ppermute | solution.py:18
  101.5 1.9 copy-start.2
  106.4 5.4 %copy-start.3 = (f32[256,256]{1,0:T(8,128)S(1)}, f32[256,256]{1,0:T(8,128)}, u32[]{:S(2)}) copy-start(f32[256,256]{1,0:T(8,128)} %param.10) | copy-start | bytes 786436
  106.5 5.5 %copy-start.5 = (f32[256]{0:T(256)S(1)}, f32[256]{0:T(256)}, u32[]{:S(2)}) copy-start(f32[256]{0:T(256)} %param.13) | copy-start | bytes 3076
  108.3 10.6 %collective-permute-start.4 = (bf16[512,256]{0,1:T(8,128)(2,1)S(1)}, bf16[512,256]{0,1:T(8,128)(2,1)S(1)}, u32[]{:S(2)}, u32[]{:S(2)}) collective-permute-start(bf16[512,256]{0,1:T(8,128)(2,1)S(1)} %pad_maximum_fusion.2), channel_id=1, source_target_pairs={{0,8},{8,0},{1,9},{9,1},{2,10},{10,2},{3,11},{11,3},{4,12},{12,4},... | collective-permute-start | bytes 786440 | tf_op jit(solution)/shard_map/ppermute | solution.py:18
  138.1 7.6 %collective-permute-start.5 = (bf16[256,256]{0,1:T(8,128)(2,1)S(1)}, bf16[256,256]{0,1:T(8,128)(2,1)S(1)}, u32[]{:S(2)}, u32[]{:S(2)}) collective-permute-start(bf16[256,256]{0,1:T(8,128)(2,1)S(1)} %get-tuple-element.29), channel_id=1, source_target_pairs={{0,8},{8,0},{1,9},{9,1},{2,10},{10,2},{3,11},{11,3},{4,12},{12,4},... | collective-permute-start | bytes 393224 | tf_op jit(solution)/shard_map/ppermute | solution.py:18
  149.0 54.9 %all-to-all-start.2 = ((bf16[16,128,256]{2,1,0:T(8,128)(2,1)}), bf16[16,128,256]{2,1,0:T(8,128)(2,1)S(1)}, u32[]{:S(2)}, u32[]{:S(2)}) async-start(bf16[16,128,256]{2,1,0:T(8,128)(2,1)} %bitcast.39), calls=%async_computation.2 | async-start | bytes 2097152 | tf_op jit(solution)/shard_map/all_to_all | solution.py:158
Sparse Core Ops, SparseCore 0:
  11.6 79.4 all-gather.6
